TPU v7x, 512 devices: a whole 4x4x16 slice. The times are simulated.
512 devices in a mesh: ctx: 32 (over z_hi, y, x), chan: 16 (over z_lo, core).
Axes of the slice: x: 4, y: 4, z: 16 (z_hi: 2, z_lo: 8; z = z_hi * 8 + z_lo), core: 2. Of those that a mesh axis runs over, the one named last changes fastest.
Arguments:
- key_branch: float32 [4096, 4096], P('ctx', 'chan'), may hold values from -6 to 6
- value_branch: float32 [4096, 4096], P('ctx', 'chan'), may hold values from -6 to 6
- query_branch: float32 [4096, 4096], P('ctx', 'chan'), may hold values from -6 to 6
- long_filter: float32 [4096, 4096], P('ctx', 'chan'), may hold values from -6 to 6
- skip_weight: float32 [4096], P('chan'), may hold values from -4 to 4
- out_weight: float32 [4096, 4096], P('chan', 'ctx'), may hold values from -0.09375 to 0.09375
- cotangent: float32 [4096, 4096], P('ctx', 'chan'), may hold values from -6 to 6
Outputs:
- projected: float32 [4096, 4096], P('ctx', 'chan')
- key_grad: float32 [4096, 4096], P('ctx', 'chan')
- value_grad: float32 [4096, 4096], P('ctx', 'chan')
- query_grad: float32 [4096, 4096], P('ctx', 'chan')
- filter_grad: float32 [4096, 4096], P('ctx', 'chan')
- skip_grad: float32 [4096], P('chan')
- weight_grad: float32 [4096, 4096], P('chan', 'ctx')
All inputs are finite; a program needn't handle non-finite values.
Results may differ from a plain program's by a relative error of at most 0.000076.
Values sent between devices are 32-bit elements; how exact they have to be, the bound alone decides.
No kernel may reach another device: no remote copies, remote signals or barrier semaphores. Data moves between devices by JAX's collectives and lax.ppermute only.
A program may use at most 64 MiB of HBM per device.

v0:
```python
import math

import jax
import jax.numpy as jnp
from jax import lax
from jax.sharding import PartitionSpec as P

radix_side = 128


def angle_table(first_len, second_len, modulus):
    first_idx = lax.broadcasted_iota(jnp.int32, (first_len, second_len), 0)
    second_idx = lax.broadcasted_iota(jnp.int32, (first_len, second_len), 1)
    phases = (first_idx * second_idx % modulus).astype(jnp.float32)
    return phases * (2.0 * math.pi / modulus)


def fourier_tables(seq_len):
    blocks = 2 * seq_len // radix_side
    half_rows = seq_len // radix_side
    first_angle = angle_table(blocks, half_rows, blocks)
    twiddle_angle = angle_table(blocks, radix_side, 2 * seq_len)
    inner_angle = angle_table(radix_side, radix_side, radix_side)
    return (
        jnp.cos(first_angle),
        jnp.sin(first_angle),
        jnp.cos(twiddle_angle),
        jnp.sin(twiddle_angle),
        jnp.cos(inner_angle),
        jnp.sin(inner_angle),
    )


def forward_fourier(signal, tables):
    first_cos, first_sin, twiddle_cos, twiddle_sin, inner_cos, inner_sin = tables
    channels = signal.shape[0]
    folded = signal.reshape(channels, first_cos.shape[1], radix_side)
    section_real = jnp.einsum("kn,cnm->ckm", first_cos, folded, precision=lax.Precision.HIGHEST)
    section_imag = -jnp.einsum("kn,cnm->ckm", first_sin, folded, precision=lax.Precision.HIGHEST)
    turned_real = section_real * twiddle_cos + section_imag * twiddle_sin
    turned_imag = section_imag * twiddle_cos - section_real * twiddle_sin
    spec_real = jnp.einsum(
        "ckn,nm->ckm", turned_real, inner_cos, precision=lax.Precision.HIGHEST
    ) + jnp.einsum("ckn,nm->ckm", turned_imag, inner_sin, precision=lax.Precision.HIGHEST)
    spec_imag = jnp.einsum(
        "ckn,nm->ckm", turned_imag, inner_cos, precision=lax.Precision.HIGHEST
    ) - jnp.einsum("ckn,nm->ckm", turned_real, inner_sin, precision=lax.Precision.HIGHEST)
    return (spec_real, spec_imag)


def inverse_fourier(spec_real, spec_imag, tables):
    first_cos, first_sin, twiddle_cos, twiddle_sin, inner_cos, inner_sin = tables
    channels = spec_real.shape[0]
    back_real = jnp.einsum(
        "ckj,jn->ckn", spec_real, inner_cos, precision=lax.Precision.HIGHEST
    ) - jnp.einsum("ckj,jn->ckn", spec_imag, inner_sin, precision=lax.Precision.HIGHEST)
    back_imag = jnp.einsum(
        "ckj,jn->ckn", spec_imag, inner_cos, precision=lax.Precision.HIGHEST
    ) + jnp.einsum("ckj,jn->ckn", spec_real, inner_sin, precision=lax.Precision.HIGHEST)
    untwist_real = back_real * twiddle_cos - back_imag * twiddle_sin
    untwist_imag = back_imag * twiddle_cos + back_real * twiddle_sin
    folded = jnp.einsum(
        "kn,ckm->cnm", first_cos, untwist_real, precision=lax.Precision.HIGHEST
    ) - jnp.einsum("kn,ckm->cnm", first_sin, untwist_imag, precision=lax.Precision.HIGHEST)
    length_full = 2 * first_cos.shape[1] * radix_side
    return folded.reshape(channels, -1) * (1.0 / length_full)


def local(key_branch, value_branch, query_branch, long_filter, skip_weight, out_weight, cotangent):
    tok_rows, local_chans = key_branch.shape
    seq_len = tok_rows * lax.axis_size("ctx")
    norm_scale = 1.0 / math.sqrt(seq_len)
    tables = fourier_tables(seq_len)
    product = key_branch * value_branch
    filter_taps = long_filter * norm_scale
    chan_product, chan_taps = (
        lax.all_to_all(product.T, "ctx", split_axis=0, concat_axis=1, tiled=True),
        lax.all_to_all(filter_taps.T, "ctx", split_axis=0, concat_axis=1, tiled=True),
    )
    prod_real, prod_imag = forward_fourier(chan_product, tables)
    taps_real, taps_imag = forward_fourier(chan_taps, tables)
    conv_chan = inverse_fourier(
        prod_real * taps_real - prod_imag * taps_imag,
        prod_real * taps_imag + prod_imag * taps_real,
        tables,
    )
    convolved = lax.all_to_all(conv_chan, "ctx", split_axis=1, concat_axis=0, tiled=True).T
    pre_gate = convolved + skip_weight * product
    mixed_rows = query_branch * pre_gate
    partial_value = jnp.dot(
        mixed_rows,
        lax.all_gather(out_weight, "ctx", axis=1, tiled=True),
        precision=lax.Precision.HIGHEST,
        preferred_element_type=jnp.float32,
    )
    projected = lax.psum_scatter(partial_value, "chan", scatter_dimension=1, tiled=True)
    cot_full = lax.all_gather(cotangent, "chan", axis=1, tiled=True)
    cot_cols = cot_full
    mixed_grad = lax.dot_general(
        cot_cols,
        lax.all_gather(out_weight, "ctx", axis=1, tiled=True),
        (((1,), (1,)), ((), ())),
        precision=lax.Precision.HIGHEST,
        preferred_element_type=jnp.float32,
    )
    query_grad = mixed_grad * pre_gate
    pre_grad = mixed_grad * query_branch
    skip_grad = lax.psum(jnp.sum(pre_grad * product, axis=0), "ctx") * norm_scale
    chan_grad = lax.all_to_all(pre_grad.T, "ctx", split_axis=0, concat_axis=1, tiled=True)
    grad_real, grad_imag = forward_fourier(chan_grad, tables)
    prod_grad_chan = inverse_fourier(
        grad_real * taps_real + grad_imag * taps_imag,
        grad_imag * taps_real - grad_real * taps_imag,
        tables,
    )
    taps_grad_chan = inverse_fourier(
        grad_real * prod_real + grad_imag * prod_imag,
        grad_imag * prod_real - grad_real * prod_imag,
        tables,
    )
    prod_grad_rows, taps_grad_rows = (
        lax.all_to_all(prod_grad_chan, "ctx", split_axis=1, concat_axis=0, tiled=True),
        lax.all_to_all(taps_grad_chan, "ctx", split_axis=1, concat_axis=0, tiled=True),
    )
    product_grad = prod_grad_rows.T + skip_weight * pre_grad
    key_grad = product_grad * value_branch
    value_grad = product_grad * key_branch
    filter_grad = taps_grad_rows.T * norm_scale
    cot_cols = cot_full
    weight_grad = (
        lax.psum_scatter(
            lax.dot_general(
                cot_cols,
                mixed_rows,
                (((0,), (0,)), ((), ())),
                precision=lax.Precision.HIGHEST,
                preferred_element_type=jnp.float32,
            ),
            "ctx",
            scatter_dimension=0,
            tiled=True,
        ).T
        * norm_scale
    )
    return (projected, key_grad, value_grad, query_grad, filter_grad, skip_grad, weight_grad)


def solution(mesh):
    placed = (
        P("ctx", "chan"),
        P("ctx", "chan"),
        P("ctx", "chan"),
        P("ctx", "chan"),
        P("chan"),
        P("chan", "ctx"),
        P("ctx", "chan"),
    )
    return jax.shard_map(
        local,
        mesh=mesh,
        in_specs=placed,
        out_specs=(
            P("ctx", "chan"),
            P("ctx", "chan"),
            P("ctx", "chan"),
            P("ctx", "chan"),
            P("ctx", "chan"),
            P("chan"),
            P("chan", "ctx"),
        ),
        check_vma=False,
    )
```

profile of v0, /device:TPU:6, one launch (start us, length us, event | category | flops | bytes accessed | tf_op | source)
XLA Modules:
  0.0 984.5 jit_solution(5690534173177075492)
XLA Ops:
  7.2 0.7 all-gather.5.cloned.1.call-update
  7.9 0.7 all-gather.3.cloned.1.call-update
  8.6 1.0 copy.30
  9.6 0.7 multiply_bitcast_fusion.2
  10.3 20.9 %all-to-all-start.1 = ((f32[32,8,128]{2,1,0:T(8,128)}), f32[32,8,128]{2,1,0:T(8,128)S(1)}, u32[]{:S(2)}, u32[]{:S(2)}) async-start(f32[32,8,128]{2,1,0:T(8,128)} %multiply_bitcast_fusion.2), calls=%async_computation.1 | async-start | bytes 262144 | tf_op jit(solution)/shard_map/all_to_all | solution.py:78
  31.4 16.4 %all-to-all-done.1 = f32[32,8,128]{2,1,0:T(8,128)S(1)} async-done(((f32[32,8,128]{2,1,0:T(8,128)}), f32[32,8,128]{2,1,0:T(8,128)S(1)}, u32[]{:S(2)}, u32[]{:S(2)}) %all-to-all-start.1) | async-done | bytes 131104 | tf_op jit(solution)/shard_map/all_to_all | solution.py:78
  49.5 66.2 %all-gather.5.cloned.1.call-done = f32[128,4096]{1,0:T(8,128)} async-done(((f32[128,256]{1,0:T(8,128)}), f32[128,4096]{1,0:T(8,128)}) %all-gather.5.cloned.1.call-update) | async-done | bytes 2097168 | tf_op jit(solution)/shard_map/all_gather | solution.py:97
  115.6 200.9 %all-gather.3.cloned.1.call-done = f32[256,4096]{1,0:T(8,128)} async-done(((f32[256,128]{1,0:T(8,128)}), f32[256,4096]{1,0:T(8,128)}) %all-gather.3.cloned.1.call-update) | async-done | bytes 4194320 | tf_op jit(solution)/shard_map/all_gather | solution.py:92
  316.6 7.1 fusion.312
  323.8 0.8 copy.28
  324.6 6.8 all-to-all-start
  331.4 0.6 fusion.89
  332.0 0.6 convolution_subtract_fusion.4
  332.6 0.6 convolution_add_fusion.4
  333.3 0.8 copy.34
  334.0 13.0 %all-to-all-done = f32[32,8,128]{2,1,0:T(8,128)S(1)} async-done(((f32[32,8,128]{2,1,0:T(8,128)}), f32[32,8,128]{2,1,0:T(8,128)S(1)}, u32[]{:S(2)}, u32[]{:S(2)}) %all-to-all-start) | async-done | bytes 131104 | tf_op jit(solution)/shard_map/all_to_all | solution.py:77
  347.1 5.4 all-to-all-start.3
  353.5 0.6 fusion.87
  354.7 13.5 %all-to-all-done.3 = f32[32,8,128]{2,1,0:T(8,128)S(1)} async-done(((f32[32,8,128]{2,1,0:T(8,128)}), f32[32,8,128]{2,1,0:T(8,128)S(1)}, u32[]{:S(2)}, u32[]{:S(2)}) %all-to-all-start.3) | async-done | bytes 131104 | tf_op jit(solution)/shard_map/all_to_all | solution.py:109
  369.8 0.6 fusion.79
  370.4 0.6 convolution_subtract_fusion.5
  371.0 0.6 convolution_add_fusion.5
  371.7 0.6 convolution_add_fusion.2
  372.3 0.7 multiply_add_fusion
  374.3 0.6 convolution_add_fusion.3
  374.9 0.6 convolution_subtract_fusion.3
  376.3 0.7 copy.32
  377.1 6.0 all-to-all-start.2
  383.7 0.6 fusion.75
  384.3 0.6 convolution_add_fusion.1
  384.9 0.6 convolution_subtract_fusion.1
  386.4 0.7 copy.36
  387.1 11.8 %all-to-all-done.2 = f32[8,32,128]{2,0,1:T(8,128)} async-done(((f32[8,32,128]{2,0,1:T(8,128)}), f32[8,32,128]{2,0,1:T(8,128)}, u32[]{:S(2)}, u32[]{:S(2)}) %all-to-all-start.2) | async-done | bytes 131104 | tf_op jit(solution)/shard_map/all_to_all | solution.py:87
  398.9 6.0 all-to-all-start.4
  404.9 1.0 copy.33
  405.9 14.6 %all-to-all-done.4 = f32[8,32,128]{2,0,1:T(8,128)S(1)} async-done(((f32[8,32,128]{2,0,1:T(8,128)}), f32[8,32,128]{2,0,1:T(8,128)S(1)}, u32[]{:S(2)}, u32[]{:S(2)}) %all-to-all-start.4) | async-done | bytes 131104 | tf_op jit(solution)/shard_map/all_to_all | solution.py:122
  420.6 1.8 fusion.99
  422.4 5.1 convolution_bitcast_fusion
  427.6 5.9 fusion.97
  434.7 0.6 convolution_subtract_fusion
  435.3 0.6 convolution_add_fusion
  436.8 0.7 copy.38
  437.5 5.4 all-to-all-start.5
  442.9 145.0 %psum.7 = f32[256]{0:T(256)S(1)} all-reduce(f32[256]{0:T(256)S(1)} %get-tuple-element.21), channel_id=1, replica_groups=mesh['ctx'=32,'chan'=16] {'ctx'}, use_global_device_ids=true, to_apply=%region_2.3 | all-reduce | flops 256 | bytes 2048 | tf_op jit(solution)/shard_map/psum | solution.py:108
  588.4 0.8 copy.39
  589.2 138.6 %reduce-scatter.5.cloned.1.call-done = f32[128,256]{0,1:T(8,128)} async-done(((f32[4096,256]{0,1:T(8,128)}), f32[128,256]{0,1:T(8,128)}) %reduce-scatter.5.cloned.1.call-update) | async-done | bytes 131088 | tf_op jit(solution)/shard_map/reduce_scatter | solution.py:131
  727.8 1.6 multiply_bitcast_fusion
  729.4 248.6 %reduce-scatter.3.cloned.1.call-done = f32[128,256]{1,0:T(8,128)} async-done(((f32[128,4096]{1,0:T(8,128)}), f32[128,256]{1,0:T(8,128)}) %reduce-scatter.3.cloned.1.call-update) | async-done | bytes 131088 | tf_op jit(solution)/shard_map/reduce_scatter | solution.py:96
  (44 shorter events, 11.3 us)
Async XLA Ops:
  7.2 108.5 %all-gather.5.cloned.1.call-start = ((), (), s32[]{:S(2)}) async-start(), calls=%async_computation.10 | async-start | bytes 2228224 | tf_op jit(solution)/shard_map/all_gather | solution.py:97
  7.9 308.7 %all-gather.3.cloned.1.call-start = ((), (), s32[]{:S(2)}) async-start(), calls=%async_computation.8 | async-start | bytes 4325376 | tf_op jit(solution)/shard_map/all_gather | solution.py:92
  10.3 313.4 %copy-start.1 = (f32[128,256]{1,0:T(8,128)S(1)}, f32[128,256]{1,0:T(8,128)}, u32[]{:S(2)}) copy-start(f32[128,256]{1,0:T(8,128)} %param.9) | copy-start | bytes 393220
  10.3 313.4 %copy-start.3 = (f32[128,256]{1,0:T(8,128)S(1)}, f32[128,256]{1,0:T(8,128)}, u32[]{:S(2)}) copy-start(f32[128,256]{1,0:T(8,128)} %param.7) | copy-start | bytes 393220
  10.3 313.4 %copy-start.4 = (f32[128,256]{1,0:T(8,128)S(1)}, f32[128,256]{1,0:T(8,128)}, u32[]{:S(2)}) copy-start(f32[128,256]{1,0:T(8,128)} %param.8) | copy-start | bytes 393220
  10.3 37.5 %all-to-all-start.1 = ((f32[32,8,128]{2,1,0:T(8,128)}), f32[32,8,128]{2,1,0:T(8,128)S(1)}, u32[]{:S(2)}, u32[]{:S(2)}) async-start(f32[32,8,128]{2,1,0:T(8,128)} %multiply_bitcast_fusion.2), calls=%async_computation.1 | async-start | bytes 262144 | tf_op jit(solution)/shard_map/all_to_all | solution.py:78
  323.8 30.9 %copy-start.2 = (f32[128,256]{1,0:T(8,128)}, f32[128,256]{1,0:T(8,128)S(1)}, u32[]{:S(2)}) copy-start(f32[128,256]{1,0:T(8,128)S(1)} %get-tuple-element.22) | copy-start | bytes 393220
  324.6 22.5 %all-to-all-start = ((f32[32,8,128]{2,1,0:T(8,128)}), f32[32,8,128]{2,1,0:T(8,128)S(1)}, u32[]{:S(2)}, u32[]{:S(2)}) async-start(f32[32,8,128]{2,1,0:T(8,128)} %bitcast.1), calls=%async_computation | async-start | bytes 262144 | tf_op jit(solution)/shard_map/all_to_all | solution.py:77
  347.1 21.1 %all-to-all-start.3 = ((f32[32,8,128]{2,1,0:T(8,128)}), f32[32,8,128]{2,1,0:T(8,128)S(1)}, u32[]{:S(2)}, u32[]{:S(2)}) async-start(f32[32,8,128]{2,1,0:T(8,128)} %bitcast.19), calls=%async_computation.4 | async-start | bytes 262144 | tf_op jit(solution)/shard_map/all_to_all | solution.py:109
  374.9 45.7 %copy-start.5 = (f32[256]{0:T(256)S(1)}, f32[256]{0:T(256)}, u32[]{:S(2)}) copy-start(f32[256]{0:T(256)} %param.11) | copy-start | bytes 3076
  375.5 46.9 %copy-start = (f32[128,4096]{1,0:T(8,128)S(1)}, f32[128,4096]{1,0:T(8,128)}, u32[]{:S(2)}) copy-start(f32[128,4096]{1,0:T(8,128)} %all-gather.5.cloned.1.call-done) | copy-start | bytes 6291460
  377.1 21.8 %all-to-all-start.2 = ((f32[8,32,128]{2,0,1:T(8,128)}), f32[8,32,128]{2,0,1:T(8,128)}, u32[]{:S(2)}, u32[]{:S(2)}) async-start(f32[8,32,128]{2,0,1:T(8,128)} %copy.32), calls=%async_computation.2 | async-start | bytes 262144 | tf_op jit(solution)/shard_map/all_to_all | solution.py:87
  398.9 21.6 %all-to-all-start.4 = ((f32[8,32,128]{2,0,1:T(8,128)}), f32[8,32,128]{2,0,1:T(8,128)S(1)}, u32[]{:S(2)}, u32[]{:S(2)}) async-start(f32[8,32,128]{2,0,1:T(8,128)} %copy.36), calls=%async_computation.5 | async-start | bytes 262144 | tf_op jit(solution)/shard_map/all_to_all | solution.py:122
  404.9 323.0 %reduce-scatter.5.cloned.1.call-start = ((), (), s32[]{:S(2)}) async-start(), calls=%async_computation.11 | async-start | bytes 4325376 | tf_op jit(solution)/shard_map/reduce_scatter | solution.py:131
  427.5 550.4 %reduce-scatter.3.cloned.1.call-start = ((), (), s32[]{:S(2)}) async-start(), calls=%async_computation.9 | async-start | bytes 2228224 | tf_op jit(solution)/shard_map/reduce_scatter | solution.py:96
  437.5 150.9 %all-to-all-start.5 = ((f32[8,32,128]{2,0,1:T(8,128)}), f32[8,32,128]{2,0,1:T(8,128)S(1)}, u32[]{:S(2)}, u32[]{:S(2)}) async-start(f32[8,32,128]{2,0,1:T(8,128)} %copy.38), calls=%async_computation.6 | async-start | bytes 262144 | tf_op jit(solution)/shard_map/all_to_all | solution.py:123
Sparse Core Ops, SparseCore 0:
  10.1 105.5 all-gather.4
  119.7 196.8 all-gather.2
  427.6 300.1 reduce-scatter.4
  731.1 246.8 reduce-scatter.2
where the time goes:
time: 986 us; the launch traced here: 984 us
  waiting for transfers between devices  725 us (74%)
  blocking collectives  145 us (15%)
  starting transfers between devices  50.7 us (5%)
  matrix products  38.2 us (4%)
  between operations  14.2 us (1%)
    reduce_scatter x1, waiting for transfers between devices, local(): lax.psum_scatter(partial_value, 'chan', scatter_dimension=1, tiled=True)  249 us
    all_gather x1, waiting for transfers between devices, local(): lax.all_gather(out_weight, 'ctx', axis=1, tiled=True)  201 us
    psum x1, blocking collectives, local(): lax.psum(jnp.sum(pre_grad * product, axis=0), 'ctx') * norm_scale  145 us
    reduce_scatter x1, waiting for transfers between devices, local(): lax.psum_scatter(lax.dot_general(cot_cols, mixed_rows, (((0,), (0,)), (()...  139 us
    all_gather x1, waiting for transfers between devices, local(): cot_full = lax.all_gather(cotangent, 'chan', axis=1, tiled=True)  66.2 us
    all_to_all x1, starting transfers between devices, local(): lax.all_to_all(filter_taps.T, 'ctx', split_axis=0, concat_axis=1, tiled=T...  20.9 us
  transfers between devices with their start and end apart: 10, of which 9 were waited for; matrix products, arithmetic and copies ran while one was open for 3% of the time, Pallas kernels for 0%

commit v1 on v0

v1 whole, which is shorter than its diff:
```python
import math

import jax
import jax.numpy as jnp
import numpy as np
from jax import lax
from jax.sharding import Mesh
from jax.sharding import PartitionSpec as P

AXES = ("h", "y", "x", "m", "l", "k")
SIZES = (2, 4, 4, 2, 4, 2)
CTX = ("h", "y", "x")
PLANE = ("y", "x")
LINE = ("m", "l")
side = 128
exact = lax.Precision.HIGHEST
close = lax.Precision.HIGH


def tables(seq_len):
    full = 2 * seq_len
    blocks = full // side
    kept = blocks // 2 + 1
    rows = np.arange(kept)
    first = 2.0 * np.pi * np.outer(rows, np.arange(seq_len // side)) / blocks
    turn = 2.0 * np.pi * np.outer(rows, np.arange(side)) / full
    inner = 2.0 * np.pi * np.outer(np.arange(side), np.arange(side)) / side
    weight = np.where((rows == 0) | (rows == blocks // 2), 1.0, 2.0)[:, None] / full
    cos, sin = np.cos(inner), np.sin(inner)
    as32 = lambda a: jnp.asarray(a.astype(np.float32))
    return dict(
        first=as32(np.concatenate([np.cos(first), -np.sin(first)], 0)),
        turn_cos=as32(np.cos(turn))[:, None, :],
        turn_sin=as32(np.sin(turn))[:, None, :],
        inner=as32(np.block([[cos, -sin], [sin, cos]])),
        outer=as32(np.block([[cos, sin], [-sin, cos]])),
        last=as32(np.concatenate([weight * np.cos(first), -weight * np.sin(first)], 0).T),
        kept=kept,
    )


def forward_fourier(signal, tab):
    both = jnp.einsum("kn,ncm->kcm", tab["first"], signal, precision=exact)
    real, imag = both[: tab["kept"]], both[tab["kept"] :]
    turned = jnp.concatenate(
        [real * tab["turn_cos"] + imag * tab["turn_sin"], imag * tab["turn_cos"] - real * tab["turn_sin"]], 2
    )
    return jnp.einsum("kcm,mj->kcj", turned, tab["inner"], precision=exact)


def inverse_fourier(real, imag, tab):
    back = jnp.einsum("kcm,mj->kcj", jnp.concatenate([real, imag], 2), tab["outer"], precision=exact)
    real, imag = back[..., :side], back[..., side:]
    turned = jnp.concatenate(
        [real * tab["turn_cos"] - imag * tab["turn_sin"], imag * tab["turn_cos"] + real * tab["turn_sin"]], 0
    )
    return jnp.einsum("nk,kcm->ncm", tab["last"], turned, precision=exact)


def halves(spectrum):
    return spectrum[..., :side], spectrum[..., side:]


def swap_hm(block):
    pairs = [(h * 2 + m, m * 2 + h) for h in range(2) for m in range(2)]
    return lax.ppermute(block, ("h", "m"), pairs)


def other_h(block):
    return lax.ppermute(block, "h", [(0, 1), (1, 0)])


def local(key_branch, value_branch, query_branch, long_filter, skip_weight, out_weight, cotangent):
    rows, chans = key_branch.shape
    n_ctx = 32
    group = chans // n_ctx
    seq_len = rows * n_ctx
    norm_scale = 1.0 / math.sqrt(seq_len)
    tab = tables(seq_len)
    at_h = lax.axis_index("h")
    at_ctx = lax.axis_index(CTX)

    cot_mine = swap_hm(cotangent)
    cot_line = lax.all_gather(cot_mine, LINE, axis=0)

    product = key_branch * value_branch
    sent = jnp.concatenate(
        [product.T.reshape(n_ctx, group, rows), (long_filter * norm_scale).T.reshape(n_ctx, group, rows)], 1
    )
    signals = lax.all_to_all(sent, CTX, 0, 0)
    query_own = query_branch.T
    query_far = other_h(query_own)
    query_both = jnp.where(at_h == 0, jnp.stack([query_own, query_far]), jnp.stack([query_far, query_own]))

    weights = lax.all_to_all(jnp.broadcast_to(out_weight[None], (16,) + out_weight.shape), PLANE, 0, 0)
    weights = weights.transpose(1, 0, 2).reshape(chans, -1)

    spectra = forward_fourier(signals, tab)
    prod_real, prod_imag = halves(spectra[:, :group])
    taps_real, taps_imag = halves(spectra[:, group:])
    conv = inverse_fourier(
        prod_real * taps_real - prod_imag * taps_imag, prod_real * taps_imag + prod_imag * taps_real, tab
    )
    skip = lax.dynamic_slice(skip_weight, (at_ctx * group,), (group,))[None, :, None]
    chan_product = signals[:, :group]
    gate_chan = conv + skip * chan_product
    gate_pair = gate_chan.reshape(2, 16, group, rows).transpose(1, 0, 2, 3)
    gate_sent = jnp.broadcast_to(gate_pair[None], (2,) + gate_pair.shape).reshape(n_ctx, 2, group, rows)
    gate_got = lax.all_to_all(gate_sent, CTX, 0, 0)
    gate_both = gate_got.transpose(1, 0, 2, 3).reshape(2, chans, rows)
    mixed = query_both * gate_both
    mixed_flat = mixed.transpose(1, 0, 2).reshape(chans, 2 * rows)

    cot_cores = lax.all_to_all(jnp.broadcast_to(cot_line[None], (2,) + cot_line.shape), "k", 0, 0)
    cot_full = (
        cot_cores.reshape(2, 2, 4, rows, chans).transpose(1, 3, 2, 0, 4).reshape(2 * rows, 8 * chans)
    )

    mixed_grad = lax.dot_general(
        weights, cot_full, (((1,), (1,)), ((), ())), precision=close, preferred_element_type=jnp.float32
    )
    mixed_grad = mixed_grad.reshape(chans, 2, rows).transpose(1, 0, 2)
    grad_sent = (mixed_grad * query_both).reshape(2, n_ctx, group, rows).transpose(1, 0, 2, 3)
    grad_got = lax.all_to_all(grad_sent, CTX, 0, 0)
    grad_chan = grad_got.reshape(2, 16, 2, group, rows).sum(0).transpose(1, 0, 2, 3).reshape(n_ctx, group, rows)

    own_grad = lax.dynamic_index_in_dim(mixed_grad, at_h, 0, False)
    far_grad = lax.dynamic_index_in_dim(mixed_grad, 1 - at_h, 0, False)
    own_gate = lax.dynamic_index_in_dim(gate_both, at_h, 0, False)
    query_grad = ((own_grad + other_h(far_grad)) * own_gate).T

    partial = lax.dot_general(
        mixed_flat, weights, (((0,), (0,)), ((), ())), precision=close, preferred_element_type=jnp.float32
    )
    partial = partial.reshape(2, rows, 4, 2, chans).transpose(3, 0, 2, 1, 4).reshape(2, 8, rows, chans)
    partial = lax.all_to_all(partial, "k", 0, 0).sum(0)
    projected = lax.psum_scatter(partial, LINE, scatter_dimension=0, tiled=False)
    projected = swap_hm(projected)

    weight_part = lax.dot_general(
        mixed_flat, cot_full, (((1,), (0,)), ((), ())), precision=close, preferred_element_type=jnp.float32
    )
    weight_part = weight_part.reshape(chans, 16, rows).transpose(1, 0, 2)
    weight_grad = lax.all_to_all(weight_part, PLANE, 0, 0).sum(0) * norm_scale

    grad_real, grad_imag = halves(forward_fourier(grad_chan, tab))
    lead_real = jnp.concatenate([taps_real, prod_real], 1)
    lead_imag = jnp.concatenate([taps_imag, prod_imag], 1)
    grad_real = jnp.concatenate([grad_real, grad_real], 1)
    grad_imag = jnp.concatenate([grad_imag, grad_imag], 1)
    lagged = inverse_fourier(
        grad_real * lead_real + grad_imag * lead_imag, grad_imag * lead_real - grad_real * lead_imag, tab
    )
    prod_grad = lagged[:, :group] + skip * grad_chan
    skip_part = jnp.sum(grad_chan * chan_product, axis=(0, 2)) * norm_scale
    skip_row = jnp.broadcast_to(jnp.pad(skip_part, (0, rows - group))[None, None], (n_ctx, 1, rows))
    back = lax.all_to_all(jnp.concatenate([prod_grad, lagged[:, group:] * norm_scale, skip_row], 1), CTX, 0, 0)
    product_grad = back[:, :group].reshape(chans, rows).T
    filter_grad = back[:, group : 2 * group].reshape(chans, rows).T
    skip_grad = back[:, 2 * group, :group].reshape(chans)
    return (
        projected,
        product_grad * value_branch,
        product_grad * key_branch,
        query_grad,
        filter_grad,
        skip_grad,
        weight_grad,
    )


def solution(mesh):
    grid = Mesh(mesh.devices.reshape(SIZES), AXES)
    wide = P(("h", "y", "x"), ("m", "l", "k"))
    tall = P(("m", "l", "k"), ("h", "y", "x"))
    flat = P(("m", "l", "k"))
    return jax.shard_map(
        local,
        mesh=grid,
        in_specs=(wide, wide, wide, wide, flat, tall, wide),
        out_specs=(wide, wide, wide, wide, wide, flat, tall),
        check_vma=False,
    )
```

time: 986 us -> 318 us (0.32)
  the two profiles are of different devices: /device:TPU:6 before, /device:TPU:129 now
where the time goes in v1:
time: 318 us; the launch traced here: 316 us
  starting transfers between devices  121 us (38%)
  waiting for transfers between devices  109 us (34%)
  local copies, waits for them, and re-layouts  40.6 us (13%)
  between operations  14.7 us (5%)
  blocking collectives  12.3 us (4%)
  matrix products  9.73 us (3%)
  other arithmetic  9.44 us (3%)
    all_gather x1, waiting for transfers between devices, local(): cot_line = lax.all_gather(cot_mine, LINE, axis=0)  42.2 us
    ppermute x2, starting transfers between devices, swap_hm(): return lax.ppermute(block, ('h', 'm'), pairs)  37.3 us
    ppermute x2, starting transfers between devices, other_h(): return lax.ppermute(block, 'h', [(0, 1), (1, 0)])  23.7 us
    all_to_all x1, waiting for transfers between devices, local(): weight_grad = lax.all_to_all(weight_part, PLANE, 0, 0).sum(0) * norm_scale  20.1 us
    all_to_all x1, starting transfers between devices, local(): signals = lax.all_to_all(sent, CTX, 0, 0)  15.5 us
    all_to_all x1, starting transfers between devices, local(): lax.all_to_all(jnp.concatenate([prod_grad, lagged[:, group:] * norm_scale...  14.6 us
    all_to_all x1, blocking collectives, local(): lax.all_to_all(jnp.broadcast_to(cot_line[None], (2,) + cot_line.shape), '...  12.3 us
    ppermute x2, waiting for transfers between devices, swap_hm(): return lax.ppermute(block, ('h', 'm'), pairs)  11.9 us
  transfers between devices with their start and end apart: 13, of which 9 were waited for; matrix products, arithmetic and copies ran while one was open for 15% of the time, Pallas kernels for 0%

profile of v1, /device:TPU:129, one launch (start us, length us, event | category | flops | bytes accessed | tf_op | source)
XLA Modules:
  0.0 316.0 jit_solution(1504722997925365318)
XLA Ops:
  7.2 1.0 copy.121
  8.2 1.0 copy.119
  9.2 1.0 copy.120
  11.0 15.5 %all-to-all-start = ((f32[32,16,128]{2,1,0:T(8,128)}), f32[32,16,128]{2,1,0:T(8,128)S(1)}, u32[]{:S(2)}, u32[]{:S(2)}) async-start(f32[32,16,128]{2,1,0:T(8,128)} %pad_maximum_fusion.8), calls=%async_computation | async-start | bytes 524288 | tf_op jit(solution)/shard_map/all_to_all | solution.py:90
  26.5 10.0 %collective-permute-start.2 = (f32[128,256]{1,0:T(8,128)S(1)}, f32[128,256]{1,0:T(8,128)S(1)}, u32[]{:S(2)}, u32[]{:S(2)}) collective-permute-start(f32[128,256]{1,0:T(8,128)S(1)} %copy-done.21), channel_id=1, source_target_pairs={{0,0},{8,256},{256,8},{264,264},{1,1},{9,257},{257,9},{265,265},{2... | collective-permute-start | bytes 393224 | tf_op jit(solution)/shard_map/ppermute | solution.py:66
  36.5 6.7 %all-to-all-done = f32[32,16,128]{2,1,0:T(8,128)S(1)} async-done(((f32[32,16,128]{2,1,0:T(8,128)}), f32[32,16,128]{2,1,0:T(8,128)S(1)}, u32[]{:S(2)}, u32[]{:S(2)}) %all-to-all-start) | async-done | bytes 262176 | tf_op jit(solution)/shard_map/all_to_all | solution.py:90
  43.3 1.6 broadcast_in_dim.9
  44.8 3.9 %all-to-all-start.2 = ((f32[16,256,128]{2,1,0:T(8,128)}), f32[16,256,128]{2,1,0:T(8,128)S(1)}, u32[]{:S(2)}, u32[]{:S(2)}) async-start(f32[16,256,128]{2,1,0:T(8,128)} %broadcast_in_dim.9), calls=%async_computation.2 | async-start | bytes 4194304 | tf_op jit(solution)/shard_map/all_to_all | solution.py:95
  48.8 9.9 %collective-permute-done.2 = f32[128,256]{1,0:T(8,128)S(1)} collective-permute-done((f32[128,256]{1,0:T(8,128)S(1)}, f32[128,256]{1,0:T(8,128)S(1)}, u32[]{:S(2)}, u32[]{:S(2)}) %collective-permute-start.2) | collective-permute-done | bytes 131104 | tf_op jit(solution)/shard_map/ppermute | solution.py:66
  61.2 0.8 fusion.37
  62.9 8.5 %all-to-all-done.2 = f32[16,256,128]{2,1,0:T(8,128)S(1)} async-done(((f32[16,256,128]{2,1,0:T(8,128)}), f32[16,256,128]{2,1,0:T(8,128)S(1)}, u32[]{:S(2)}, u32[]{:S(2)}) %all-to-all-start.2) | async-done | bytes 2097184 | tf_op jit(solution)/shard_map/all_to_all | solution.py:95
  71.4 42.2 %all-gather.3.cloned.1.call-done = f32[1024,256]{1,0:T(8,128)} async-done(((f32[128,256]{1,0:T(8,128)}), f32[1024,256]{1,0:T(8,128)}) %all-gather.3.cloned.1.call-update) | async-done | bytes 1048592 | tf_op jit(solution)/shard_map/all_gather | solution.py:84
  113.6 1.4 broadcast_in_dim.10
  115.0 12.3 %all_to_all.40 = f32[2,8,128,256]{3,2,1,0:T(8,128)} all-to-all(f32[2,8,128,256]{3,2,1,0:T(8,128)S(1)} %broadcast_in_dim.10), channel_id=1, replica_groups=mesh['h'=2,'y'=4,'x'=4,'m'=2,'l'=4,'k'=2] {'k'}, dimensions={0} | all-to-all | bytes 4194304 | tf_op jit(solution)/shard_map/all_to_all | solution.py:114
  128.1 8.7 %all-to-all-start.1 = ((f32[32,2,8,128]{3,2,1,0:T(8,128)}), f32[32,2,8,128]{3,2,1,0:T(8,128)S(1)}, u32[]{:S(2)}, u32[]{:S(2)}) async-start(f32[32,2,8,128]{3,2,1,0:T(8,128)} %bitcast.14), calls=%async_computation.1 | async-start | bytes 524288 | tf_op jit(solution)/shard_map/all_to_all | solution.py:109
  136.9 11.9 %collective-permute-start = (f32[256,128]{1,0:T(8,128)S(1)}, f32[256,128]{1,0:T(8,128)S(1)}, u32[]{:S(2)}, u32[]{:S(2)}) collective-permute-start(f32[256,128]{1,0:T(8,128)S(1)} %bitcast.137), channel_id=1, source_target_pairs={{0,256},{256,0},{1,257},{257,1},{2,258},{258,2},{3,259},{259,3},{4... | collective-permute-start | bytes 393224 | tf_op jit(solution)/shard_map/ppermute | solution.py:70
  148.8 2.6 copy.129
  151.4 2.7 reshape.105
  154.1 4.6 %copy.132 = f32[2,128,4,2,256]{4,3,2,1,0:T(2,128)} copy(f32[2,128,4,2,256]{4,1,2,0,3:T(8,128)} %bitcast.126) | data formatting | bytes 4194304 | tf_op jit(solution)/shard_map/transpose | solution.py:116
  158.6 4.0 %dot_general.66 = f32[2,128,2048]{2,1,0:T(8,128)} reshape(f32[2,128,4,2,256]{4,3,2,1,0:T(2,128)} %copy.132) | data formatting | bytes 4194304 | tf_op jit(solution)/shard_map/dot_general | solution.py:119
  162.6 1.6 bitcast_bitcast_fusion
  165.6 1.2 fusion.40
  166.8 1.9 copy.130
  169.5 1.1 copy.128
  170.6 1.1 fusion.23
  171.7 1.5 copy.131
  173.2 6.2 %all-to-all-start.3 = ((f32[2,8,128,256]{3,2,1,0:T(8,128)}), f32[2,8,128,256]{3,2,1,0:T(8,128)}, u32[]{:S(2)}, u32[]{:S(2)}) async-start(f32[2,8,128,256]{3,2,1,0:T(8,128)} %copy.131), calls=%async_computation.3 | async-start | bytes 4194304 | tf_op jit(solution)/shard_map/all_to_all | solution.py:136
  180.1 1.9 all-to-all-done.3
  182.0 7.0 %all-to-all-start.5 = ((f32[32,2,8,128]{3,2,1,0:T(8,128)}), f32[32,2,8,128]{3,2,1,0:T(8,128)S(1)}, u32[]{:S(2)}, u32[]{:S(2)}) async-start(f32[32,2,8,128]{3,2,1,0:T(8,128)} %bitcast.136), calls=%async_computation.6 | async-start | bytes 524288 | tf_op jit(solution)/shard_map/all_to_all | solution.py:124
  189.1 2.7 reshape.94
  191.7 1.9 copy.146
  193.7 2.9 reduce_sum.36
  196.6 3.2 %convolution_bitcast_fusion = f32[16,256,128]{2,1,0:T(8,128)} fusion(f32[256,256,1]{0,1,2:T(8,128)S(1)} %bitcast.131, f32[16,128,256]{2,1,0:T(8,128)S(1)} %bitcast.128), kind=kOutput, calls=%fused_computation.1 | convolution fusion | flops 805306368 | bytes 4456448 | tf_op jit(solution)/shard_map/dot_general | solution.py:140
  199.8 5.8 %all-to-all-done.5 = f32[32,2,8,128]{3,2,1,0:T(8,128)S(1)} async-done(((f32[32,2,8,128]{3,2,1,0:T(8,128)}), f32[32,2,8,128]{3,2,1,0:T(8,128)S(1)}, u32[]{:S(2)}, u32[]{:S(2)}) %all-to-all-start.5) | async-done | bytes 262176 | tf_op jit(solution)/shard_map/all_to_all | solution.py:124
  206.3 3.7 %all-to-all-start.7 = ((f32[16,256,128]{2,1,0:T(8,128)}), f32[16,256,128]{2,1,0:T(8,128)S(1)}, u32[]{:S(2)}, u32[]{:S(2)}) async-start(f32[16,256,128]{2,1,0:T(8,128)} %convolution_bitcast_fusion), calls=%async_computation.8 | async-start | bytes 4194304 | tf_op jit(solution)/shard_map/all_to_all | solution.py:144
  210.1 1.0 reduce_sum.37
  211.6 0.8 multiply_add_fusion.2
  212.9 1.1 fusion.19
  214.1 0.9 fusion
  215.8 0.9 copy.142
  216.8 20.1 %all-to-all-done.7 = f32[16,256,128]{2,1,0:T(8,128)S(1)} async-done(((f32[16,256,128]{2,1,0:T(8,128)}), f32[16,256,128]{2,1,0:T(8,128)S(1)}, u32[]{:S(2)}, u32[]{:S(2)}) %all-to-all-start.7) | async-done | bytes 2097184 | tf_op jit(solution)/shard_map/all_to_all | solution.py:144
  236.9 14.6 %all-to-all-start.6 = ((f32[32,17,128]{2,1,0:T(8,128)}), f32[32,17,128]{2,1,0:T(8,128)S(1)}, u32[]{:S(2)}, u32[]{:S(2)}) async-start(f32[32,17,128]{2,1,0:T(8,128)} %copy.142), calls=%async_computation.7 | async-start | bytes 786432 | tf_op jit(solution)/shard_map/all_to_all | solution.py:157
  251.5 11.9 %collective-permute-start.3 = (f32[256,128]{1,0:T(8,128)S(1)}, f32[256,128]{1,0:T(8,128)S(1)}, u32[]{:S(2)}, u32[]{:S(2)}) collective-permute-start(f32[256,128]{1,0:T(8,128)S(1)} %dynamic-slice_bitcast_fusion), channel_id=1, source_target_pairs={{0,256},{256,0},{1,257},{257,1},{2,258},{258,2},{3,259},{259,3},{4... | collective-permute-start | bytes 393224 | tf_op jit(solution)/shard_map/ppermute | solution.py:70
  263.4 11.3 %collective-permute-done.3 = f32[256,128]{1,0:T(8,128)S(1)} collective-permute-done((f32[256,128]{1,0:T(8,128)S(1)}, f32[256,128]{1,0:T(8,128)S(1)}, u32[]{:S(2)}, u32[]{:S(2)}) %collective-permute-start.3) | collective-permute-done | bytes 131104 | tf_op jit(solution)/shard_map/ppermute | solution.py:70
  274.7 0.8 copy.150
  276.3 27.3 %collective-permute-start.1 = (f32[128,256]{1,0:T(8,128)}, f32[128,256]{1,0:T(8,128)S(1)}, u32[]{:S(2)}, u32[]{:S(2)}) collective-permute-start(f32[128,256]{1,0:T(8,128)} %bitcast.141), channel_id=1, source_target_pairs={{0,0},{8,256},{256,8},{264,264},{1,1},{9,257},{257,9},{265,265},{2... | collective-permute-start | bytes 393224 | tf_op jit(solution)/shard_map/ppermute | solution.py:66
  303.6 0.8 copy.148
  306.6 2.0 collective-permute-done.1
  (96 shorter events, 13.9 us)
Async XLA Ops:
  7.2 19.3 %copy-start.21 = (f32[128,256]{1,0:T(8,128)S(1)}, f32[128,256]{1,0:T(8,128)}, u32[]{:S(2)}) copy-start(f32[128,256]{1,0:T(8,128)} %param.19) | copy-start | bytes 393220
  7.2 36.1 %copy-start.14 = (f32[256,128]{1,0:T(8,128)S(1)}, f32[256,128]{1,0:T(8,128)}, u32[]{:S(2)}) copy-start(f32[256,128]{1,0:T(8,128)} %param.18) | copy-start | bytes 393220
  11.0 32.3 %all-to-all-start = ((f32[32,16,128]{2,1,0:T(8,128)}), f32[32,16,128]{2,1,0:T(8,128)S(1)}, u32[]{:S(2)}, u32[]{:S(2)}) async-start(f32[32,16,128]{2,1,0:T(8,128)} %pad_maximum_fusion.8), calls=%async_computation | async-start | bytes 524288 | tf_op jit(solution)/shard_map/all_to_all | solution.py:90
  26.5 32.3 %collective-permute-start.2 = (f32[128,256]{1,0:T(8,128)S(1)}, f32[128,256]{1,0:T(8,128)S(1)}, u32[]{:S(2)}, u32[]{:S(2)}) collective-permute-start(f32[128,256]{1,0:T(8,128)S(1)} %copy-done.21), channel_id=1, source_target_pairs={{0,0},{8,256},{256,8},{264,264},{1,1},{9,257},{257,9},{265,265},{2... | collective-permute-start | bytes 393224 | tf_op jit(solution)/shard_map/ppermute | solution.py:66
  44.8 3.9 %copy-start.22 = (f32[256]{0:T(256)S(1)}, f32[256]{0:T(256)}, u32[]{:S(2)}) copy-start(f32[256]{0:T(256)} %param.17) | copy-start | bytes 3076
  44.8 14.6 %copy-start.20 = (f32[66,32,1]{0,1,2:T(8,128)S(1)}, f32[66,32,1]{0,1,2:T(8,128)}, u32[]{:S(2)}) copy-start(f32[66,32,1]{0,1,2:T(8,128)} %constant.71) | copy-start | bytes 25348
  44.8 15.4 %copy-start.10 = (f32[33,128]{1,0:T(8,128)S(1)}, f32[33,128]{1,0:T(8,128)}, u32[]{:S(2)}) copy-start(f32[33,128]{1,0:T(8,128)} %constant.61.clone) | copy-start | bytes 50692
  44.8 15.4 %copy-start.12 = (f32[33,128]{1,0:T(8,128)S(1)}, f32[33,128]{1,0:T(8,128)}, u32[]{:S(2)}) copy-start(f32[33,128]{1,0:T(8,128)} %constant.60.clone) | copy-start | bytes 50692
  44.8 26.6 %all-to-all-start.2 = ((f32[16,256,128]{2,1,0:T(8,128)}), f32[16,256,128]{2,1,0:T(8,128)S(1)}, u32[]{:S(2)}, u32[]{:S(2)}) async-start(f32[16,256,128]{2,1,0:T(8,128)} %broadcast_in_dim.9), calls=%async_computation.2 | async-start | bytes 4194304 | tf_op jit(solution)/shard_map/all_to_all | solution.py:95
  48.7 64.9 %all-gather.3.cloned.1.call-start = ((), (), s32[]{:S(2)}) async-start(), calls=%async_computation.10 | async-start | bytes 1179648 | tf_op jit(solution)/shard_map/all_gather | solution.py:84
  48.8 11.6 %copy-start.5 = (f32[256,256,1]{1,0,2:T(8,128)S(1)}, f32[256,256,1]{1,0,2:T(8,128)}, u32[]{:S(2)}) copy-start(f32[256,256,1]{1,0,2:T(8,128)} %constant.72) | copy-start | bytes 786436
  58.8 0.7 copy-start.16
  60.3 2.2 copy-start.8
  60.4 1.6 copy-start.3
  60.5 2.0 copy-start.17
  115.0 21.8 %copy-start.15 = (f32[128,256]{1,0:T(8,128)S(1)}, f32[128,256]{1,0:T(8,128)}, u32[]{:S(2)}) copy-start(f32[128,256]{1,0:T(8,128)} %param.15) | copy-start | bytes 393220
  128.1 40.7 %all-to-all-start.1 = ((f32[32,2,8,128]{3,2,1,0:T(8,128)}), f32[32,2,8,128]{3,2,1,0:T(8,128)S(1)}, u32[]{:S(2)}, u32[]{:S(2)}) async-start(f32[32,2,8,128]{3,2,1,0:T(8,128)} %bitcast.14), calls=%async_computation.1 | async-start | bytes 524288 | tf_op jit(solution)/shard_map/all_to_all | solution.py:109
  136.9 31.8 %collective-permute-start = (f32[256,128]{1,0:T(8,128)S(1)}, f32[256,128]{1,0:T(8,128)S(1)}, u32[]{:S(2)}, u32[]{:S(2)}) collective-permute-start(f32[256,128]{1,0:T(8,128)S(1)} %bitcast.137), channel_id=1, source_target_pairs={{0,256},{256,0},{1,257},{257,1},{2,258},{258,2},{3,259},{259,3},{4... | collective-permute-start | bytes 393224 | tf_op jit(solution)/shard_map/ppermute | solution.py:70
  162.6 2.3 copy-start.1
  162.6 3.0 copy-start.2
  173.2 15.8 %copy-start = (f32[2,128,4,2,256]{4,3,2,1,0:T(2,128)S(1)}, f32[2,128,4,2,256]{4,3,2,1,0:T(2,128)}, u32[]{:S(2)}) copy-start(f32[2,128,4,2,256]{4,3,2,1,0:T(2,128)} %copy.132) | copy-start | bytes 6291460
  173.2 8.8 %all-to-all-start.3 = ((f32[2,8,128,256]{3,2,1,0:T(8,128)}), f32[2,8,128,256]{3,2,1,0:T(8,128)}, u32[]{:S(2)}, u32[]{:S(2)}) async-start(f32[2,8,128,256]{3,2,1,0:T(8,128)} %copy.131), calls=%async_computation.3 | async-start | bytes 4194304 | tf_op jit(solution)/shard_map/all_to_all | solution.py:136
  182.0 23.6 %all-to-all-start.5 = ((f32[32,2,8,128]{3,2,1,0:T(8,128)}), f32[32,2,8,128]{3,2,1,0:T(8,128)S(1)}, u32[]{:S(2)}, u32[]{:S(2)}) async-start(f32[32,2,8,128]{3,2,1,0:T(8,128)} %bitcast.136), calls=%async_computation.6 | async-start | bytes 524288 | tf_op jit(solution)/shard_map/all_to_all | solution.py:124
  189.0 87.3 %reduce-scatter.2.cloned.1.call-start = ((), (), s32[]{:S(2)}) async-start(), calls=%async_computation.9 | async-start | bytes 1179648 | tf_op jit(solution)/shard_map/reduce_scatter | solution.py:137
  199.8 11.3 %copy-start.19 = (f32[66,32,1]{0,1,2:T(8,128)S(1)}, f32[66,32,1]{0,1,2:T(8,128)}, u32[]{:S(2)}) copy-start(f32[66,32,1]{0,1,2:T(8,128)} %constant.74) | copy-start | bytes 25348
  205.6 0.7 copy-start.7
  206.3 30.6 %all-to-all-start.7 = ((f32[16,256,128]{2,1,0:T(8,128)}), f32[16,256,128]{2,1,0:T(8,128)S(1)}, u32[]{:S(2)}, u32[]{:S(2)}) async-start(f32[16,256,128]{2,1,0:T(8,128)} %convolution_bitcast_fusion), calls=%async_computation.8 | async-start | bytes 4194304 | tf_op jit(solution)/shard_map/all_to_all | solution.py:144
  210.1 2.4 copy-start.6
  211.6 2.5 copy-start.4
  212.9 2.2 copy-start.11
  212.9 2.2 copy-start.13
  214.1 1.1 copy-start.18
  214.1 1.5 copy-start.9
  236.9 39.4 %all-to-all-start.6 = ((f32[32,17,128]{2,1,0:T(8,128)}), f32[32,17,128]{2,1,0:T(8,128)S(1)}, u32[]{:S(2)}, u32[]{:S(2)}) async-start(f32[32,17,128]{2,1,0:T(8,128)} %copy.142), calls=%async_computation.7 | async-start | bytes 786432 | tf_op jit(solution)/shard_map/all_to_all | solution.py:157
  251.5 23.2 %collective-permute-start.3 = (f32[256,128]{1,0:T(8,128)S(1)}, f32[256,128]{1,0:T(8,128)S(1)}, u32[]{:S(2)}, u32[]{:S(2)}) collective-permute-start(f32[256,128]{1,0:T(8,128)S(1)} %dynamic-slice_bitcast_fusion), channel_id=1, source_target_pairs={{0,256},{256,0},{1,257},{257,1},{2,258},{258,2},{3,259},{259,3},{4... | collective-permute-start | bytes 393224 | tf_op jit(solution)/shard_map/ppermute | solution.py:70
  276.3 32.2 %collective-permute-start.1 = (f32[128,256]{1,0:T(8,128)}, f32[128,256]{1,0:T(8,128)S(1)}, u32[]{:S(2)}, u32[]{:S(2)}) collective-permute-start(f32[128,256]{1,0:T(8,128)} %bitcast.141), channel_id=1, source_target_pairs={{0,0},{8,256},{256,8},{264,264},{1,1},{9,257},{257,9},{265,265},{2... | collective-permute-start | bytes 393224 | tf_op jit(solution)/shard_map/ppermute | solution.py:66
Sparse Core Ops, SparseCore 0:
  59.6 53.9 all-gather.2
  196.7 63.5 reduce-scatter.1

commit v2 on v1

--- a/solution.py
+++ b/solution.py
@@ -61,13 +61,21 @@
     return spectrum[..., :side], spectrum[..., side:]
 
 
-def swap_hm(block):
-    pairs = [(h * 2 + m, m * 2 + h) for h in range(2) for m in range(2)]
+def across(block, target):
+    pairs = []
+    for h in range(2):
+        for m in range(2):
+            to_h, to_m = target(h, m)
+            pairs.append((h * 2 + m, to_h * 2 + to_m))
     return lax.ppermute(block, ("h", "m"), pairs)
 
 
 def other_h(block):
     return lax.ppermute(block, "h", [(0, 1), (1, 0)])
+
+
+def tie(value, first):
+    return value + 0.0 * first[(0,) * first.ndim]
 
 
 def local(key_branch, value_branch, query_branch, long_filter, skip_weight, out_weight, cotangent):
@@ -78,10 +86,14 @@
     norm_scale = 1.0 / math.sqrt(seq_len)
     tab = tables(seq_len)
     at_h = lax.axis_index("h")
+    at_m = lax.axis_index("m")
     at_ctx = lax.axis_index(CTX)
 
-    cot_mine = swap_hm(cotangent)
-    cot_line = lax.all_gather(cot_mine, LINE, axis=0)
+    weights = lax.all_gather(out_weight, PLANE, axis=1, tiled=True)
+
+    cot_same = across(cotangent, lambda h, m: (m, h))
+    cot_swap = across(cotangent, lambda h, m: (m, 1 - h))
+    cot_pair = jnp.where(at_m == 0, jnp.stack([cot_same, cot_swap]), jnp.stack([cot_swap, cot_same]))
 
     product = key_branch * value_branch
     sent = jnp.concatenate(
@@ -92,8 +104,8 @@
     query_far = other_h(query_own)
     query_both = jnp.where(at_h == 0, jnp.stack([query_own, query_far]), jnp.stack([query_far, query_own]))
 
-    weights = lax.all_to_all(jnp.broadcast_to(out_weight[None], (16,) + out_weight.shape), PLANE, 0, 0)
-    weights = weights.transpose(1, 0, 2).reshape(chans, -1)
+    cot_pair = tie(cot_pair, signals)
+    cot_line = lax.all_to_all(jnp.broadcast_to(cot_pair[None], (4,) + cot_pair.shape), "l", 0, 0)
 
     spectra = forward_fourier(signals, tab)
     prod_real, prod_imag = halves(spectra[:, :group])
@@ -104,6 +116,7 @@
     skip = lax.dynamic_slice(skip_weight, (at_ctx * group,), (group,))[None, :, None]
     chan_product = signals[:, :group]
     gate_chan = conv + skip * chan_product
+    gate_chan = tie(tie(gate_chan, cot_line), weights)
     gate_pair = gate_chan.reshape(2, 16, group, rows).transpose(1, 0, 2, 3)
     gate_sent = jnp.broadcast_to(gate_pair[None], (2,) + gate_pair.shape).reshape(n_ctx, 2, group, rows)
     gate_got = lax.all_to_all(gate_sent, CTX, 0, 0)
@@ -111,9 +124,17 @@
     mixed = query_both * gate_both
     mixed_flat = mixed.transpose(1, 0, 2).reshape(chans, 2 * rows)
 
+    partial = lax.dot_general(
+        mixed_flat, weights, (((0,), (0,)), ((), ())), precision=close, preferred_element_type=jnp.float32
+    )
+    partial = partial.reshape(2, rows, 4, 2, chans).transpose(3, 0, 2, 1, 4).reshape(2, 8, rows, chans)
+    partial = lax.all_to_all(partial, "k", 0, 0).sum(0)
+    projected = lax.psum_scatter(partial, LINE, scatter_dimension=0, tiled=False)
+    projected = across(projected, lambda h, m: (m, h))
+
     cot_cores = lax.all_to_all(jnp.broadcast_to(cot_line[None], (2,) + cot_line.shape), "k", 0, 0)
     cot_full = (
-        cot_cores.reshape(2, 2, 4, rows, chans).transpose(1, 3, 2, 0, 4).reshape(2 * rows, 8 * chans)
+        cot_cores.transpose(2, 3, 1, 0, 4).reshape(2 * rows, 8 * chans)
     )
 
     mixed_grad = lax.dot_general(
@@ -128,14 +149,6 @@
     far_grad = lax.dynamic_index_in_dim(mixed_grad, 1 - at_h, 0, False)
     own_gate = lax.dynamic_index_in_dim(gate_both, at_h, 0, False)
     query_grad = ((own_grad + other_h(far_grad)) * own_gate).T
-
-    partial = lax.dot_general(
-        mixed_flat, weights, (((0,), (0,)), ((), ())), precision=close, preferred_element_type=jnp.float32
-    )
-    partial = partial.reshape(2, rows, 4, 2, chans).transpose(3, 0, 2, 1, 4).reshape(2, 8, rows, chans)
-    partial = lax.all_to_all(partial, "k", 0, 0).sum(0)
-    projected = lax.psum_scatter(partial, LINE, scatter_dimension=0, tiled=False)
-    projected = swap_hm(projected)
 
     weight_part = lax.dot_general(
         mixed_flat, cot_full, (((1,), (0,)), ((), ())), precision=close, preferred_element_type=jnp.float32

time: 318 us -> 295 us (0.928)
  waiting for transfers between devices: 109 us -> 88 us
  local copies, waits for them, and re-layouts: 40.6 us -> 30.5 us
  starting transfers between devices: 121 us -> 116 us
    all_gather x1, waiting for transfers between devices: 42.2 us -> 30 us  [local(): weights = lax.all_gather(out_weight, PLANE, axis=1, tiled=True)]
    all_to_all x2 -> x1, waiting for transfers between devices: 10.5 us -> 0.01 us  [local(): lax.all_to_all(jnp.broadcast_to(cot_pair[None], (4,) + cot_pair.shape), '...]
    all_to_all x0 -> x1, blocking collectives: none -> 7.27 us  [local(): partial = lax.all_to_all(partial, 'k', 0, 0).sum(0)]
    all_to_all x1, starting transfers between devices: 6.99 us -> 13.8 us  [local(): grad_got = lax.all_to_all(grad_sent, CTX, 0, 0)]
    all_to_all x2 -> x1, starting transfers between devices: 10 us -> 3.51 us  [local(): lax.all_to_all(jnp.broadcast_to(cot_pair[None], (4,) + cot_pair.shape), '...]
    ppermute x2 -> x3, starting transfers between devices: 37.3 us -> 32.4 us  [across(): return lax.ppermute(block, ('h', 'm'), pairs)]
    all_to_all x1, blocking collectives: 12.3 us -> 7.64 us  [local(): lax.all_to_all(jnp.broadcast_to(cot_line[None], (2,) + cot_line.shape), '...]
    all_to_all x1, waiting for transfers between devices: 20.1 us -> 16 us  [local(): weight_grad = lax.all_to_all(weight_part, PLANE, 0, 0).sum(0) * norm_scale]
  transfers between devices with their start and end apart: 13 -> 13, of which waited for: 9 -> 8; matrix products, arithmetic and copies ran while one was open for 15% -> 14% of each run, Pallas kernels for 0% -> 0%
where the time goes in v2:
time: 295 us; the launch traced here: 290 us
  starting transfers between devices  116 us (39%)
  waiting for transfers between devices  88 us (30%)
  local copies, waits for them, and re-layouts  30.5 us (10%)
  between operations  16.7 us (6%)
  blocking collectives  14.9 us (5%)
  matrix products  12.8 us (4%)
  other arithmetic  10.9 us (4%)
    ppermute x3, starting transfers between devices, across(): return lax.ppermute(block, ('h', 'm'), pairs)  32.4 us
    all_gather x1, waiting for transfers between devices, local(): weights = lax.all_gather(out_weight, PLANE, axis=1, tiled=True)  30 us
    ppermute x2, starting transfers between devices, other_h(): return lax.ppermute(block, 'h', [(0, 1), (1, 0)])  23.7 us
    all_to_all x1, waiting for transfers between devices, local(): weight_grad = lax.all_to_all(weight_part, PLANE, 0, 0).sum(0) * norm_scale  16 us
    all_to_all x1, starting transfers between devices, local(): signals = lax.all_to_all(sent, CTX, 0, 0)  15.5 us
    ppermute x3, waiting for transfers between devices, across(): return lax.ppermute(block, ('h', 'm'), pairs)  15.1 us
    ppermute x2, waiting for transfers between devices, other_h(): return lax.ppermute(block, 'h', [(0, 1), (1, 0)])  14.3 us
    all_to_all x1, starting transfers between devices, local(): grad_got = lax.all_to_all(grad_sent, CTX, 0, 0)  13.8 us
  transfers between devices with their start and end apart: 13, of which 8 were waited for; matrix products, arithmetic and copies ran while one was open for 14% of the time, Pallas kernels for 0%

profile of v2, /device:TPU:129, one launch (start us, length us, event | category | flops | bytes accessed | tf_op | source)
XLA Modules:
  0.0 290.2 jit_solution(17169942520298958060)
XLA Ops:
  7.2 1.0 copy.118
  8.2 1.0 copy.119
  9.2 1.0 copy.120
  10.3 0.7 pad_maximum_fusion.8
  11.0 15.5 %all-to-all-start = ((f32[32,16,128]{2,1,0:T(8,128)}), f32[32,16,128]{2,1,0:T(8,128)S(1)}, u32[]{:S(2)}, u32[]{:S(2)}) async-start(f32[32,16,128]{2,1,0:T(8,128)} %pad_maximum_fusion.8), calls=%async_computation | async-start | bytes 524288 | tf_op jit(solution)/shard_map/all_to_all | solution.py:102
  27.2 10.0 %collective-permute-start.1 = (f32[128,256]{1,0:T(8,128)S(1)}, f32[128,256]{1,0:T(8,128)S(1)}, u32[]{:S(2)}, u32[]{:S(2)}) collective-permute-start(f32[128,256]{1,0:T(8,128)S(1)} %copy-done.21), channel_id=1, source_target_pairs={{0,0},{8,256},{256,8},{264,264},{1,1},{9,257},{257,9},{265,265},{2... | collective-permute-start | bytes 393224 | tf_op jit(solution)/shard_map/ppermute | solution.py:70
  37.3 2.5 collective-permute-start.2
  39.8 3.5 %all-to-all-done = f32[32,16,128]{2,1,0:T(8,128)S(1)} async-done(((f32[32,16,128]{2,1,0:T(8,128)}), f32[32,16,128]{2,1,0:T(8,128)S(1)}, u32[]{:S(2)}, u32[]{:S(2)}) %all-to-all-start) | async-done | bytes 262176 | tf_op jit(solution)/shard_map/all_to_all | solution.py:102
  44.4 14.5 %collective-permute-done.1 = f32[128,256]{1,0:T(8,128)S(1)} collective-permute-done((f32[128,256]{1,0:T(8,128)S(1)}, f32[128,256]{1,0:T(8,128)S(1)}, u32[]{:S(2)}, u32[]{:S(2)}) %collective-permute-start.1) | collective-permute-done | bytes 131104 | tf_op jit(solution)/shard_map/ppermute | solution.py:70
  59.2 1.3 broadcast_in_dim.8
  60.4 3.5 %all-to-all-start.1 = ((f32[4,2,128,256]{2,1,3,0:T(2,128)}), f32[4,2,128,256]{2,1,3,0:T(2,128)S(1)}, u32[]{:S(2)}, u32[]{:S(2)}) async-start(f32[4,2,128,256]{2,1,3,0:T(2,128)} %broadcast_in_dim.8), calls=%async_computation.1 | async-start | bytes 2097152 | tf_op jit(solution)/shard_map/all_to_all | solution.py:108
  65.8 0.8 fusion.40
  67.0 30.0 %all-gather.2.cloned.1.call-done = f32[256,2048]{1,0:T(8,128)} async-done(((f32[256,128]{1,0:T(8,128)}), f32[256,2048]{1,0:T(8,128)}) %all-gather.2.cloned.1.call-update) | async-done | bytes 2097168 | tf_op jit(solution)/shard_map/all_gather | solution.py:92
  97.0 1.2 slice.109
  101.0 7.6 %all_to_all.40 = f32[2,4,2,128,256]{3,2,4,1,0:T(2,128)} all-to-all(f32[2,4,2,128,256]{3,2,4,1,0:T(2,128)S(1)} %broadcast_in_dim.10), channel_id=1, replica_groups=mesh['h'=2,'y'=4,'x'=4,'m'=2,'l'=4,'k'=2] {'k'}, dimensions={0} | all-to-all | bytes 4194304 | tf_op jit(solution)/shard_map/all_to_all | solution.py:135
  108.7 0.7 broadcast_in_dim.9
  109.4 10.5 %all-to-all-start.2 = ((f32[32,2,8,128]{3,2,1,0:T(8,128)}), f32[32,2,8,128]{3,2,1,0:T(8,128)S(1)}, u32[]{:S(2)}, u32[]{:S(2)}) async-start(f32[32,2,8,128]{3,2,1,0:T(8,128)} %bitcast.19), calls=%async_computation.2 | async-start | bytes 524288 | tf_op jit(solution)/shard_map/all_to_all | solution.py:122
  120.0 11.9 %collective-permute-start = (f32[256,128]{1,0:T(8,128)S(1)}, f32[256,128]{1,0:T(8,128)S(1)}, u32[]{:S(2)}, u32[]{:S(2)}) collective-permute-start(f32[256,128]{1,0:T(8,128)S(1)} %bitcast.132), channel_id=1, source_target_pairs={{0,256},{256,0},{1,257},{257,1},{2,258},{258,2},{3,259},{259,3},{4... | collective-permute-start | bytes 393224 | tf_op jit(solution)/shard_map/ppermute | solution.py:74
  131.9 1.8 copy.129
  133.7 6.1 %copy.131 = f32[2,128,4,2,256]{4,3,2,1,0:T(2,128)} copy(f32[2,128,4,2,256]{1,0,4,2,3:T(2,128)} %bitcast.122) | data formatting | bytes 4194304 | tf_op jit(solution)/shard_map/transpose | solution.py:137
  139.9 2.9 %reshape.120 = f32[256,2048]{1,0:T(8,128)S(1)} reshape(f32[2,128,4,2,256]{4,3,2,1,0:T(2,128)} %copy.131) | data formatting | bytes 4194304 | tf_op jit(solution)/shard_map/reshape | solution.py:137
  142.8 2.6 fusion.43
  146.4 1.2 fusion.28
  147.5 0.7 copy.133
  148.4 2.6 fusion.26
  151.2 7.3 %all_to_all.41 = f32[2,8,128,256]{3,2,1,0:T(8,128)} all-to-all(f32[2,8,128,256]{3,2,1,0:T(8,128)S(1)} %copy.130), channel_id=1, replica_groups=mesh['h'=2,'y'=4,'x'=4,'m'=2,'l'=4,'k'=2] {'k'}, dimensions={0} | all-to-all | bytes 4194304 | tf_op jit(solution)/shard_map/all_to_all | solution.py:131
  158.5 13.8 %all-to-all-start.5 = ((f32[32,2,8,128]{3,2,1,0:T(8,128)}), f32[32,2,8,128]{3,2,1,0:T(8,128)S(1)}, u32[]{:S(2)}, u32[]{:S(2)}) async-start(f32[32,2,8,128]{3,2,1,0:T(8,128)} %copy.133), calls=%async_computation.6 | async-start | bytes 524288 | tf_op jit(solution)/shard_map/all_to_all | solution.py:145
  172.5 1.9 copy.147
  174.3 3.0 %reduce_sum.36 = f32[8,128,256]{2,1,0:T(8,128)} reduce(f32[2,8,128,256]{3,2,1,0:T(8,128)} %all_to_all.41, f32[]{:T(128)} %constant.64.clone.1), dimensions={0}, to_apply=%region_0.1 | reduce | flops 262144 | bytes 3145732 | tf_op jit(solution)/shard_map/reduce_sum | solution.py:131
  177.4 3.2 %convolution_bitcast_fusion = f32[16,256,128]{2,1,0:T(8,128)} fusion(f32[256,256,1]{0,1,2:T(8,128)S(1)} %bitcast.125, f32[16,128,256]{2,1,0:T(8,128)S(1)} %bitcast.123), kind=kOutput, calls=%fused_computation | convolution fusion | flops 805306368 | bytes 4456448 | tf_op jit(solution)/shard_map/dot_general | solution.py:153
  180.6 8.5 %all-to-all-done.5 = f32[32,2,8,128]{3,2,1,0:T(8,128)S(1)} async-done(((f32[32,2,8,128]{3,2,1,0:T(8,128)}), f32[32,2,8,128]{3,2,1,0:T(8,128)S(1)}, u32[]{:S(2)}, u32[]{:S(2)}) %all-to-all-start.5) | async-done | bytes 262176 | tf_op jit(solution)/shard_map/all_to_all | solution.py:145
  189.8 3.7 %all-to-all-start.7 = ((f32[16,256,128]{2,1,0:T(8,128)}), f32[16,256,128]{2,1,0:T(8,128)S(1)}, u32[]{:S(2)}, u32[]{:S(2)}) async-start(f32[16,256,128]{2,1,0:T(8,128)} %convolution_bitcast_fusion), calls=%async_computation.8 | async-start | bytes 4194304 | tf_op jit(solution)/shard_map/all_to_all | solution.py:157
  193.6 1.0 reduce_sum.37
  195.1 0.8 multiply_add_fusion.2
  196.4 1.1 fusion.21
  197.6 0.9 fusion.2
  199.3 0.9 copy.142
  200.3 16.0 %all-to-all-done.7 = f32[16,256,128]{2,1,0:T(8,128)S(1)} async-done(((f32[16,256,128]{2,1,0:T(8,128)}), f32[16,256,128]{2,1,0:T(8,128)S(1)}, u32[]{:S(2)}, u32[]{:S(2)}) %all-to-all-start.7) | async-done | bytes 2097184 | tf_op jit(solution)/shard_map/all_to_all | solution.py:157
  216.3 13.0 %all-to-all-start.6 = ((f32[32,17,128]{2,1,0:T(8,128)}), f32[32,17,128]{2,1,0:T(8,128)S(1)}, u32[]{:S(2)}, u32[]{:S(2)}) async-start(f32[32,17,128]{2,1,0:T(8,128)} %copy.142), calls=%async_computation.7 | async-start | bytes 786432 | tf_op jit(solution)/shard_map/all_to_all | solution.py:170
  229.3 0.8 copy.146
  230.0 11.8 %collective-permute-start.4 = (f32[256,128]{1,0:T(8,128)}, f32[256,128]{1,0:T(8,128)S(1)}, u32[]{:S(2)}, u32[]{:S(2)}) collective-permute-start(f32[256,128]{1,0:T(8,128)} %bitcast.50), channel_id=1, source_target_pairs={{0,256},{256,0},{1,257},{257,1},{2,258},{258,2},{3,259},{259,3},{4... | collective-permute-start | bytes 393224 | tf_op jit(solution)/shard_map/ppermute | solution.py:74
  242.0 14.2 %collective-permute-done.4 = f32[256,128]{1,0:T(8,128)S(1)} collective-permute-done((f32[256,128]{1,0:T(8,128)}, f32[256,128]{1,0:T(8,128)S(1)}, u32[]{:S(2)}, u32[]{:S(2)}) %collective-permute-start.4) | collective-permute-done | bytes 131104 | tf_op jit(solution)/shard_map/ppermute | solution.py:74
  256.8 0.9 fusion.29
  257.7 0.8 copy.151
  259.3 19.9 %collective-permute-start.3 = (f32[128,256]{1,0:T(8,128)}, f32[128,256]{1,0:T(8,128)S(1)}, u32[]{:S(2)}, u32[]{:S(2)}) collective-permute-start(f32[128,256]{1,0:T(8,128)} %bitcast.138), channel_id=1, source_target_pairs={{0,0},{8,256},{256,8},{264,264},{1,1},{9,257},{257,9},{265,265},{2... | collective-permute-start | bytes 393224 | tf_op jit(solution)/shard_map/ppermute | solution.py:70
  279.2 0.8 copy.149
  280.0 0.8 copy.150
  280.7 0.8 copy.152
  (101 shorter events, 12.5 us)
Async XLA Ops:
  7.2 20.0 %copy-start.21 = (f32[128,256]{1,0:T(8,128)S(1)}, f32[128,256]{1,0:T(8,128)}, u32[]{:S(2)}) copy-start(f32[128,256]{1,0:T(8,128)} %param.19) | copy-start | bytes 393220
  11.0 32.3 %all-to-all-start = ((f32[32,16,128]{2,1,0:T(8,128)}), f32[32,16,128]{2,1,0:T(8,128)S(1)}, u32[]{:S(2)}, u32[]{:S(2)}) async-start(f32[32,16,128]{2,1,0:T(8,128)} %pad_maximum_fusion.8), calls=%async_computation | async-start | bytes 524288 | tf_op jit(solution)/shard_map/all_to_all | solution.py:102
  26.5 70.5 %all-gather.2.cloned.1.call-start = ((), (), s32[]{:S(2)}) async-start(), calls=%async_computation.9 | async-start | bytes 2228224 | tf_op jit(solution)/shard_map/all_gather | solution.py:92
  27.2 31.7 %collective-permute-start.1 = (f32[128,256]{1,0:T(8,128)S(1)}, f32[128,256]{1,0:T(8,128)S(1)}, u32[]{:S(2)}, u32[]{:S(2)}) collective-permute-start(f32[128,256]{1,0:T(8,128)S(1)} %copy-done.21), channel_id=1, source_target_pairs={{0,0},{8,256},{256,8},{264,264},{1,1},{9,257},{257,9},{265,265},{2... | collective-permute-start | bytes 393224 | tf_op jit(solution)/shard_map/ppermute | solution.py:70
  37.3 21.7 %collective-permute-start.2 = (f32[128,256]{1,0:T(8,128)S(1)}, f32[128,256]{1,0:T(8,128)S(1)}, u32[]{:S(2)}, u32[]{:S(2)}) collective-permute-start(f32[128,256]{1,0:T(8,128)S(1)} %copy-done.21), channel_id=1, source_target_pairs={{0,8},{8,264},{256,0},{264,256},{1,9},{9,265},{257,1},{265,257},{2... | collective-permute-start | bytes 393224 | tf_op jit(solution)/shard_map/ppermute | solution.py:70
  59.0 5.0 %copy-start.22 = (f32[256]{0:T(256)S(1)}, f32[256]{0:T(256)}, u32[]{:S(2)}) copy-start(f32[256]{0:T(256)} %param.17) | copy-start | bytes 3076
  59.1 5.0 %copy-start.20 = (f32[66,32,1]{0,1,2:T(8,128)S(1)}, f32[66,32,1]{0,1,2:T(8,128)}, u32[]{:S(2)}) copy-start(f32[66,32,1]{0,1,2:T(8,128)} %constant.80) | copy-start | bytes 25348
  59.1 5.7 %copy-start.10 = (f32[33,128]{1,0:T(8,128)S(1)}, f32[33,128]{1,0:T(8,128)}, u32[]{:S(2)}) copy-start(f32[33,128]{1,0:T(8,128)} %constant.69.clone) | copy-start | bytes 50692
  59.1 5.7 %copy-start.12 = (f32[33,128]{1,0:T(8,128)S(1)}, f32[33,128]{1,0:T(8,128)}, u32[]{:S(2)}) copy-start(f32[33,128]{1,0:T(8,128)} %constant.70.clone) | copy-start | bytes 50692
  60.4 38.4 %all-to-all-start.1 = ((f32[4,2,128,256]{2,1,3,0:T(2,128)}), f32[4,2,128,256]{2,1,3,0:T(2,128)S(1)}, u32[]{:S(2)}, u32[]{:S(2)}) async-start(f32[4,2,128,256]{2,1,3,0:T(2,128)} %broadcast_in_dim.8), calls=%async_computation.1 | async-start | bytes 2097152 | tf_op jit(solution)/shard_map/all_to_all | solution.py:108
  63.9 1.1 copy-start.4
  64.1 35.9 %copy-start.7 = (f32[32,16,128]{2,0,1:T(8,128)}, f32[32,16,128]{2,0,1:T(8,128)S(1)}, u32[]{:S(2)}) copy-start(f32[32,16,128]{2,0,1:T(8,128)S(1)} %copy.121) | copy-start | bytes 786436
  65.0 1.6 copy-start.2
  65.0 35.0 %copy-start.17 = (f32[32,66,1]{1,0,2:T(8,128)S(1)}, f32[32,66,1]{1,0,2:T(8,128)}, u32[]{:S(2)}) copy-start(f32[32,66,1]{1,0,2:T(8,128)} %constant.79) | copy-start | bytes 25348
  101.0 18.9 %copy-start.16 = (f32[128,256]{1,0:T(8,128)S(1)}, f32[128,256]{1,0:T(8,128)}, u32[]{:S(2)}) copy-start(f32[128,256]{1,0:T(8,128)} %param.15) | copy-start | bytes 393220
  101.0 30.9 %copy-start = (f32[256,2048]{1,0:T(8,128)S(1)}, f32[256,2048]{1,0:T(8,128)}, u32[]{:S(2)}) copy-start(f32[256,2048]{1,0:T(8,128)} %all-gather.2.cloned.1.call-done) | copy-start | bytes 6291460
  109.4 36.3 %all-to-all-start.2 = ((f32[32,2,8,128]{3,2,1,0:T(8,128)}), f32[32,2,8,128]{3,2,1,0:T(8,128)S(1)}, u32[]{:S(2)}, u32[]{:S(2)}) async-start(f32[32,2,8,128]{3,2,1,0:T(8,128)} %bitcast.19), calls=%async_computation.2 | async-start | bytes 524288 | tf_op jit(solution)/shard_map/all_to_all | solution.py:122
  120.0 13.7 %copy-start.9 = (f32[128,256]{0,1:T(8,128)}, f32[128,256]{0,1:T(8,128)S(1)}, u32[]{:S(2)}) copy-start(f32[128,256]{0,1:T(8,128)S(1)} %copy.117) | copy-start | bytes 393220
  120.0 25.7 %collective-permute-start = (f32[256,128]{1,0:T(8,128)S(1)}, f32[256,128]{1,0:T(8,128)S(1)}, u32[]{:S(2)}, u32[]{:S(2)}) collective-permute-start(f32[256,128]{1,0:T(8,128)S(1)} %bitcast.132), channel_id=1, source_target_pairs={{0,256},{256,0},{1,257},{257,1},{2,258},{258,2},{3,259},{259,3},{4... | collective-permute-start | bytes 393224 | tf_op jit(solution)/shard_map/ppermute | solution.py:74
  145.7 0.7 copy-start.14
  158.5 30.7 %all-to-all-start.5 = ((f32[32,2,8,128]{3,2,1,0:T(8,128)}), f32[32,2,8,128]{3,2,1,0:T(8,128)S(1)}, u32[]{:S(2)}, u32[]{:S(2)}) async-start(f32[32,2,8,128]{3,2,1,0:T(8,128)} %copy.133), calls=%async_computation.6 | async-start | bytes 524288 | tf_op jit(solution)/shard_map/all_to_all | solution.py:145
  172.3 87.1 %reduce-scatter.2.cloned.1.call-start = ((), (), s32[]{:S(2)}) async-start(), calls=%async_computation.10 | async-start | bytes 1179648 | tf_op jit(solution)/shard_map/reduce_scatter | solution.py:132
  174.3 3.0 %copy-start.1 = (f32[2048,256]{1,0:T(8,128)S(1)}, f32[2048,256]{1,0:T(8,128)}, u32[]{:S(2)}) copy-start(f32[2048,256]{1,0:T(8,128)} %copy.147) | copy-start | bytes 6291460
  180.6 14.0 %copy-start.19 = (f32[66,32,1]{0,1,2:T(8,128)S(1)}, f32[66,32,1]{0,1,2:T(8,128)}, u32[]{:S(2)}) copy-start(f32[66,32,1]{0,1,2:T(8,128)} %constant.83) | copy-start | bytes 25348
  189.1 0.7 copy-start.6
  189.8 26.4 %all-to-all-start.7 = ((f32[16,256,128]{2,1,0:T(8,128)}), f32[16,256,128]{2,1,0:T(8,128)S(1)}, u32[]{:S(2)}, u32[]{:S(2)}) async-start(f32[16,256,128]{2,1,0:T(8,128)} %convolution_bitcast_fusion), calls=%async_computation.8 | async-start | bytes 4194304 | tf_op jit(solution)/shard_map/all_to_all | solution.py:157
  193.6 2.4 copy-start.5
  195.1 2.5 copy-start.3
  196.4 2.2 copy-start.11
  196.4 2.2 copy-start.13
  197.6 1.1 copy-start.18
  197.6 1.5 copy-start.8
  216.3 43.0 %all-to-all-start.6 = ((f32[32,17,128]{2,1,0:T(8,128)}), f32[32,17,128]{2,1,0:T(8,128)S(1)}, u32[]{:S(2)}, u32[]{:S(2)}) async-start(f32[32,17,128]{2,1,0:T(8,128)} %copy.142), calls=%async_computation.7 | async-start | bytes 786432 | tf_op jit(solution)/shard_map/all_to_all | solution.py:170
  230.0 26.1 %collective-permute-start.4 = (f32[256,128]{1,0:T(8,128)}, f32[256,128]{1,0:T(8,128)S(1)}, u32[]{:S(2)}, u32[]{:S(2)}) collective-permute-start(f32[256,128]{1,0:T(8,128)} %bitcast.50), channel_id=1, source_target_pairs={{0,256},{256,0},{1,257},{257,1},{2,258},{258,2},{3,259},{259,3},{4... | collective-permute-start | bytes 393224 | tf_op jit(solution)/shard_map/ppermute | solution.py:74
  256.2 0.7 copy-start.15
  259.3 23.4 %collective-permute-start.3 = (f32[128,256]{1,0:T(8,128)}, f32[128,256]{1,0:T(8,128)S(1)}, u32[]{:S(2)}, u32[]{:S(2)}) collective-permute-start(f32[128,256]{1,0:T(8,128)} %bitcast.138), channel_id=1, source_target_pairs={{0,0},{8,256},{256,8},{264,264},{1,1},{9,257},{257,9},{265,265},{2... | collective-permute-start | bytes 393224 | tf_op jit(solution)/shard_map/ppermute | solution.py:70
Sparse Core Ops, SparseCore 0:
  30.3 66.6 all-gather.1
  177.5 56.9 reduce-scatter.1

commit v3 on v2

--- a/solution.py
+++ b/solution.py
@@ -116,7 +116,7 @@
     skip = lax.dynamic_slice(skip_weight, (at_ctx * group,), (group,))[None, :, None]
     chan_product = signals[:, :group]
     gate_chan = conv + skip * chan_product
-    gate_chan = tie(tie(gate_chan, cot_line), weights)
+    gate_chan = tie(gate_chan, cot_line)
     gate_pair = gate_chan.reshape(2, 16, group, rows).transpose(1, 0, 2, 3)
     gate_sent = jnp.broadcast_to(gate_pair[None], (2,) + gate_pair.shape).reshape(n_ctx, 2, group, rows)
     gate_got = lax.all_to_all(gate_sent, CTX, 0, 0)
@@ -130,8 +130,7 @@
     partial = partial.reshape(2, rows, 4, 2, chans).transpose(3, 0, 2, 1, 4).reshape(2, 8, rows, chans)
     partial = lax.all_to_all(partial, "k", 0, 0).sum(0)
     projected = lax.psum_scatter(partial, LINE, scatter_dimension=0, tiled=False)
-    projected = across(projected, lambda h, m: (m, h))
-
+    cot_line = tie(cot_line, gate_got)
     cot_cores = lax.all_to_all(jnp.broadcast_to(cot_line[None], (2,) + cot_line.shape), "k", 0, 0)
     cot_full = (
         cot_cores.transpose(2, 3, 1, 0, 4).reshape(2 * rows, 8 * chans)
@@ -141,14 +140,15 @@
         weights, cot_full, (((1,), (1,)), ((), ())), precision=close, preferred_element_type=jnp.float32
     )
     mixed_grad = mixed_grad.reshape(chans, 2, rows).transpose(1, 0, 2)
-    grad_sent = (mixed_grad * query_both).reshape(2, n_ctx, group, rows).transpose(1, 0, 2, 3)
+    grad_sent = tie(mixed_grad * query_both, partial).reshape(2, n_ctx, group, rows).transpose(1, 0, 2, 3)
     grad_got = lax.all_to_all(grad_sent, CTX, 0, 0)
     grad_chan = grad_got.reshape(2, 16, 2, group, rows).sum(0).transpose(1, 0, 2, 3).reshape(n_ctx, group, rows)
 
     own_grad = lax.dynamic_index_in_dim(mixed_grad, at_h, 0, False)
     far_grad = lax.dynamic_index_in_dim(mixed_grad, 1 - at_h, 0, False)
     own_gate = lax.dynamic_index_in_dim(gate_both, at_h, 0, False)
-    query_grad = ((own_grad + other_h(far_grad)) * own_gate).T
+    far_grad = other_h(far_grad)
+    query_grad = ((own_grad + far_grad) * own_gate).T
 
     weight_part = lax.dot_general(
         mixed_flat, cot_full, (((1,), (0,)), ((), ())), precision=close, preferred_element_type=jnp.float32
@@ -167,7 +167,9 @@
     prod_grad = lagged[:, :group] + skip * grad_chan
     skip_part = jnp.sum(grad_chan * chan_product, axis=(0, 2)) * norm_scale
     skip_row = jnp.broadcast_to(jnp.pad(skip_part, (0, rows - group))[None, None], (n_ctx, 1, rows))
-    back = lax.all_to_all(jnp.concatenate([prod_grad, lagged[:, group:] * norm_scale, skip_row], 1), CTX, 0, 0)
+    back_sent = jnp.concatenate([tie(tie(tie(prod_grad, weight_grad), projected), far_grad), lagged[:, group:] * norm_scale, skip_row], 1)
+    back = lax.all_to_all(back_sent, CTX, 0, 0)
+    projected = across(projected, lambda h, m: (m, h))
     product_grad = back[:, :group].reshape(chans, rows).T
     filter_grad = back[:, group : 2 * group].reshape(chans, rows).T
     skip_grad = back[:, 2 * group, :group].reshape(chans)

time: 295 us -> 313 us (1.061)
  the two profiles are of different devices: /device:TPU:129 before, /device:TPU:32 now
where the time goes in v3:
time: 313 us; the launch traced here: 312 us
  waiting for transfers between devices  131 us (42%)
  starting transfers between devices  94.8 us (30%)
  local copies, waits for them, and re-layouts  32.1 us (10%)
  between operations  19.5 us (6%)
  matrix products  14.3 us (5%)
  blocking collectives  11.7 us (4%)
  other arithmetic  7.72 us (2%)
    all_to_all x1, waiting for transfers between devices, local(): back = lax.all_to_all(back_sent, CTX, 0, 0)  28.6 us
    ppermute x2, starting transfers between devices, other_h(): return lax.ppermute(block, 'h', [(0, 1), (1, 0)])  24.9 us
    all_to_all x1, waiting for transfers between devices, local(): signals = lax.all_to_all(sent, CTX, 0, 0)  23.6 us
    all_to_all x1, waiting for transfers between devices, local(): weight_grad = lax.all_to_all(weight_part, PLANE, 0, 0).sum(0) * norm_scale  23.5 us
    all_to_all x1, starting transfers between devices, local(): signals = lax.all_to_all(sent, CTX, 0, 0)  19.7 us
    all_gather x1, waiting for transfers between devices, local(): weights = lax.all_gather(out_weight, PLANE, axis=1, tiled=True)  18 us
    all_to_all x1, waiting for transfers between devices, local(): lax.all_to_all(jnp.broadcast_to(cot_pair[None], (4,) + cot_pair.shape), '...  15.4 us
    all_to_all x1, starting transfers between devices, local(): grad_got = lax.all_to_all(grad_sent, CTX, 0, 0)  14.1 us
  transfers between devices with their start and end apart: 13, of which 7 were waited for; matrix products, arithmetic and copies ran while one was open for 8% of the time, Pallas kernels for 0%

profile of v3, /device:TPU:32, one launch (start us, length us, event | category | flops | bytes accessed | tf_op | source)
XLA Modules:
  0.0 311.5 jit_solution(10311018351108746189)
XLA Ops:
  7.2 1.0 copy.127
  8.2 1.0 copy.128
  9.2 1.0 copy.129
  10.3 0.7 pad_maximum_fusion.8
  11.0 19.7 %all-to-all-start = ((f32[32,16,128]{2,1,0:T(8,128)}), f32[32,16,128]{2,1,0:T(8,128)S(1)}, u32[]{:S(2)}, u32[]{:S(2)}) async-start(f32[32,16,128]{2,1,0:T(8,128)} %pad_maximum_fusion.8), calls=%async_computation | async-start | bytes 524288 | tf_op jit(solution)/shard_map/all_to_all | solution.py:102
  30.7 4.3 %collective-permute-start.2 = (f32[128,256]{1,0:T(8,128)S(1)}, f32[128,256]{1,0:T(8,128)S(1)}, u32[]{:S(2)}, u32[]{:S(2)}) collective-permute-start(f32[128,256]{1,0:T(8,128)S(1)} %copy-done.29), channel_id=1, source_target_pairs={{0,8},{8,264},{256,0},{264,256},{1,9},{9,265},{257,1},{265,257},{2... | collective-permute-start | bytes 393224 | tf_op jit(solution)/shard_map/ppermute | solution.py:70
  35.7 23.6 %all-to-all-done = f32[32,16,128]{2,1,0:T(8,128)S(1)} async-done(((f32[32,16,128]{2,1,0:T(8,128)}), f32[32,16,128]{2,1,0:T(8,128)S(1)}, u32[]{:S(2)}, u32[]{:S(2)}) %all-to-all-start) | async-done | bytes 262176 | tf_op jit(solution)/shard_map/all_to_all | solution.py:102
  60.4 7.4 %collective-permute-done.2 = f32[128,256]{1,0:T(8,128)S(1)} collective-permute-done((f32[128,256]{1,0:T(8,128)S(1)}, f32[128,256]{1,0:T(8,128)S(1)}, u32[]{:S(2)}, u32[]{:S(2)}) %collective-permute-start.2) | collective-permute-done | bytes 131104 | tf_op jit(solution)/shard_map/ppermute | solution.py:70
  67.9 1.1 broadcast_in_dim.8
  69.0 3.6 %all-to-all-start.1 = ((f32[4,2,128,256]{3,2,1,0:T(8,128)}), f32[4,2,128,256]{3,2,1,0:T(8,128)S(1)}, u32[]{:S(2)}, u32[]{:S(2)}) async-start(f32[4,2,128,256]{3,2,1,0:T(8,128)} %broadcast_in_dim.8), calls=%async_computation.1 | async-start | bytes 2097152 | tf_op jit(solution)/shard_map/all_to_all | solution.py:108
  74.5 0.7 fusion.7
  75.2 0.8 fusion.43
  76.5 15.4 %all-to-all-done.1 = f32[4,2,128,256]{3,2,1,0:T(8,128)S(1)} async-done(((f32[4,2,128,256]{3,2,1,0:T(8,128)}), f32[4,2,128,256]{3,2,1,0:T(8,128)S(1)}, u32[]{:S(2)}, u32[]{:S(2)}) %all-to-all-start.1) | async-done | bytes 1048608 | tf_op jit(solution)/shard_map/all_to_all | solution.py:108
  93.5 0.7 broadcast_in_dim.9
  94.3 10.6 %all-to-all-start.2 = ((f32[32,2,8,128]{3,2,1,0:T(8,128)}), f32[32,2,8,128]{3,2,1,0:T(8,128)S(1)}, u32[]{:S(2)}, u32[]{:S(2)}) async-start(f32[32,2,8,128]{3,2,1,0:T(8,128)} %bitcast.18), calls=%async_computation.2 | async-start | bytes 524288 | tf_op jit(solution)/shard_map/all_to_all | solution.py:122
  105.0 12.4 %collective-permute-start = (f32[256,128]{1,0:T(8,128)S(1)}, f32[256,128]{1,0:T(8,128)S(1)}, u32[]{:S(2)}, u32[]{:S(2)}) collective-permute-start(f32[256,128]{1,0:T(8,128)S(1)} %bitcast.136), channel_id=1, source_target_pairs={{0,256},{256,0},{1,257},{257,1},{2,258},{258,2},{3,259},{259,3},{4... | collective-permute-start | bytes 393224 | tf_op jit(solution)/shard_map/ppermute | solution.py:74
  117.4 18.0 %all-gather.2.cloned.1.call-done = f32[256,2048]{1,0:T(8,128)} async-done(((f32[256,128]{1,0:T(8,128)}), f32[256,2048]{1,0:T(8,128)}) %all-gather.2.cloned.1.call-update) | async-done | bytes 2097168 | tf_op jit(solution)/shard_map/all_gather | solution.py:92
  135.5 2.9 copy.137
  141.0 5.4 %all_to_all.40 = f32[2,4,2,128,256]{3,2,4,1,0:T(2,128)S(1)} all-to-all(f32[2,4,2,128,256]{3,2,4,1,0:T(2,128)S(1)} %broadcast_in_dim.10), channel_id=1, replica_groups=mesh['h'=2,'y'=4,'x'=4,'m'=2,'l'=4,'k'=2] {'k'}, dimensions={0} | all-to-all | bytes 4194304 | tf_op jit(solution)/shard_map/all_to_all | solution.py:134
  146.4 3.8 %copy.141 = f32[2,128,4,2,256]{4,3,2,1,0:T(2,128)} copy(f32[2,128,4,2,256]{1,0,4,2,3:T(2,128)S(1)} %bitcast.129) | data formatting | bytes 4194304 | tf_op jit(solution)/shard_map/transpose | solution.py:136
  150.2 2.9 reshape.128
  153.1 2.6 fusion.46
  155.8 0.8 copy.142
  156.7 2.6 fusion.25
  159.5 6.3 %all_to_all.41 = f32[2,8,128,256]{3,2,1,0:T(8,128)} all-to-all(f32[2,8,128,256]{3,2,1,0:T(8,128)S(1)} %copy.138), channel_id=1, replica_groups=mesh['h'=2,'y'=4,'x'=4,'m'=2,'l'=4,'k'=2] {'k'}, dimensions={0} | all-to-all | bytes 4194304 | tf_op jit(solution)/shard_map/all_to_all | solution.py:131
  165.8 1.9 reduce_sum.36
  168.9 1.2 fusion.28
  170.1 0.7 copy.143
  170.8 14.1 %all-to-all-start.5 = ((f32[32,2,8,128]{3,2,1,0:T(8,128)}), f32[32,2,8,128]{3,2,1,0:T(8,128)}, u32[]{:S(2)}, u32[]{:S(2)}) async-start(f32[32,2,8,128]{3,2,1,0:T(8,128)} %copy.143), calls=%async_computation.6 | async-start | bytes 524288 | tf_op jit(solution)/shard_map/all_to_all | solution.py:144
  185.7 1.6 constant_dynamic-slice_fusion
  187.4 12.5 %collective-permute-start.4 = (f32[256,128]{1,0:T(8,128)S(1)}, f32[256,128]{1,0:T(8,128)S(1)}, u32[]{:S(2)}, u32[]{:S(2)}) collective-permute-start(f32[256,128]{1,0:T(8,128)S(1)} %bitcast.143), channel_id=1, source_target_pairs={{0,256},{256,0},{1,257},{257,1},{2,258},{258,2},{3,259},{259,3},{4... | collective-permute-start | bytes 393224 | tf_op jit(solution)/shard_map/ppermute | solution.py:74
  199.9 1.8 copy.152
  201.8 4.8 %convolution_bitcast_fusion = f32[16,256,128]{2,1,0:T(8,128)} fusion(f32[256,256,1]{0,1,2:T(8,128)S(1)} %bitcast.131, f32[16,128,256]{2,1,0:T(8,128)} %bitcast.128), kind=kOutput, calls=%fused_computation | convolution fusion | flops 805306368 | bytes 4456448 | tf_op jit(solution)/shard_map/dot_general | solution.py:153
  206.5 13.4 %collective-permute-done.4 = f32[256,128]{1,0:T(8,128)S(1)} collective-permute-done((f32[256,128]{1,0:T(8,128)S(1)}, f32[256,128]{1,0:T(8,128)S(1)}, u32[]{:S(2)}, u32[]{:S(2)}) %collective-permute-start.4) | collective-permute-done | bytes 131104 | tf_op jit(solution)/shard_map/ppermute | solution.py:74
  221.2 5.7 %all-to-all-start.6 = ((f32[16,256,128]{2,1,0:T(8,128)}), f32[16,256,128]{2,1,0:T(8,128)S(1)}, u32[]{:S(2)}, u32[]{:S(2)}) async-start(f32[16,256,128]{2,1,0:T(8,128)} %convolution_bitcast_fusion), calls=%async_computation.7 | async-start | bytes 4194304 | tf_op jit(solution)/shard_map/all_to_all | solution.py:157
  227.0 1.0 reduce_sum.37
  228.5 0.7 copy.151
  229.7 1.2 fusion.20
  231.0 0.9 fusion.1
  232.5 23.5 %all-to-all-done.6 = f32[16,256,128]{2,1,0:T(8,128)S(1)} async-done(((f32[16,256,128]{2,1,0:T(8,128)}), f32[16,256,128]{2,1,0:T(8,128)S(1)}, u32[]{:S(2)}, u32[]{:S(2)}) %all-to-all-start.6) | async-done | bytes 2097184 | tf_op jit(solution)/shard_map/all_to_all | solution.py:157
  257.3 1.2 slice.135
  259.5 0.9 copy.155
  260.4 10.4 %all-to-all-start.7 = ((f32[32,17,128]{2,1,0:T(8,128)}), f32[32,17,128]{2,1,0:T(8,128)S(1)}, u32[]{:S(2)}, u32[]{:S(2)}) async-start(f32[32,17,128]{2,1,0:T(8,128)} %copy.155), calls=%async_computation.8 | async-start | bytes 786432 | tf_op jit(solution)/shard_map/all_to_all | solution.py:171
  271.7 0.8 copy.161
  272.4 28.6 %all-to-all-done.7 = f32[32,17,128]{2,1,0:T(8,128)S(1)} async-done(((f32[32,17,128]{2,1,0:T(8,128)}), f32[32,17,128]{2,1,0:T(8,128)S(1)}, u32[]{:S(2)}, u32[]{:S(2)}) %all-to-all-start.7) | async-done | bytes 278560 | tf_op jit(solution)/shard_map/all_to_all | solution.py:171
  301.0 0.8 copy.160
  302.5 0.8 copy.162
  303.3 0.8 copy.159
  (125 shorter events, 13.1 us)
Async XLA Ops:
  7.2 23.5 %copy-start.29 = (f32[128,256]{1,0:T(8,128)S(1)}, f32[128,256]{1,0:T(8,128)}, u32[]{:S(2)}) copy-start(f32[128,256]{1,0:T(8,128)} %param.19) | copy-start | bytes 393220
  9.2 59.8 %copy-start.4 = (f32[128,256]{0,1:T(8,128)}, f32[128,256]{0,1:T(8,128)S(1)}, u32[]{:S(2)}) copy-start(f32[128,256]{0,1:T(8,128)S(1)} %copy.128) | copy-start | bytes 393220
  11.0 48.2 %all-to-all-start = ((f32[32,16,128]{2,1,0:T(8,128)}), f32[32,16,128]{2,1,0:T(8,128)S(1)}, u32[]{:S(2)}, u32[]{:S(2)}) async-start(f32[32,16,128]{2,1,0:T(8,128)} %pad_maximum_fusion.8), calls=%async_computation | async-start | bytes 524288 | tf_op jit(solution)/shard_map/all_to_all | solution.py:102
  30.7 42.7 %copy-start.31 = (f32[256]{0:T(256)S(1)}, f32[256]{0:T(256)}, u32[]{:S(2)}) copy-start(f32[256]{0:T(256)} %param.17) | copy-start | bytes 3076
  30.7 37.1 %collective-permute-start.2 = (f32[128,256]{1,0:T(8,128)S(1)}, f32[128,256]{1,0:T(8,128)S(1)}, u32[]{:S(2)}, u32[]{:S(2)}) collective-permute-start(f32[128,256]{1,0:T(8,128)S(1)} %copy-done.29), channel_id=1, source_target_pairs={{0,8},{8,264},{256,0},{264,256},{1,9},{9,265},{257,1},{265,257},{2... | collective-permute-start | bytes 393224 | tf_op jit(solution)/shard_map/ppermute | solution.py:70
  35.0 32.8 %collective-permute-start.1 = (f32[128,256]{1,0:T(8,128)S(1)}, f32[128,256]{1,0:T(8,128)S(1)}, u32[]{:S(2)}, u32[]{:S(2)}) collective-permute-start(f32[128,256]{1,0:T(8,128)S(1)} %copy-done.29), channel_id=1, source_target_pairs={{0,0},{8,256},{256,8},{264,264},{1,1},{9,257},{257,9},{265,265},{2... | collective-permute-start | bytes 393224 | tf_op jit(solution)/shard_map/ppermute | solution.py:70
  67.9 5.7 %copy-start.26 = (f32[66,32,1]{0,1,2:T(8,128)S(1)}, f32[66,32,1]{0,1,2:T(8,128)}, u32[]{:S(2)}) copy-start(f32[66,32,1]{0,1,2:T(8,128)} %constant.84) | copy-start | bytes 25348
  69.0 5.3 %copy-start.16 = (f32[33,128]{1,0:T(8,128)S(1)}, f32[33,128]{1,0:T(8,128)}, u32[]{:S(2)}) copy-start(f32[33,128]{1,0:T(8,128)} %constant.74.clone) | copy-start | bytes 50692
  69.0 5.3 %copy-start.18 = (f32[33,128]{1,0:T(8,128)S(1)}, f32[33,128]{1,0:T(8,128)}, u32[]{:S(2)}) copy-start(f32[33,128]{1,0:T(8,128)} %constant.73.clone) | copy-start | bytes 50692
  69.0 22.9 %all-to-all-start.1 = ((f32[4,2,128,256]{3,2,1,0:T(8,128)}), f32[4,2,128,256]{3,2,1,0:T(8,128)S(1)}, u32[]{:S(2)}, u32[]{:S(2)}) async-start(f32[4,2,128,256]{3,2,1,0:T(8,128)} %broadcast_in_dim.8), calls=%async_computation.1 | async-start | bytes 2097152 | tf_op jit(solution)/shard_map/all_to_all | solution.py:108
  72.6 1.8 copy-start.9
  72.6 62.8 %all-gather.2.cloned.1.call-start = ((), (), s32[]{:S(2)}) async-start(), calls=%async_computation.9 | async-start | bytes 2228224 | tf_op jit(solution)/shard_map/all_gather | solution.py:92
  73.5 19.6 %copy-start.27 = (f32[8]{0:T(128)}, f32[8]{0:T(128)S(1)}, u32[]{:S(2)}) copy-start(f32[8]{0:T(128)S(1)} %dynamic_slice.9) | copy-start | bytes 100
  73.6 19.5 %copy-start.11 = (f32[32,16,128]{2,0,1:T(8,128)}, f32[32,16,128]{2,0,1:T(8,128)S(1)}, u32[]{:S(2)}) copy-start(f32[32,16,128]{2,0,1:T(8,128)S(1)} %copy.130) | copy-start | bytes 786436
  74.4 1.6 copy-start.7
  74.5 18.7 %copy-start.24 = (f32[32,66,1]{1,0,2:T(8,128)S(1)}, f32[32,66,1]{1,0,2:T(8,128)}, u32[]{:S(2)}) copy-start(f32[32,66,1]{1,0,2:T(8,128)} %constant.83) | copy-start | bytes 25348
  76.0 28.9 %copy-start.22 = (f32[128,256]{1,0:T(8,128)S(1)}, f32[128,256]{1,0:T(8,128)}, u32[]{:S(2)}) copy-start(f32[128,256]{1,0:T(8,128)} %param.15) | copy-start | bytes 393220
  94.3 44.1 %all-to-all-start.2 = ((f32[32,2,8,128]{3,2,1,0:T(8,128)}), f32[32,2,8,128]{3,2,1,0:T(8,128)S(1)}, u32[]{:S(2)}, u32[]{:S(2)}) async-start(f32[32,2,8,128]{3,2,1,0:T(8,128)} %bitcast.18), calls=%async_computation.2 | async-start | bytes 524288 | tf_op jit(solution)/shard_map/all_to_all | solution.py:122
  105.0 35.3 %copy-start.6 = (f32[128,256]{0,1:T(8,128)}, f32[128,256]{0,1:T(8,128)S(1)}, u32[]{:S(2)}) copy-start(f32[128,256]{0,1:T(8,128)S(1)} %copy.126) | copy-start | bytes 393220
  105.0 35.3 %collective-permute-start = (f32[256,128]{1,0:T(8,128)S(1)}, f32[256,128]{1,0:T(8,128)S(1)}, u32[]{:S(2)}, u32[]{:S(2)}) collective-permute-start(f32[256,128]{1,0:T(8,128)S(1)} %bitcast.136), channel_id=1, source_target_pairs={{0,256},{256,0},{1,257},{257,1},{2,258},{258,2},{3,259},{259,3},{4... | collective-permute-start | bytes 393224 | tf_op jit(solution)/shard_map/ppermute | solution.py:74
  138.4 1.9 copy-start.2
  140.3 0.8 copy-start.15
  155.8 3.5 %copy-start.1 = (f32[256,256]{1,0:T(8,128)}, f32[256,256]{1,0:T(8,128)S(1)}, u32[]{:S(2)}) copy-start(f32[256,256]{1,0:T(8,128)S(1)} %fusion.46) | copy-start | bytes 786436
  167.7 17.3 %copy-start = (f32[8,128,256]{2,1,0:T(8,128)}, f32[8,128,256]{2,1,0:T(8,128)S(1)}, u32[]{:S(2)}) copy-start(f32[8,128,256]{2,1,0:T(8,128)S(1)} %reduce_sum.36) | copy-start | bytes 3145732
  170.8 50.4 %all-to-all-start.5 = ((f32[32,2,8,128]{3,2,1,0:T(8,128)}), f32[32,2,8,128]{3,2,1,0:T(8,128)}, u32[]{:S(2)}, u32[]{:S(2)}) async-start(f32[32,2,8,128]{3,2,1,0:T(8,128)} %copy.143), calls=%async_computation.6 | async-start | bytes 524288 | tf_op jit(solution)/shard_map/all_to_all | solution.py:144
  184.9 72.4 %reduce-scatter.2.cloned.1.call-start = ((), (), s32[]{:S(2)}) async-start(), calls=%async_computation.10 | async-start | bytes 1179648 | tf_op jit(solution)/shard_map/reduce_scatter | solution.py:132
  187.4 32.6 %collective-permute-start.4 = (f32[256,128]{1,0:T(8,128)S(1)}, f32[256,128]{1,0:T(8,128)S(1)}, u32[]{:S(2)}, u32[]{:S(2)}) collective-permute-start(f32[256,128]{1,0:T(8,128)S(1)} %bitcast.143), channel_id=1, source_target_pairs={{0,256},{256,0},{1,257},{257,1},{2,258},{258,2},{3,259},{259,3},{4... | collective-permute-start | bytes 393224 | tf_op jit(solution)/shard_map/ppermute | solution.py:74
  220.0 1.3 copy-start.20
  221.2 6.8 %copy-start.25 = (f32[66,32,1]{0,1,2:T(8,128)S(1)}, f32[66,32,1]{0,1,2:T(8,128)}, u32[]{:S(2)}) copy-start(f32[66,32,1]{0,1,2:T(8,128)} %constant.87) | copy-start | bytes 25348
  221.2 8.0 %copy-start.17 = (f32[33,128]{1,0:T(8,128)S(1)}, f32[33,128]{1,0:T(8,128)}, u32[]{:S(2)}) copy-start(f32[33,128]{1,0:T(8,128)} %constant.74.clone) | copy-start | bytes 50692
  221.2 8.0 %copy-start.19 = (f32[33,128]{1,0:T(8,128)S(1)}, f32[33,128]{1,0:T(8,128)}, u32[]{:S(2)}) copy-start(f32[33,128]{1,0:T(8,128)} %constant.73.clone) | copy-start | bytes 50692
  221.2 34.7 %all-to-all-start.6 = ((f32[16,256,128]{2,1,0:T(8,128)}), f32[16,256,128]{2,1,0:T(8,128)S(1)}, u32[]{:S(2)}, u32[]{:S(2)}) async-start(f32[16,256,128]{2,1,0:T(8,128)} %convolution_bitcast_fusion), calls=%async_computation.7 | async-start | bytes 4194304 | tf_op jit(solution)/shard_map/all_to_all | solution.py:157
  227.0 2.3 copy-start.10
  229.2 1.7 copy-start.8
  231.9 27.3 %copy-start.12 = (f32[32,16,128]{2,0,1:T(8,128)S(1)}, f32[32,16,128]{2,0,1:T(8,128)}, u32[]{:S(2)}) copy-start(f32[32,16,128]{2,0,1:T(8,128)} %copy-done.11) | copy-start | bytes 786436
  231.9 27.3 %copy-start.14 = (f32[2,16,8,128]{3,1,0,2:T(8,128)S(1)}, f32[2,16,8,128]{3,1,0,2:T(8,128)}, u32[]{:S(2)}) copy-start(f32[2,16,8,128]{3,1,0,2:T(8,128)} %copy.151) | copy-start | bytes 393220
  231.9 27.3 %copy-start.28 = (f32[8]{0:T(128)S(1)}, f32[8]{0:T(128)}, u32[]{:S(2)}) copy-start(f32[8]{0:T(128)} %copy-done.27) | copy-start | bytes 100
  256.0 14.7 %copy-start.13 = (f32[256,1,128]{0,2,1:T(8,128)S(1)}, f32[256,1,128]{0,2,1:T(8,128)}, u32[]{:S(2)}) copy-start(f32[256,1,128]{0,2,1:T(8,128)} %get-tuple-element.64) | copy-start | bytes 393220
  256.1 14.8 %copy-start.3 = (f32[32,2,8,128]{3,2,1,0:T(8,128)S(1)}, f32[32,2,8,128]{3,2,1,0:T(8,128)}, u32[]{:S(2)}) copy-start(f32[32,2,8,128]{3,2,1,0:T(8,128)} %copy-done.2) | copy-start | bytes 786436
  256.1 15.6 %copy-start.21 = (f32[256,128]{1,0:T(8,128)S(1)}, f32[256,128]{1,0:T(8,128)}, u32[]{:S(2)}) copy-start(f32[256,128]{1,0:T(8,128)} %copy-done.20) | copy-start | bytes 393220
  256.1 16.3 %copy-start.23 = (f32[256,128]{1,0:T(8,128)}, f32[256,128]{1,0:T(8,128)S(1)}, u32[]{:S(2)}) copy-start(f32[256,128]{1,0:T(8,128)S(1)} %broadcast_multiply_fusion) | copy-start | bytes 393220
  257.3 13.6 %copy-start.30 = (f32[1,128,256]{2,1,0:T(8,128)S(1)}, f32[1,128,256]{2,1,0:T(8,128)}, u32[]{:S(2)}) copy-start(f32[1,128,256]{2,1,0:T(8,128)} %reduce-scatter.2.cloned.1.call-done) | copy-start | bytes 393220
  259.3 41.8 %copy-start.5 = (f32[128,256]{0,1:T(8,128)S(1)}, f32[128,256]{0,1:T(8,128)}, u32[]{:S(2)}) copy-start(f32[128,256]{0,1:T(8,128)} %copy-done.4) | copy-start | bytes 393220
  260.4 40.6 %all-to-all-start.7 = ((f32[32,17,128]{2,1,0:T(8,128)}), f32[32,17,128]{2,1,0:T(8,128)S(1)}, u32[]{:S(2)}, u32[]{:S(2)}) async-start(f32[32,17,128]{2,1,0:T(8,128)} %copy.155), calls=%async_computation.8 | async-start | bytes 786432 | tf_op jit(solution)/shard_map/all_to_all | solution.py:171
  270.9 1.5 collective-permute-start.3
Sparse Core Ops, SparseCore 0:
  76.5 58.9 all-gather.1
  188.6 65.8 reduce-scatter.1

commit v4 on v3

--- a/solution.py
+++ b/solution.py
@@ -86,26 +86,24 @@
     norm_scale = 1.0 / math.sqrt(seq_len)
     tab = tables(seq_len)
     at_h = lax.axis_index("h")
-    at_m = lax.axis_index("m")
     at_ctx = lax.axis_index(CTX)
 
-    weights = lax.all_gather(out_weight, PLANE, axis=1, tiled=True)
+    cot_mine = across(cotangent, lambda h, m: (m, h))
+    cot_line = lax.all_gather(cot_mine, LINE, axis=0)
 
-    cot_same = across(cotangent, lambda h, m: (m, h))
-    cot_swap = across(cotangent, lambda h, m: (m, 1 - h))
-    cot_pair = jnp.where(at_m == 0, jnp.stack([cot_same, cot_swap]), jnp.stack([cot_swap, cot_same]))
+    query_own = query_branch.T
+    query_far = other_h(query_own)
+    query_both = jnp.where(at_h == 0, jnp.stack([query_own, query_far]), jnp.stack([query_far, query_own]))
+
+    weights = lax.all_to_all(jnp.broadcast_to(out_weight[None], (16,) + out_weight.shape), PLANE, 0, 0)
 
     product = key_branch * value_branch
     sent = jnp.concatenate(
         [product.T.reshape(n_ctx, group, rows), (long_filter * norm_scale).T.reshape(n_ctx, group, rows)], 1
     )
+    sent = tie(tie(tie(sent, weights), query_far), cot_mine)
     signals = lax.all_to_all(sent, CTX, 0, 0)
-    query_own = query_branch.T
-    query_far = other_h(query_own)
-    query_both = jnp.where(at_h == 0, jnp.stack([query_own, query_far]), jnp.stack([query_far, query_own]))
-
-    cot_pair = tie(cot_pair, signals)
-    cot_line = lax.all_to_all(jnp.broadcast_to(cot_pair[None], (4,) + cot_pair.shape), "l", 0, 0)
+    weights = weights.transpose(1, 0, 2).reshape(chans, -1)
 
     spectra = forward_fourier(signals, tab)
     prod_real, prod_imag = halves(spectra[:, :group])
@@ -116,7 +114,6 @@
     skip = lax.dynamic_slice(skip_weight, (at_ctx * group,), (group,))[None, :, None]
     chan_product = signals[:, :group]
     gate_chan = conv + skip * chan_product
-    gate_chan = tie(gate_chan, cot_line)
     gate_pair = gate_chan.reshape(2, 16, group, rows).transpose(1, 0, 2, 3)
     gate_sent = jnp.broadcast_to(gate_pair[None], (2,) + gate_pair.shape).reshape(n_ctx, 2, group, rows)
     gate_got = lax.all_to_all(gate_sent, CTX, 0, 0)
@@ -130,24 +127,24 @@
     partial = partial.reshape(2, rows, 4, 2, chans).transpose(3, 0, 2, 1, 4).reshape(2, 8, rows, chans)
     partial = lax.all_to_all(partial, "k", 0, 0).sum(0)
     projected = lax.psum_scatter(partial, LINE, scatter_dimension=0, tiled=False)
-    cot_line = tie(cot_line, gate_got)
+    cot_line = tie(cot_line, partial)
     cot_cores = lax.all_to_all(jnp.broadcast_to(cot_line[None], (2,) + cot_line.shape), "k", 0, 0)
     cot_full = (
-        cot_cores.transpose(2, 3, 1, 0, 4).reshape(2 * rows, 8 * chans)
+        cot_cores.reshape(2, 2, 4, rows, chans).transpose(1, 3, 2, 0, 4).reshape(2 * rows, 8 * chans)
     )
 
     mixed_grad = lax.dot_general(
         weights, cot_full, (((1,), (1,)), ((), ())), precision=close, preferred_element_type=jnp.float32
     )
     mixed_grad = mixed_grad.reshape(chans, 2, rows).transpose(1, 0, 2)
-    grad_sent = tie(mixed_grad * query_both, partial).reshape(2, n_ctx, group, rows).transpose(1, 0, 2, 3)
+    grad_sent = (mixed_grad * query_both).reshape(2, n_ctx, group, rows).transpose(1, 0, 2, 3)
     grad_got = lax.all_to_all(grad_sent, CTX, 0, 0)
     grad_chan = grad_got.reshape(2, 16, 2, group, rows).sum(0).transpose(1, 0, 2, 3).reshape(n_ctx, group, rows)
 
     own_grad = lax.dynamic_index_in_dim(mixed_grad, at_h, 0, False)
     far_grad = lax.dynamic_index_in_dim(mixed_grad, 1 - at_h, 0, False)
     own_gate = lax.dynamic_index_in_dim(gate_both, at_h, 0, False)
-    far_grad = other_h(far_grad)
+    far_grad = other_h(tie(far_grad, grad_got))
     query_grad = ((own_grad + far_grad) * own_gate).T
 
     weight_part = lax.dot_general(

time: 313 us -> 307 us (0.981)
  waiting for transfers between devices: 131 us -> 150 us
  starting transfers between devices: 94.8 us -> 76.4 us
  local copies, waits for them, and re-layouts: 32.1 us -> 27.3 us
    all_to_all x1, waiting for transfers between devices: 0.01 us -> 24.1 us  [local(): gate_got = lax.all_to_all(gate_sent, CTX, 0, 0)]
    reduce_scatter x1, waiting for transfers between devices: 0.02 us -> 18.4 us  [local(): lax.psum_scatter(partial, LINE, scatter_dimension=0, tiled=False)]
    all_gather x1, waiting for transfers between devices: 18 us -> 2.29 us  [local(): cot_line = lax.all_gather(cot_mine, LINE, axis=0)]
    all_to_all x1, waiting for transfers between devices: 15.4 us -> 0.01 us  [local(): lax.all_to_all(jnp.broadcast_to(out_weight[None], (16,) + out_weight.shap...]
    all_to_all x1, waiting for transfers between devices: 23.5 us -> 8.54 us  [local(): weight_grad = lax.all_to_all(weight_part, PLANE, 0, 0).sum(0) * norm_scale]
    ppermute x2, waiting for transfers between devices: 13.4 us -> 27.6 us  [other_h(): return lax.ppermute(block, 'h', [(0, 1), (1, 0)])]
    all_to_all x1, waiting for transfers between devices: 0.01 us -> 13.6 us  [local(): grad_got = lax.all_to_all(grad_sent, CTX, 0, 0)]
    ppermute x2, starting transfers between devices: 24.9 us -> 17.2 us  [other_h(): return lax.ppermute(block, 'h', [(0, 1), (1, 0)])]
  transfers between devices with their start and end apart: 13 -> 12, of which waited for: 7 -> 9; matrix products, arithmetic and copies ran while one was open for 8% -> 8% of each run, Pallas kernels for 0% -> 0%
where the time goes in v4:
time: 307 us; the launch traced here: 306 us
  waiting for transfers between devices  150 us (49%)
  starting transfers between devices  76.4 us (25%)
  local copies, waits for them, and re-layouts  27.3 us (9%)
  between operations  20.2 us (7%)
  matrix products  13.8 us (4%)
  blocking collectives  11.7 us (4%)
  other arithmetic  6.73 us (2%)
    all_to_all x1, waiting for transfers between devices, local(): back = lax.all_to_all(back_sent, CTX, 0, 0)  29.2 us
    ppermute x2, waiting for transfers between devices, other_h(): return lax.ppermute(block, 'h', [(0, 1), (1, 0)])  27.6 us
    all_to_all x1, waiting for transfers between devices, local(): signals = lax.all_to_all(sent, CTX, 0, 0)  24.9 us
    all_to_all x1, waiting for transfers between devices, local(): gate_got = lax.all_to_all(gate_sent, CTX, 0, 0)  24.1 us
    reduce_scatter x1, waiting for transfers between devices, local(): lax.psum_scatter(partial, LINE, scatter_dimension=0, tiled=False)  18.4 us
    ppermute x2, starting transfers between devices, other_h(): return lax.ppermute(block, 'h', [(0, 1), (1, 0)])  17.2 us
    all_to_all x1, starting transfers between devices, local(): signals = lax.all_to_all(sent, CTX, 0, 0)  15 us
    all_to_all x1, starting transfers between devices, local(): grad_got = lax.all_to_all(grad_sent, CTX, 0, 0)  14 us
  transfers between devices with their start and end apart: 12, of which 9 were waited for; matrix products, arithmetic and copies ran while one was open for 8% of the time, Pallas kernels for 0%

profile of v4, /device:TPU:32, one launch (start us, length us, event | category | flops | bytes accessed | tf_op | source)
XLA Modules:
  0.0 305.9 jit_solution(6682273916929241052)
XLA Ops:
  7.2 2.4 broadcast_in_dim.8
  9.6 7.2 %all-to-all-start = ((f32[16,256,128]{2,1,0:T(8,128)}), f32[16,256,128]{2,1,0:T(8,128)S(1)}, u32[]{:S(2)}, u32[]{:S(2)}) async-start(f32[16,256,128]{2,1,0:T(8,128)} %broadcast_in_dim.8), calls=%async_computation | async-start | bytes 4194304 | tf_op jit(solution)/shard_map/all_to_all | solution.py:98
  17.0 14.8 %collective-permute-start = (f32[256,128]{1,0:T(8,128)S(1)}, f32[256,128]{1,0:T(8,128)S(1)}, u32[]{:S(2)}, u32[]{:S(2)}) collective-permute-start(f32[256,128]{1,0:T(8,128)S(1)} %bitcast.143), channel_id=1, source_target_pairs={{0,256},{256,0},{1,257},{257,1},{2,258},{258,2},{3,259},{259,3},{4... | collective-permute-start | bytes 393224 | tf_op jit(solution)/shard_map/ppermute | solution.py:74
  31.8 0.7 collective-permute-start.1
  34.1 16.1 %collective-permute-done = f32[256,128]{1,0:T(8,128)S(1)} collective-permute-done((f32[256,128]{1,0:T(8,128)S(1)}, f32[256,128]{1,0:T(8,128)S(1)}, u32[]{:S(2)}, u32[]{:S(2)}) %collective-permute-start) | collective-permute-done | bytes 131104 | tf_op jit(solution)/shard_map/ppermute | solution.py:74
  52.7 0.7 fusion.24
  53.4 15.0 %all-to-all-start.1 = ((f32[32,16,128]{2,1,0:T(8,128)}), f32[32,16,128]{2,1,0:T(8,128)S(1)}, u32[]{:S(2)}, u32[]{:S(2)}) async-start(f32[32,16,128]{2,1,0:T(8,128)} %fusion.24), calls=%async_computation.1 | async-start | bytes 524288 | tf_op jit(solution)/shard_map/all_to_all | solution.py:105
  69.2 24.9 %all-to-all-done.1 = f32[32,16,128]{2,1,0:T(8,128)S(1)} async-done(((f32[32,16,128]{2,1,0:T(8,128)}), f32[32,16,128]{2,1,0:T(8,128)S(1)}, u32[]{:S(2)}, u32[]{:S(2)}) %all-to-all-start.1) | async-done | bytes 262176 | tf_op jit(solution)/shard_map/all_to_all | solution.py:105
  94.1 0.7 fusion.40
  95.0 0.7 fusion.6
  95.7 0.8 fusion.42
  97.6 0.7 broadcast_in_dim.9
  98.3 4.0 %all-to-all-start.2 = ((f32[32,2,8,128]{3,2,1,0:T(8,128)}), f32[32,2,8,128]{3,2,1,0:T(8,128)S(1)}, u32[]{:S(2)}, u32[]{:S(2)}) async-start(f32[32,2,8,128]{3,2,1,0:T(8,128)} %bitcast.17), calls=%async_computation.2 | async-start | bytes 524288 | tf_op jit(solution)/shard_map/all_to_all | solution.py:119
  102.3 2.0 copy.134
  104.3 24.1 %all-to-all-done.2 = f32[32,2,8,128]{3,2,1,0:T(8,128)S(1)} async-done(((f32[32,2,8,128]{3,2,1,0:T(8,128)}), f32[32,2,8,128]{3,2,1,0:T(8,128)S(1)}, u32[]{:S(2)}, u32[]{:S(2)}) %all-to-all-start.2) | async-done | bytes 262176 | tf_op jit(solution)/shard_map/all_to_all | solution.py:119
  128.6 1.1 fusion.25
  129.9 6.3 %all_to_all.40 = f32[2,8,128,256]{3,2,1,0:T(8,128)} all-to-all(f32[2,8,128,256]{3,2,1,0:T(8,128)S(1)} %copy.135), channel_id=1, replica_groups=mesh['h'=2,'y'=4,'x'=4,'m'=2,'l'=4,'k'=2] {'k'}, dimensions={0} | all-to-all | bytes 4194304 | tf_op jit(solution)/shard_map/all_to_all | solution.py:128
  136.2 1.9 reduce_sum.36
  139.3 2.3 all-gather.3.cloned.1.call-done
  141.6 1.3 broadcast_add_fusion
  143.1 5.4 %all_to_all.41 = f32[2,8,128,256]{3,2,1,0:T(8,128)S(1)} all-to-all(f32[2,8,128,256]{3,2,1,0:T(8,128)S(1)} %broadcast_in_dim.10), channel_id=1, replica_groups=mesh['h'=2,'y'=4,'x'=4,'m'=2,'l'=4,'k'=2] {'k'}, dimensions={0} | all-to-all | bytes 4194304 | tf_op jit(solution)/shard_map/all_to_all | solution.py:131
  148.6 3.0 copy.136
  151.5 3.9 %reshape.107 = f32[256,2048]{1,0:T(8,128)} reshape(f32[2,128,4,2,256]{4,3,2,1,0:T(2,128)} %copy.136) | data formatting | bytes 4194304 | tf_op jit(solution)/shard_map/reshape | solution.py:133
  155.4 2.7 fusion.45
  158.3 0.7 copy.138
  159.0 14.0 %all-to-all-start.5 = ((f32[32,2,8,128]{3,2,1,0:T(8,128)}), f32[32,2,8,128]{3,2,1,0:T(8,128)S(1)}, u32[]{:S(2)}, u32[]{:S(2)}) async-start(f32[32,2,8,128]{3,2,1,0:T(8,128)} %copy.138), calls=%async_computation.6 | async-start | bytes 524288 | tf_op jit(solution)/shard_map/all_to_all | solution.py:141
  173.8 1.8 copy.147
  175.6 4.8 %convolution_bitcast_fusion = f32[16,256,128]{2,1,0:T(8,128)} fusion(f32[256,256,1]{0,1,2:T(8,128)S(1)} %bitcast.138, f32[16,128,256]{2,1,0:T(8,128)} %bitcast.134), kind=kOutput, calls=%fused_computation | convolution fusion | flops 805306368 | bytes 4456448 | tf_op jit(solution)/shard_map/dot_general | solution.py:150
  180.4 13.6 %all-to-all-done.5 = f32[32,2,8,128]{3,2,1,0:T(8,128)S(1)} async-done(((f32[32,2,8,128]{3,2,1,0:T(8,128)}), f32[32,2,8,128]{3,2,1,0:T(8,128)S(1)}, u32[]{:S(2)}, u32[]{:S(2)}) %all-to-all-start.5) | async-done | bytes 262176 | tf_op jit(solution)/shard_map/all_to_all | solution.py:141
  194.0 3.7 %all-to-all-start.6 = ((f32[16,256,128]{2,1,0:T(8,128)}), f32[16,256,128]{2,1,0:T(8,128)S(1)}, u32[]{:S(2)}, u32[]{:S(2)}) async-start(f32[16,256,128]{2,1,0:T(8,128)} %convolution_bitcast_fusion), calls=%async_computation.7 | async-start | bytes 4194304 | tf_op jit(solution)/shard_map/all_to_all | solution.py:154
  197.7 0.7 copy.146
  199.6 2.4 collective-permute-start.3
  202.6 1.3 fusion.13
  204.0 1.2 fusion.19
  205.2 0.9 fusion
  206.7 11.5 %collective-permute-done.3 = f32[256,128]{1,0:T(8,128)S(1)} collective-permute-done((f32[256,128]{1,0:T(8,128)S(1)}, f32[256,128]{1,0:T(8,128)S(1)}, u32[]{:S(2)}, u32[]{:S(2)}) %collective-permute-start.3) | collective-permute-done | bytes 131104 | tf_op jit(solution)/shard_map/ppermute | solution.py:74
  219.5 8.5 %all-to-all-done.6 = f32[16,256,128]{2,1,0:T(8,128)S(1)} async-done(((f32[16,256,128]{2,1,0:T(8,128)}), f32[16,256,128]{2,1,0:T(8,128)S(1)}, u32[]{:S(2)}, u32[]{:S(2)}) %all-to-all-start.6) | async-done | bytes 2097184 | tf_op jit(solution)/shard_map/all_to_all | solution.py:154
  229.3 18.4 %reduce-scatter.2.cloned.1.call-done = f32[1,128,256]{2,1,0:T(8,128)} async-done(((f32[8,128,256]{2,1,0:T(8,128)}), f32[1,128,256]{2,1,0:T(8,128)}) %reduce-scatter.2.cloned.1.call-update) | async-done | bytes 131088 | tf_op jit(solution)/shard_map/reduce_scatter | solution.py:129
  247.7 1.3 slice.139
  249.9 0.9 copy.150
  250.8 13.8 %all-to-all-start.7 = ((f32[32,17,128]{2,1,0:T(8,128)}), f32[32,17,128]{2,1,0:T(8,128)S(1)}, u32[]{:S(2)}, u32[]{:S(2)}) async-start(f32[32,17,128]{2,1,0:T(8,128)} %copy.150), calls=%async_computation.8 | async-start | bytes 786432 | tf_op jit(solution)/shard_map/all_to_all | solution.py:168
  264.7 0.7 collective-permute-start.2
  265.5 0.8 copy.156
  266.2 29.2 %all-to-all-done.7 = f32[32,17,128]{2,1,0:T(8,128)S(1)} async-done(((f32[32,17,128]{2,1,0:T(8,128)}), f32[32,17,128]{2,1,0:T(8,128)S(1)}, u32[]{:S(2)}, u32[]{:S(2)}) %all-to-all-start.7) | async-done | bytes 278560 | tf_op jit(solution)/shard_map/all_to_all | solution.py:168
  295.4 0.8 copy.154
  296.2 0.8 copy.155
  297.0 0.8 copy.157
  298.4 0.7 copy.186
  (134 shorter events, 10.0 us)
Async XLA Ops:
  9.6 7.2 %copy-start.24 = (f32[128,256]{1,0:T(8,128)S(1)}, f32[128,256]{1,0:T(8,128)}, u32[]{:S(2)}) copy-start(f32[128,256]{1,0:T(8,128)} %param.15) | copy-start | bytes 393220
  9.6 22.2 %copy-start.35 = (f32[128,256]{1,0:T(8,128)S(1)}, f32[128,256]{1,0:T(8,128)}, u32[]{:S(2)}) copy-start(f32[128,256]{1,0:T(8,128)} %param.19) | copy-start | bytes 393220
  9.6 22.9 %copy-start.25 = (f32[128,256]{1,0:T(8,128)S(1)}, f32[128,256]{1,0:T(8,128)}, u32[]{:S(2)}) copy-start(f32[128,256]{1,0:T(8,128)} %param.16) | copy-start | bytes 393220
  9.6 23.0 %copy-start.26 = (f32[128,256]{1,0:T(8,128)S(1)}, f32[128,256]{1,0:T(8,128)}, u32[]{:S(2)}) copy-start(f32[128,256]{1,0:T(8,128)} %param.13) | copy-start | bytes 393220
  9.6 23.1 %copy-start.27 = (f32[128,256]{1,0:T(8,128)S(1)}, f32[128,256]{1,0:T(8,128)}, u32[]{:S(2)}) copy-start(f32[128,256]{1,0:T(8,128)} %param.14) | copy-start | bytes 393220
  9.6 41.8 %all-to-all-start = ((f32[16,256,128]{2,1,0:T(8,128)}), f32[16,256,128]{2,1,0:T(8,128)S(1)}, u32[]{:S(2)}, u32[]{:S(2)}) async-start(f32[16,256,128]{2,1,0:T(8,128)} %broadcast_in_dim.8), calls=%async_computation | async-start | bytes 4194304 | tf_op jit(solution)/shard_map/all_to_all | solution.py:98
  16.8 51.7 %copy-start.37 = (f32[256]{0:T(256)S(1)}, f32[256]{0:T(256)}, u32[]{:S(2)}) copy-start(f32[256]{0:T(256)} %param.17) | copy-start | bytes 3076
  16.8 77.3 %copy-start.32 = (f32[66,32,1]{0,1,2:T(8,128)S(1)}, f32[66,32,1]{0,1,2:T(8,128)}, u32[]{:S(2)}) copy-start(f32[66,32,1]{0,1,2:T(8,128)} %constant.82) | copy-start | bytes 25348
  16.8 78.0 %copy-start.18 = (f32[33,128]{1,0:T(8,128)S(1)}, f32[33,128]{1,0:T(8,128)}, u32[]{:S(2)}) copy-start(f32[33,128]{1,0:T(8,128)} %constant.72.clone) | copy-start | bytes 50692
  16.9 78.0 %copy-start.20 = (f32[33,128]{1,0:T(8,128)S(1)}, f32[33,128]{1,0:T(8,128)}, u32[]{:S(2)}) copy-start(f32[33,128]{1,0:T(8,128)} %constant.71.clone) | copy-start | bytes 50692
  17.0 111.5 %copy-start.7 = (f32[128,256]{0,1:T(8,128)}, f32[128,256]{0,1:T(8,128)S(1)}, u32[]{:S(2)}) copy-start(f32[128,256]{0,1:T(8,128)S(1)} %copy.123) | copy-start | bytes 393220
  17.0 33.2 %collective-permute-start = (f32[256,128]{1,0:T(8,128)S(1)}, f32[256,128]{1,0:T(8,128)S(1)}, u32[]{:S(2)}, u32[]{:S(2)}) collective-permute-start(f32[256,128]{1,0:T(8,128)S(1)} %bitcast.143), channel_id=1, source_target_pairs={{0,256},{256,0},{1,257},{257,1},{2,258},{258,2},{3,259},{259,3},{4... | collective-permute-start | bytes 393224 | tf_op jit(solution)/shard_map/ppermute | solution.py:74
  31.8 1.0 collective-permute-start.1
  32.8 20.6 %copy-start.5 = (f32[128,256]{0,1:T(8,128)}, f32[128,256]{0,1:T(8,128)S(1)}, u32[]{:S(2)}) copy-start(f32[128,256]{0,1:T(8,128)S(1)} %copy.125) | copy-start | bytes 393220
  32.9 35.7 %copy-start.28 = (f32[128,256]{1,0:T(8,128)}, f32[128,256]{1,0:T(8,128)S(1)}, u32[]{:S(2)}) copy-start(f32[128,256]{1,0:T(8,128)S(1)} %collective-permute-done.1) | copy-start | bytes 393220
  50.2 44.6 %copy-start.15 = (f32[256,128]{1,0:T(8,128)}, f32[256,128]{1,0:T(8,128)S(1)}, u32[]{:S(2)}) copy-start(f32[256,128]{1,0:T(8,128)S(1)} %collective-permute-done) | copy-start | bytes 393220
  51.4 43.6 %copy-start.1 = (f32[16,256,128]{2,1,0:T(8,128)}, f32[16,256,128]{2,1,0:T(8,128)S(1)}, u32[]{:S(2)}) copy-start(f32[16,256,128]{2,1,0:T(8,128)S(1)} %all-to-all-done) | copy-start | bytes 6291460
  53.4 41.6 %copy-start.11 = (f32[256,256,1]{1,0,2:T(8,128)S(1)}, f32[256,256,1]{1,0,2:T(8,128)}, u32[]{:S(2)}) copy-start(f32[256,256,1]{1,0,2:T(8,128)} %constant.83) | copy-start | bytes 786436
  53.4 40.7 %all-to-all-start.1 = ((f32[32,16,128]{2,1,0:T(8,128)}), f32[32,16,128]{2,1,0:T(8,128)S(1)}, u32[]{:S(2)}, u32[]{:S(2)}) async-start(f32[32,16,128]{2,1,0:T(8,128)} %fusion.24), calls=%async_computation.1 | async-start | bytes 524288 | tf_op jit(solution)/shard_map/all_to_all | solution.py:105
  68.4 73.2 %all-gather.3.cloned.1.call-start = ((), (), s32[]{:S(2)}) async-start(), calls=%async_computation.10 | async-start | bytes 1179648 | tf_op jit(solution)/shard_map/all_gather | solution.py:92
  68.6 28.6 %copy-start.33 = (f32[8]{0:T(128)}, f32[8]{0:T(128)S(1)}, u32[]{:S(2)}) copy-start(f32[8]{0:T(128)S(1)} %dynamic_slice.9) | copy-start | bytes 100
  94.9 1.6 copy-start.9
  95.7 1.4 copy-start.30
  97.2 7.2 %copy-start.12 = (f32[32,16,128]{2,0,1:T(8,128)}, f32[32,16,128]{2,0,1:T(8,128)S(1)}, u32[]{:S(2)}) copy-start(f32[32,16,128]{2,0,1:T(8,128)S(1)} %copy.127) | copy-start | bytes 786436
  98.3 30.1 %all-to-all-start.2 = ((f32[32,2,8,128]{3,2,1,0:T(8,128)}), f32[32,2,8,128]{3,2,1,0:T(8,128)S(1)}, u32[]{:S(2)}, u32[]{:S(2)}) async-start(f32[32,2,8,128]{3,2,1,0:T(8,128)} %bitcast.17), calls=%async_computation.2 | async-start | bytes 524288 | tf_op jit(solution)/shard_map/all_to_all | solution.py:119
  102.3 26.1 %copy-start.16 = (f32[256,128]{1,0:T(8,128)S(1)}, f32[256,128]{1,0:T(8,128)}, u32[]{:S(2)}) copy-start(f32[256,128]{1,0:T(8,128)} %copy-done.15) | copy-start | bytes 393220
  138.1 5.0 %copy-start.2 = (f32[8,128,256]{2,1,0:T(8,128)}, f32[8,128,256]{2,1,0:T(8,128)S(1)}, u32[]{:S(2)}) copy-start(f32[8,128,256]{2,1,0:T(8,128)S(1)} %reduce_sum.36) | copy-start | bytes 3145732
  155.4 2.8 copy-start.8
  155.4 2.9 copy-start.17
  158.1 15.7 %copy-start = (f32[256,2048]{1,0:T(8,128)S(1)}, f32[256,2048]{1,0:T(8,128)}, u32[]{:S(2)}) copy-start(f32[256,2048]{1,0:T(8,128)} %reshape.107) | copy-start | bytes 6291460
  159.0 34.9 %all-to-all-start.5 = ((f32[32,2,8,128]{3,2,1,0:T(8,128)}), f32[32,2,8,128]{3,2,1,0:T(8,128)S(1)}, u32[]{:S(2)}, u32[]{:S(2)}) async-start(f32[32,2,8,128]{3,2,1,0:T(8,128)} %copy.138), calls=%async_computation.6 | async-start | bytes 524288 | tf_op jit(solution)/shard_map/all_to_all | solution.py:141
  173.0 74.7 %reduce-scatter.2.cloned.1.call-start = ((), (), s32[]{:S(2)}) async-start(), calls=%async_computation.9 | async-start | bytes 1179648 | tf_op jit(solution)/shard_map/reduce_scatter | solution.py:129
  180.4 21.6 %copy-start.31 = (f32[66,32,1]{0,1,2:T(8,128)S(1)}, f32[66,32,1]{0,1,2:T(8,128)}, u32[]{:S(2)}) copy-start(f32[66,32,1]{0,1,2:T(8,128)} %constant.85) | copy-start | bytes 25348
  180.4 22.1 %copy-start.19 = (f32[33,128]{1,0:T(8,128)S(1)}, f32[33,128]{1,0:T(8,128)}, u32[]{:S(2)}) copy-start(f32[33,128]{1,0:T(8,128)} %constant.72.clone) | copy-start | bytes 50692
  180.4 22.1 %copy-start.21 = (f32[33,128]{1,0:T(8,128)S(1)}, f32[33,128]{1,0:T(8,128)}, u32[]{:S(2)}) copy-start(f32[33,128]{1,0:T(8,128)} %constant.71.clone) | copy-start | bytes 50692
  194.0 34.0 %all-to-all-start.6 = ((f32[16,256,128]{2,1,0:T(8,128)}), f32[16,256,128]{2,1,0:T(8,128)S(1)}, u32[]{:S(2)}, u32[]{:S(2)}) async-start(f32[16,256,128]{2,1,0:T(8,128)} %convolution_bitcast_fusion), calls=%async_computation.7 | async-start | bytes 4194304 | tf_op jit(solution)/shard_map/all_to_all | solution.py:154
  199.6 18.5 %collective-permute-start.3 = (f32[256,128]{1,0:T(8,128)S(1)}, f32[256,128]{1,0:T(8,128)S(1)}, u32[]{:S(2)}, u32[]{:S(2)}) collective-permute-start(f32[256,128]{1,0:T(8,128)S(1)} %add_bitcast_fusion), channel_id=1, source_target_pairs={{0,256},{256,0},{1,257},{257,1},{2,258},{258,2},{3,259},{259,3},{4... | collective-permute-start | bytes 393224 | tf_op jit(solution)/shard_map/ppermute | solution.py:74
  202.5 2.7 copy-start.10
  206.1 43.5 %copy-start.13 = (f32[32,16,128]{2,0,1:T(8,128)S(1)}, f32[32,16,128]{2,0,1:T(8,128)}, u32[]{:S(2)}) copy-start(f32[32,16,128]{2,0,1:T(8,128)} %copy-done.12) | copy-start | bytes 786436
  206.1 43.5 %copy-start.14 = (f32[2,16,8,128]{3,1,0,2:T(8,128)S(1)}, f32[2,16,8,128]{3,1,0,2:T(8,128)}, u32[]{:S(2)}) copy-start(f32[2,16,8,128]{3,1,0,2:T(8,128)} %copy.146) | copy-start | bytes 393220
  206.2 43.5 %copy-start.34 = (f32[8]{0:T(128)S(1)}, f32[8]{0:T(128)}, u32[]{:S(2)}) copy-start(f32[8]{0:T(128)} %copy-done.33) | copy-start | bytes 100
  228.1 36.6 %copy-start.4 = (f32[32,2,8,128]{3,2,1,0:T(8,128)S(1)}, f32[32,2,8,128]{3,2,1,0:T(8,128)}, u32[]{:S(2)}) copy-start(f32[32,2,8,128]{3,2,1,0:T(8,128)} %copy-done.3) | copy-start | bytes 786436
  228.1 37.3 %copy-start.23 = (f32[256,128]{1,0:T(8,128)S(1)}, f32[256,128]{1,0:T(8,128)}, u32[]{:S(2)}) copy-start(f32[256,128]{1,0:T(8,128)} %copy-done.22) | copy-start | bytes 393220
  228.2 37.3 %copy-start.29 = (f32[256,128]{1,0:T(8,128)}, f32[256,128]{1,0:T(8,128)S(1)}, u32[]{:S(2)}) copy-start(f32[256,128]{1,0:T(8,128)S(1)} %broadcast_multiply_fusion) | copy-start | bytes 393220
  247.7 17.0 %copy-start.36 = (f32[1,128,256]{2,1,0:T(8,128)S(1)}, f32[1,128,256]{2,1,0:T(8,128)}, u32[]{:S(2)}) copy-start(f32[1,128,256]{2,1,0:T(8,128)} %reduce-scatter.2.cloned.1.call-done) | copy-start | bytes 393220
  249.8 45.6 %copy-start.6 = (f32[128,256]{0,1:T(8,128)S(1)}, f32[128,256]{0,1:T(8,128)}, u32[]{:S(2)}) copy-start(f32[128,256]{0,1:T(8,128)} %copy-done.5) | copy-start | bytes 393220
  250.8 44.6 %all-to-all-start.7 = ((f32[32,17,128]{2,1,0:T(8,128)}), f32[32,17,128]{2,1,0:T(8,128)S(1)}, u32[]{:S(2)}, u32[]{:S(2)}) async-start(f32[32,17,128]{2,1,0:T(8,128)} %copy.150), calls=%async_computation.8 | async-start | bytes 786432 | tf_op jit(solution)/shard_map/all_to_all | solution.py:168
  264.7 1.5 collective-permute-start.2
  (2 other events, 1.9 us)
Sparse Core Ops, SparseCore 0:
  71.9 69.6 all-gather.2
  176.7 70.9 reduce-scatter.1

commit v5 on v2

--- a/solution.py
+++ b/solution.py
@@ -74,8 +74,28 @@
     return lax.ppermute(block, "h", [(0, 1), (1, 0)])
 
 
-def tie(value, first):
-    return value + 0.0 * first[(0,) * first.ndim]
+def other_core(block):
+    return lax.ppermute(block, "k", [(0, 1), (1, 0)])
+
+
+def in_order(own, other, at):
+    return jnp.where(at == 0, jnp.stack([own, other]), jnp.stack([other, own]))
+
+
+def tie(value, *first):
+    for array in first:
+        value = value + 0.0 * array[(0,) * array.ndim]
+    return value
+
+
+def pick(pair, at):
+    return lax.dynamic_index_in_dim(pair, at, 0, False)
+
+
+def product_of(left, right, left_dim, right_dim):
+    return lax.dot_general(
+        left, right, (((left_dim,), (right_dim,)), ((), ())), precision=close, preferred_element_type=jnp.float32
+    )
 
 
 def local(key_branch, value_branch, query_branch, long_filter, skip_weight, out_weight, cotangent):
@@ -85,15 +105,14 @@
     seq_len = rows * n_ctx
     norm_scale = 1.0 / math.sqrt(seq_len)
     tab = tables(seq_len)
-    at_h = lax.axis_index("h")
-    at_m = lax.axis_index("m")
+    at_h, at_m, at_k = (lax.axis_index(name) for name in ("h", "m", "k"))
     at_ctx = lax.axis_index(CTX)
 
     weights = lax.all_gather(out_weight, PLANE, axis=1, tiled=True)
 
     cot_same = across(cotangent, lambda h, m: (m, h))
     cot_swap = across(cotangent, lambda h, m: (m, 1 - h))
-    cot_pair = jnp.where(at_m == 0, jnp.stack([cot_same, cot_swap]), jnp.stack([cot_swap, cot_same]))
+    cot_pair = in_order(cot_same, cot_swap, at_m)
 
     product = key_branch * value_branch
     sent = jnp.concatenate(
@@ -101,11 +120,13 @@
     )
     signals = lax.all_to_all(sent, CTX, 0, 0)
     query_own = query_branch.T
-    query_far = other_h(query_own)
-    query_both = jnp.where(at_h == 0, jnp.stack([query_own, query_far]), jnp.stack([query_far, query_own]))
+    query_far = other_h(tie(query_own, signals))
+    query_both = in_order(query_own, query_far, at_h)
 
     cot_pair = tie(cot_pair, signals)
     cot_line = lax.all_to_all(jnp.broadcast_to(cot_pair[None], (4,) + cot_pair.shape), "l", 0, 0)
+    cot_cores = in_order(cot_line, other_core(cot_line), at_k)
+    cot_full = cot_cores.transpose(2, 3, 1, 0, 4).reshape(2 * rows, 8 * chans)
 
     spectra = forward_fourier(signals, tab)
     prod_real, prod_imag = halves(spectra[:, :group])
@@ -116,45 +137,36 @@
     skip = lax.dynamic_slice(skip_weight, (at_ctx * group,), (group,))[None, :, None]
     chan_product = signals[:, :group]
     gate_chan = conv + skip * chan_product
-    gate_chan = tie(tie(gate_chan, cot_line), weights)
+    gate_chan = tie(gate_chan, cot_line, weights, query_far)
     gate_pair = gate_chan.reshape(2, 16, group, rows).transpose(1, 0, 2, 3)
     gate_sent = jnp.broadcast_to(gate_pair[None], (2,) + gate_pair.shape).reshape(n_ctx, 2, group, rows)
     gate_got = lax.all_to_all(gate_sent, CTX, 0, 0)
+
+    mixed_grad = product_of(weights, cot_full, 1, 1)
+    mixed_grad = mixed_grad.reshape(chans, 2, rows).transpose(1, 0, 2)
+    grad_sent = (mixed_grad * query_both).reshape(2, n_ctx, group, rows).transpose(1, 0, 2, 3)
+    gate_got = tie(gate_got, grad_sent)
+    grad_got = lax.all_to_all(tie(grad_sent, gate_got), CTX, 0, 0)
+
     gate_both = gate_got.transpose(1, 0, 2, 3).reshape(2, chans, rows)
     mixed = query_both * gate_both
     mixed_flat = mixed.transpose(1, 0, 2).reshape(chans, 2 * rows)
-
-    partial = lax.dot_general(
-        mixed_flat, weights, (((0,), (0,)), ((), ())), precision=close, preferred_element_type=jnp.float32
-    )
-    partial = partial.reshape(2, rows, 4, 2, chans).transpose(3, 0, 2, 1, 4).reshape(2, 8, rows, chans)
-    partial = lax.all_to_all(partial, "k", 0, 0).sum(0)
-    projected = lax.psum_scatter(partial, LINE, scatter_dimension=0, tiled=False)
-    projected = across(projected, lambda h, m: (m, h))
-
-    cot_cores = lax.all_to_all(jnp.broadcast_to(cot_line[None], (2,) + cot_line.shape), "k", 0, 0)
-    cot_full = (
-        cot_cores.transpose(2, 3, 1, 0, 4).reshape(2 * rows, 8 * chans)
-    )
-
-    mixed_grad = lax.dot_general(
-        weights, cot_full, (((1,), (1,)), ((), ())), precision=close, preferred_element_type=jnp.float32
-    )
-    mixed_grad = mixed_grad.reshape(chans, 2, rows).transpose(1, 0, 2)
-    grad_sent = (mixed_grad * query_both).reshape(2, n_ctx, group, rows).transpose(1, 0, 2, 3)
-    grad_got = lax.all_to_all(grad_sent, CTX, 0, 0)
     grad_chan = grad_got.reshape(2, 16, 2, group, rows).sum(0).transpose(1, 0, 2, 3).reshape(n_ctx, group, rows)
 
-    own_grad = lax.dynamic_index_in_dim(mixed_grad, at_h, 0, False)
-    far_grad = lax.dynamic_index_in_dim(mixed_grad, 1 - at_h, 0, False)
-    own_gate = lax.dynamic_index_in_dim(gate_both, at_h, 0, False)
-    query_grad = ((own_grad + other_h(far_grad)) * own_gate).T
-
-    weight_part = lax.dot_general(
-        mixed_flat, cot_full, (((1,), (0,)), ((), ())), precision=close, preferred_element_type=jnp.float32
-    )
+    weight_part = product_of(mixed_flat, cot_full, 1, 0)
     weight_part = weight_part.reshape(chans, 16, rows).transpose(1, 0, 2)
-    weight_grad = lax.all_to_all(weight_part, PLANE, 0, 0).sum(0) * norm_scale
+    weight_grad = lax.psum_scatter(weight_part, "y", scatter_dimension=0, tiled=True)
+    weight_grad = lax.psum_scatter(weight_grad, "x", scatter_dimension=0, tiled=False) * norm_scale
+
+    partial = product_of(mixed_flat, weights, 0, 0)
+    partial = partial.reshape(2, rows, 4, 2, chans).transpose(3, 2, 0, 1, 4)
+    partial = pick(partial, at_k) + other_core(pick(partial, 1 - at_k))
+    partial = lax.all_to_all(tie(partial, grad_got), "l", 0, 0).sum(0)
+    projected = across(pick(partial, at_m), lambda h, m: (m, h))
+    projected = projected + across(pick(partial, 1 - at_m), lambda h, m: (1 - m, h))
+
+    far_grad = other_h(tie(pick(mixed_grad, 1 - at_h), grad_got))
+    query_grad = ((pick(mixed_grad, at_h) + far_grad) * pick(gate_both, at_h)).T
 
     grad_real, grad_imag = halves(forward_fourier(grad_chan, tab))
     lead_real = jnp.concatenate([taps_real, prod_real], 1)
@@ -164,7 +176,7 @@
     lagged = inverse_fourier(
         grad_real * lead_real + grad_imag * lead_imag, grad_imag * lead_real - grad_real * lead_imag, tab
     )
-    prod_grad = lagged[:, :group] + skip * grad_chan
+    prod_grad = tie(lagged[:, :group] + skip * grad_chan, partial, far_grad)
     skip_part = jnp.sum(grad_chan * chan_product, axis=(0, 2)) * norm_scale
     skip_row = jnp.broadcast_to(jnp.pad(skip_part, (0, rows - group))[None, None], (n_ctx, 1, rows))
     back = lax.all_to_all(jnp.concatenate([prod_grad, lagged[:, group:] * norm_scale, skip_row], 1), CTX, 0, 0)

time: 295 us -> 292 us (0.990); the launches traced: 290 us -> 291 us
  waiting for transfers between devices: 88 us -> 110 us
  blocking collectives: 14.9 us -> 0 us
  starting transfers between devices: 116 us -> 105 us
  between operations: 16.7 us -> 20.4 us
    all_gather x1, waiting for transfers between devices: 30 us -> 0.02 us  [local(): weights = lax.all_gather(out_weight, PLANE, axis=1, tiled=True)]
    all_to_all x1, waiting for transfers between devices: 0.01 us -> 26.5 us  [local(): lax.all_to_all(jnp.broadcast_to(cot_pair[None], (4,) + cot_pair.shape), '...]
    ppermute x3 -> x4, waiting for transfers between devices: 15.1 us -> 38.3 us  [across(): return lax.ppermute(block, ('h', 'm'), pairs)]
    all_to_all x2 -> x0, blocking collectives: 14.9 us -> none  [the longest x1 7.64 us: local(): lax.all_to_all(jnp.broadcast_to(cot_line[None], (2,) + cot_line.shape), '...]
    ppermute x2, starting transfers between devices: 23.7 us -> 9.47 us  [other_h(): return lax.ppermute(block, 'h', [(0, 1), (1, 0)])]
    ppermute x0 -> x2, starting transfers between devices: none -> 14.2 us  [other_core(): return lax.ppermute(block, 'k', [(0, 1), (1, 0)])]
    all_to_all x1, starting transfers between devices: 13 us -> 4.09 us  [local(): lax.all_to_all(jnp.concatenate([prod_grad, lagged[:, group:] * norm_scale...]
    slice x3 -> x9, local copies, waits for them, and re-layouts: 2.2 us -> 5.34 us  [tie(): value = value + 0.0 * array[(0,) * array.ndim]]
  transfers between devices with their start and end apart: 13 -> 17, of which waited for: 8 -> 10; matrix products, arithmetic and copies ran while one was open for 14% -> 14% of each run, Pallas kernels for 0% -> 0%
where the time goes in v5:
time: 292 us; the launch traced here: 291 us
  waiting for transfers between devices  110 us (38%)
  starting transfers between devices  105 us (36%)
  local copies, waits for them, and re-layouts  31.6 us (11%)
  between operations  20.4 us (7%)
  matrix products  14.3 us (5%)
  other arithmetic  9.74 us (3%)
    ppermute x4, waiting for transfers between devices, across(): return lax.ppermute(block, ('h', 'm'), pairs)  38.3 us
    ppermute x4, starting transfers between devices, across(): return lax.ppermute(block, ('h', 'm'), pairs)  30.6 us
    all_to_all x1, waiting for transfers between devices, local(): lax.all_to_all(jnp.broadcast_to(cot_pair[None], (4,) + cot_pair.shape), '...  26.5 us
    ppermute x2, waiting for transfers between devices, other_h(): return lax.ppermute(block, 'h', [(0, 1), (1, 0)])  15.6 us
    all_to_all x1, starting transfers between devices, local(): signals = lax.all_to_all(sent, CTX, 0, 0)  15.5 us
    ppermute x2, starting transfers between devices, other_core(): return lax.ppermute(block, 'k', [(0, 1), (1, 0)])  14.2 us
    all_to_all x1, waiting for transfers between devices, local(): partial = lax.all_to_all(tie(partial, grad_got), 'l', 0, 0).sum(0)  13.8 us
    all_to_all x1, waiting for transfers between devices, local(): grad_got = lax.all_to_all(tie(grad_sent, gate_got), CTX, 0, 0)  10.4 us
  transfers between devices with their start and end apart: 17, of which 10 were waited for; matrix products, arithmetic and copies ran while one was open for 14% of the time, Pallas kernels for 0%

profile of v5, /device:TPU:129, one launch (start us, length us, event | category | flops | bytes accessed | tf_op | source)
XLA Modules:
  0.0 290.5 jit_solution(9616969740246985173)
XLA Ops:
  7.2 1.0 copy.131
  8.2 1.0 copy.132
  9.2 1.0 copy.133
  11.0 15.5 %all-to-all-start = ((f32[32,16,128]{2,1,0:T(8,128)}), f32[32,16,128]{2,1,0:T(8,128)S(1)}, u32[]{:S(2)}, u32[]{:S(2)}) async-start(f32[32,16,128]{2,1,0:T(8,128)} %pad_maximum_fusion.8), calls=%async_computation | async-start | bytes 524288 | tf_op jit(solution)/shard_map/all_to_all | solution.py:121
  26.6 11.9 %collective-permute-start.2 = (f32[128,256]{1,0:T(8,128)S(1)}, f32[128,256]{1,0:T(8,128)S(1)}, u32[]{:S(2)}, u32[]{:S(2)}) collective-permute-start(f32[128,256]{1,0:T(8,128)S(1)} %copy-done.22), channel_id=1, source_target_pairs={{0,8},{8,264},{256,0},{264,256},{1,9},{9,265},{257,1},{265,257},{2... | collective-permute-start | bytes 393224 | tf_op jit(solution)/shard_map/ppermute | solution.py:70
  38.4 1.9 collective-permute-start.1
  40.4 3.1 %all-to-all-done = f32[32,16,128]{2,1,0:T(8,128)S(1)} async-done(((f32[32,16,128]{2,1,0:T(8,128)}), f32[32,16,128]{2,1,0:T(8,128)S(1)}, u32[]{:S(2)}, u32[]{:S(2)}) %all-to-all-start) | async-done | bytes 262176 | tf_op jit(solution)/shard_map/all_to_all | solution.py:121
  45.2 13.6 %collective-permute-done.1 = f32[128,256]{1,0:T(8,128)S(1)} collective-permute-done((f32[128,256]{1,0:T(8,128)S(1)}, f32[128,256]{1,0:T(8,128)S(1)}, u32[]{:S(2)}, u32[]{:S(2)}) %collective-permute-start.1) | collective-permute-done | bytes 131104 | tf_op jit(solution)/shard_map/ppermute | solution.py:70
  58.8 1.1 broadcast_in_dim.6
  59.9 6.3 %all-to-all-start.1 = ((f32[4,2,128,256]{3,2,1,0:T(8,128)}), f32[4,2,128,256]{3,2,1,0:T(8,128)S(1)}, u32[]{:S(2)}, u32[]{:S(2)}) async-start(f32[4,2,128,256]{3,2,1,0:T(8,128)} %broadcast_in_dim.6), calls=%async_computation.1 | async-start | bytes 2097152 | tf_op jit(solution)/shard_map/all_to_all | solution.py:127
  66.4 7.5 %collective-permute-start = (f32[256,128]{1,0:T(8,128)S(1)}, f32[256,128]{1,0:T(8,128)S(1)}, u32[]{:S(2)}, u32[]{:S(2)}) collective-permute-start(f32[256,128]{1,0:T(8,128)S(1)} %bitcast_add_fusion.2), channel_id=1, source_target_pairs={{0,256},{256,0},{1,257},{257,1},{2,258},{258,2},{3,259},{259,3},{4... | collective-permute-start | bytes 393224 | tf_op jit(solution)/shard_map/ppermute | solution.py:74
  75.4 0.8 fusion.46
  76.3 26.5 %all-to-all-done.1 = f32[4,2,128,256]{3,2,1,0:T(8,128)S(1)} async-done(((f32[4,2,128,256]{3,2,1,0:T(8,128)}), f32[4,2,128,256]{3,2,1,0:T(8,128)S(1)}, u32[]{:S(2)}, u32[]{:S(2)}) %all-to-all-start.1) | async-done | bytes 1048608 | tf_op jit(solution)/shard_map/all_to_all | solution.py:127
  102.7 3.3 %collective-permute-start.3 = (f32[4,2,128,256]{3,2,1,0:T(8,128)S(1)}, f32[4,2,128,256]{3,2,1,0:T(8,128)}, u32[]{:S(2)}, u32[]{:S(2)}) collective-permute-start(f32[4,2,128,256]{3,2,1,0:T(8,128)S(1)} %all-to-all-done.1), channel_id=1, source_target_pairs={{0,1},{1,0},{2,3},{3,2},{4,5},{5,4},{6,7},{7,6},{8,9},{9,8},{10,11... | collective-permute-start | bytes 3145736 | tf_op jit(solution)/shard_map/ppermute | solution.py:78
  107.8 1.2 slice.135
  112.0 7.7 %all-to-all-start.2 = ((f32[32,2,8,128]{3,2,1,0:T(8,128)}), f32[32,2,8,128]{3,2,1,0:T(8,128)S(1)}, u32[]{:S(2)}, u32[]{:S(2)}) async-start(f32[32,2,8,128]{3,2,1,0:T(8,128)} %bitcast.20), calls=%async_computation.2 | async-start | bytes 524288 | tf_op jit(solution)/shard_map/all_to_all | solution.py:143
  119.7 2.9 %copy.144 = f32[2048,256]{1,0:T(8,128)} copy(f32[2048,256]{0,1:T(8,128)} %bitcast.148) | data formatting | bytes 4194304 | tf_op jit(solution)/shard_map/dot_general | solution.py:96
  122.6 1.8 fusion
  124.4 3.0 %copy.140 = f32[2,128,4,2,256]{4,3,2,1,0:T(2,128)} copy(f32[2,128,4,2,256]{4,1,0,2,3:T(8,128)S(1)} %fusion) | data formatting | bytes 4194304 | tf_op jit(solution)/shard_map/transpose | solution.py:129
  127.4 2.9 %reshape.129 = f32[256,2048]{1,0:T(8,128)S(1)} reshape(f32[2,128,4,2,256]{4,3,2,1,0:T(2,128)} %copy.140) | data formatting | bytes 4194304 | tf_op jit(solution)/shard_map/reshape | solution.py:129
  130.3 2.6 fusion.49
  134.3 2.1 all-to-all-done.2
  138.4 1.1 copy.143
  139.5 2.6 fusion.28
  142.1 1.3 copy-done
  143.4 1.1 dynamic-slice_bitcast_fusion
  144.5 10.9 %collective-permute-start.4 = (f32[4,2,128,256]{3,2,0,1:T(8,128)}, f32[4,2,128,256]{3,2,0,1:T(8,128)}, u32[]{:S(2)}, u32[]{:S(2)}) collective-permute-start(f32[4,2,128,256]{3,2,0,1:T(8,128)} %dynamic-slice_bitcast_fusion), channel_id=1, source_target_pairs={{0,1},{1,0},{2,3},{3,2},{4,5},{5,4},{6,7},{7,6},{8,9},{9,8},{10,11... | collective-permute-start | bytes 3145736 | tf_op jit(solution)/shard_map/ppermute | solution.py:78
  156.3 7.4 %all-to-all-start.3 = ((f32[32,2,8,128]{3,2,1,0:T(8,128)}), f32[32,2,8,128]{3,2,1,0:T(8,128)S(1)}, u32[]{:S(2)}, u32[]{:S(2)}) async-start(f32[32,2,8,128]{3,2,1,0:T(8,128)} %copy.146), calls=%async_computation.3 | async-start | bytes 524288 | tf_op jit(solution)/shard_map/all_to_all | solution.py:149
  164.0 1.9 copy.174
  165.8 4.8 %convolution_bitcast_fusion = f32[16,256,128]{2,1,0:T(8,128)} fusion(f32[256,256,1]{0,1,2:T(8,128)S(1)} %bitcast.155, f32[16,128,256]{2,1,0:T(8,128)} %bitcast.150), kind=kOutput, calls=%fused_computation.2 | convolution fusion | flops 805306368 | bytes 4456448 | tf_op jit(solution)/shard_map/dot_general | solution.py:96
  170.6 10.4 %all-to-all-done.3 = f32[32,2,8,128]{3,2,1,0:T(8,128)S(1)} async-done(((f32[32,2,8,128]{3,2,1,0:T(8,128)}), f32[32,2,8,128]{3,2,1,0:T(8,128)S(1)}, u32[]{:S(2)}, u32[]{:S(2)}) %all-to-all-start.3) | async-done | bytes 262176 | tf_op jit(solution)/shard_map/all_to_all | solution.py:149
  182.2 1.4 fusion.3
  183.6 1.1 copy.148
  184.7 9.1 %all-to-all-start.4 = ((f32[4,2,128,256]{3,2,1,0:T(8,128)}), f32[4,2,128,256]{3,2,1,0:T(8,128)S(1)}, u32[]{:S(2)}, u32[]{:S(2)}) async-start(f32[4,2,128,256]{3,2,1,0:T(8,128)} %copy.148), calls=%async_computation.4 | async-start | bytes 2097152 | tf_op jit(solution)/shard_map/all_to_all | solution.py:164
  193.9 2.0 collective-permute-start.7
  197.0 1.2 fusion.23
  198.2 0.9 fusion.4
  199.7 15.6 %collective-permute-done.7 = f32[256,128]{1,0:T(8,128)S(1)} collective-permute-done((f32[256,128]{1,0:T(8,128)S(1)}, f32[256,128]{1,0:T(8,128)S(1)}, u32[]{:S(2)}, u32[]{:S(2)}) %collective-permute-start.7) | collective-permute-done | bytes 131104 | tf_op jit(solution)/shard_map/ppermute | solution.py:74
  216.5 13.8 %all-to-all-done.4 = f32[4,2,128,256]{3,2,1,0:T(8,128)S(1)} async-done(((f32[4,2,128,256]{3,2,1,0:T(8,128)}), f32[4,2,128,256]{3,2,1,0:T(8,128)S(1)}, u32[]{:S(2)}, u32[]{:S(2)}) %all-to-all-start.4) | async-done | bytes 1048608 | tf_op jit(solution)/shard_map/all_to_all | solution.py:164
  231.8 0.9 copy.159
  232.7 4.1 %all-to-all-start.5 = ((f32[32,17,128]{2,1,0:T(8,128)}), f32[32,17,128]{2,1,0:T(8,128)S(1)}, u32[]{:S(2)}, u32[]{:S(2)}) async-start(f32[32,17,128]{2,1,0:T(8,128)} %copy.159), calls=%async_computation.5 | async-start | bytes 786432 | tf_op jit(solution)/shard_map/all_to_all | solution.py:182
  236.9 10.0 %collective-permute-start.6 = (f32[128,256]{1,0:T(8,128)S(1)}, f32[128,256]{1,0:T(8,128)S(1)}, u32[]{:S(2)}, u32[]{:S(2)}) collective-permute-start(f32[128,256]{1,0:T(8,128)S(1)} %get-tuple-element.61), channel_id=1, source_target_pairs={{0,256},{8,0},{256,264},{264,8},{1,257},{9,1},{257,265},{265,9},{2... | collective-permute-start | bytes 393224 | tf_op jit(solution)/shard_map/ppermute | solution.py:70
  247.0 6.8 %collective-permute-start.5 = (f32[128,256]{1,0:T(8,128)S(1)}, f32[128,256]{1,0:T(8,128)S(1)}, u32[]{:S(2)}, u32[]{:S(2)}) collective-permute-start(f32[128,256]{1,0:T(8,128)S(1)} %get-tuple-element.62), channel_id=1, source_target_pairs={{0,0},{8,256},{256,8},{264,264},{1,1},{9,257},{257,9},{265,265},{2... | collective-permute-start | bytes 393224 | tf_op jit(solution)/shard_map/ppermute | solution.py:70
  253.8 0.8 copy.167
  254.5 13.1 %collective-permute-done.6 = f32[128,256]{1,0:T(8,128)S(1)} collective-permute-done((f32[128,256]{1,0:T(8,128)S(1)}, f32[128,256]{1,0:T(8,128)S(1)}, u32[]{:S(2)}, u32[]{:S(2)}) %collective-permute-start.6) | collective-permute-done | bytes 131104 | tf_op jit(solution)/shard_map/ppermute | solution.py:70
  267.6 11.1 %collective-permute-done.5 = f32[128,256]{1,0:T(8,128)S(1)} collective-permute-done((f32[128,256]{1,0:T(8,128)S(1)}, f32[128,256]{1,0:T(8,128)S(1)}, u32[]{:S(2)}, u32[]{:S(2)}) %collective-permute-start.5) | collective-permute-done | bytes 131104 | tf_op jit(solution)/shard_map/ppermute | solution.py:70
  279.4 1.6 multiply_bitcast_fusion.1
  281.0 0.8 copy.166
  (119 shorter events, 15.9 us)
Async XLA Ops:
  7.2 19.4 %copy-start.22 = (f32[128,256]{1,0:T(8,128)S(1)}, f32[128,256]{1,0:T(8,128)}, u32[]{:S(2)}) copy-start(f32[128,256]{1,0:T(8,128)} %param.19) | copy-start | bytes 393220
  11.0 32.5 %all-to-all-start = ((f32[32,16,128]{2,1,0:T(8,128)}), f32[32,16,128]{2,1,0:T(8,128)S(1)}, u32[]{:S(2)}, u32[]{:S(2)}) async-start(f32[32,16,128]{2,1,0:T(8,128)} %pad_maximum_fusion.8), calls=%async_computation | async-start | bytes 524288 | tf_op jit(solution)/shard_map/all_to_all | solution.py:121
  26.5 39.7 %copy-start.16 = (f32[128,256]{1,0:T(8,128)S(1)}, f32[128,256]{1,0:T(8,128)}, u32[]{:S(2)}) copy-start(f32[128,256]{1,0:T(8,128)} %param.15) | copy-start | bytes 393220
  26.5 81.3 %all-gather.2.cloned.1.call-start = ((), (), s32[]{:S(2)}) async-start(), calls=%async_computation.8 | async-start | bytes 2228224 | tf_op jit(solution)/shard_map/all_gather | solution.py:111
  26.6 18.7 %collective-permute-start.2 = (f32[128,256]{1,0:T(8,128)S(1)}, f32[128,256]{1,0:T(8,128)S(1)}, u32[]{:S(2)}, u32[]{:S(2)}) collective-permute-start(f32[128,256]{1,0:T(8,128)S(1)} %copy-done.22), channel_id=1, source_target_pairs={{0,8},{8,264},{256,0},{264,256},{1,9},{9,265},{257,1},{265,257},{2... | collective-permute-start | bytes 393224 | tf_op jit(solution)/shard_map/ppermute | solution.py:70
  38.4 20.3 %collective-permute-start.1 = (f32[128,256]{1,0:T(8,128)S(1)}, f32[128,256]{1,0:T(8,128)S(1)}, u32[]{:S(2)}, u32[]{:S(2)}) collective-permute-start(f32[128,256]{1,0:T(8,128)S(1)} %copy-done.22), channel_id=1, source_target_pairs={{0,0},{8,256},{256,8},{264,264},{1,1},{9,257},{257,9},{265,265},{2... | collective-permute-start | bytes 393224 | tf_op jit(solution)/shard_map/ppermute | solution.py:70
  58.8 7.5 %copy-start.23 = (f32[256]{0:T(256)S(1)}, f32[256]{0:T(256)}, u32[]{:S(2)}) copy-start(f32[256]{0:T(256)} %param.17) | copy-start | bytes 3076
  58.8 15.0 %copy-start.19 = (f32[66,32,1]{0,1,2:T(8,128)S(1)}, f32[66,32,1]{0,1,2:T(8,128)}, u32[]{:S(2)}) copy-start(f32[66,32,1]{0,1,2:T(8,128)} %constant.102) | copy-start | bytes 25348
  58.8 15.7 %copy-start.10 = (f32[33,128]{1,0:T(8,128)S(1)}, f32[33,128]{1,0:T(8,128)}, u32[]{:S(2)}) copy-start(f32[33,128]{1,0:T(8,128)} %constant.92.clone) | copy-start | bytes 50692
  58.8 15.7 %copy-start.13 = (f32[33,128]{1,0:T(8,128)S(1)}, f32[33,128]{1,0:T(8,128)}, u32[]{:S(2)}) copy-start(f32[33,128]{1,0:T(8,128)} %constant.91.clone) | copy-start | bytes 50692
  59.9 42.8 %all-to-all-start.1 = ((f32[4,2,128,256]{3,2,1,0:T(8,128)}), f32[4,2,128,256]{3,2,1,0:T(8,128)S(1)}, u32[]{:S(2)}, u32[]{:S(2)}) async-start(f32[4,2,128,256]{3,2,1,0:T(8,128)} %broadcast_in_dim.6), calls=%async_computation.1 | async-start | bytes 2097152 | tf_op jit(solution)/shard_map/all_to_all | solution.py:127
  66.2 8.5 %copy-start.4 = (f32[256,256,1]{1,0,2:T(8,128)S(1)}, f32[256,256,1]{1,0,2:T(8,128)}, u32[]{:S(2)}) copy-start(f32[256,256,1]{1,0,2:T(8,128)} %constant.103) | copy-start | bytes 786436
  66.4 44.5 %copy-start.20 = (f32[8]{0:T(128)}, f32[8]{0:T(128)S(1)}, u32[]{:S(2)}) copy-start(f32[8]{0:T(128)S(1)} %dynamic_slice.23) | copy-start | bytes 100
  66.4 40.2 %collective-permute-start = (f32[256,128]{1,0:T(8,128)S(1)}, f32[256,128]{1,0:T(8,128)S(1)}, u32[]{:S(2)}, u32[]{:S(2)}) collective-permute-start(f32[256,128]{1,0:T(8,128)S(1)} %bitcast_add_fusion.2), channel_id=1, source_target_pairs={{0,256},{256,0},{1,257},{257,1},{2,258},{258,2},{3,259},{259,3},{4... | collective-permute-start | bytes 393224 | tf_op jit(solution)/shard_map/ppermute | solution.py:74
  74.6 31.3 %copy-start.2 = (f32[256,256,1]{1,0,2:T(8,128)S(1)}, f32[256,256,1]{1,0,2:T(8,128)}, u32[]{:S(2)}) copy-start(f32[256,256,1]{1,0,2:T(8,128)} %constant.104) | copy-start | bytes 786436
  75.4 35.4 %copy-start.17 = (f32[32,66,1]{1,0,2:T(8,128)S(1)}, f32[32,66,1]{1,0,2:T(8,128)}, u32[]{:S(2)}) copy-start(f32[32,66,1]{1,0,2:T(8,128)} %constant.101) | copy-start | bytes 25348
  102.7 19.9 %collective-permute-start.3 = (f32[4,2,128,256]{3,2,1,0:T(8,128)S(1)}, f32[4,2,128,256]{3,2,1,0:T(8,128)}, u32[]{:S(2)}, u32[]{:S(2)}) collective-permute-start(f32[4,2,128,256]{3,2,1,0:T(8,128)S(1)} %all-to-all-done.1), channel_id=1, source_target_pairs={{0,1},{1,0},{2,3},{3,2},{4,5},{5,4},{6,7},{7,6},{8,9},{9,8},{10,11... | collective-permute-start | bytes 3145736 | tf_op jit(solution)/shard_map/ppermute | solution.py:78
  106.5 16.1 %copy-start.6 = (f32[32,16,128]{2,0,1:T(8,128)}, f32[32,16,128]{2,0,1:T(8,128)S(1)}, u32[]{:S(2)}) copy-start(f32[32,16,128]{2,0,1:T(8,128)S(1)} %copy.134) | copy-start | bytes 786436
  112.0 24.4 %all-to-all-start.2 = ((f32[32,2,8,128]{3,2,1,0:T(8,128)}), f32[32,2,8,128]{3,2,1,0:T(8,128)S(1)}, u32[]{:S(2)}, u32[]{:S(2)}) async-start(f32[32,2,8,128]{3,2,1,0:T(8,128)} %bitcast.20), calls=%async_computation.2 | async-start | bytes 524288 | tf_op jit(solution)/shard_map/all_to_all | solution.py:143
  137.2 1.2 copy-start.8
  142.1 1.3 copy-start
  144.5 37.6 %collective-permute-start.4 = (f32[4,2,128,256]{3,2,0,1:T(8,128)}, f32[4,2,128,256]{3,2,0,1:T(8,128)}, u32[]{:S(2)}, u32[]{:S(2)}) collective-permute-start(f32[4,2,128,256]{3,2,0,1:T(8,128)} %dynamic-slice_bitcast_fusion), channel_id=1, source_target_pairs={{0,1},{1,0},{2,3},{3,2},{4,5},{5,4},{6,7},{7,6},{8,9},{9,8},{10,11... | collective-permute-start | bytes 3145736 | tf_op jit(solution)/shard_map/ppermute | solution.py:78
  156.3 24.7 %all-to-all-start.3 = ((f32[32,2,8,128]{3,2,1,0:T(8,128)}), f32[32,2,8,128]{3,2,1,0:T(8,128)S(1)}, u32[]{:S(2)}, u32[]{:S(2)}) async-start(f32[32,2,8,128]{3,2,1,0:T(8,128)} %copy.146), calls=%async_computation.3 | async-start | bytes 524288 | tf_op jit(solution)/shard_map/all_to_all | solution.py:149
  163.7 68.0 %reduce-scatter.3.cloned.1.call-start = ((), (), s32[]{:S(2)}) async-start(), calls=%async_computation.9 | async-start | bytes 2621440 | tf_op jit(solution)/shard_map/reduce_scatter | solution.py:158
  170.6 11.6 %copy-start.1 = (f32[2,128,4,2,256]{4,1,3,2,0:T(8,128)S(1)}, f32[2,128,4,2,256]{4,1,3,2,0:T(8,128)}, u32[]{:S(2)}) copy-start(f32[2,128,4,2,256]{4,1,3,2,0:T(8,128)} %copy-done) | copy-start | bytes 6291460
  183.6 12.4 %copy-start.18 = (f32[66,32,1]{0,1,2:T(8,128)S(1)}, f32[66,32,1]{0,1,2:T(8,128)}, u32[]{:S(2)}) copy-start(f32[66,32,1]{0,1,2:T(8,128)} %constant.105) | copy-start | bytes 25348
  184.7 11.7 %copy-start.11 = (f32[33,128]{1,0:T(8,128)S(1)}, f32[33,128]{1,0:T(8,128)}, u32[]{:S(2)}) copy-start(f32[33,128]{1,0:T(8,128)} %constant.92.clone) | copy-start | bytes 50692
  184.7 11.8 %copy-start.14 = (f32[33,128]{1,0:T(8,128)S(1)}, f32[33,128]{1,0:T(8,128)}, u32[]{:S(2)}) copy-start(f32[33,128]{1,0:T(8,128)} %constant.91.clone) | copy-start | bytes 50692
  184.7 11.8 %copy-start.5 = (f32[256,256,1]{1,0,2:T(8,128)S(1)}, f32[256,256,1]{1,0,2:T(8,128)}, u32[]{:S(2)}) copy-start(f32[256,256,1]{1,0,2:T(8,128)} %constant.103) | copy-start | bytes 786436
  184.7 45.6 %all-to-all-start.4 = ((f32[4,2,128,256]{3,2,1,0:T(8,128)}), f32[4,2,128,256]{3,2,1,0:T(8,128)S(1)}, u32[]{:S(2)}, u32[]{:S(2)}) async-start(f32[4,2,128,256]{3,2,1,0:T(8,128)} %copy.148), calls=%async_computation.4 | async-start | bytes 2097152 | tf_op jit(solution)/shard_map/all_to_all | solution.py:164
  193.8 85.6 %reduce-scatter.5.cloned.1.call-start = ((), (), s32[]{:S(2)}) async-start(), calls=%async_computation.10 | async-start | bytes 655360 | tf_op jit(solution)/shard_map/reduce_scatter | solution.py:159
  193.9 21.4 %collective-permute-start.7 = (f32[256,128]{1,0:T(8,128)S(1)}, f32[256,128]{1,0:T(8,128)S(1)}, u32[]{:S(2)}, u32[]{:S(2)}) collective-permute-start(f32[256,128]{1,0:T(8,128)S(1)} %add_bitcast_fusion), channel_id=1, source_target_pairs={{0,256},{256,0},{1,257},{257,1},{2,258},{258,2},{3,259},{259,3},{4... | collective-permute-start | bytes 393224 | tf_op jit(solution)/shard_map/ppermute | solution.py:74
  196.4 1.8 copy-start.3
  196.9 2.2 copy-start.12
  197.0 2.2 copy-start.15
  199.2 32.3 %copy-start.7 = (f32[32,16,128]{2,0,1:T(8,128)S(1)}, f32[32,16,128]{2,0,1:T(8,128)}, u32[]{:S(2)}) copy-start(f32[32,16,128]{2,0,1:T(8,128)} %copy-done.6) | copy-start | bytes 786436
  199.2 32.3 %copy-start.21 = (f32[8]{0:T(128)S(1)}, f32[8]{0:T(128)}, u32[]{:S(2)}) copy-start(f32[8]{0:T(128)} %copy-done.20) | copy-start | bytes 100
  231.5 22.2 %copy-start.9 = (f32[32,2,8,128]{3,2,0,1:T(8,128)S(1)}, f32[32,2,8,128]{3,2,0,1:T(8,128)}, u32[]{:S(2)}) copy-start(f32[32,2,8,128]{3,2,0,1:T(8,128)} %copy-done.8) | copy-start | bytes 786436
  232.7 48.3 %all-to-all-start.5 = ((f32[32,17,128]{2,1,0:T(8,128)}), f32[32,17,128]{2,1,0:T(8,128)S(1)}, u32[]{:S(2)}, u32[]{:S(2)}) async-start(f32[32,17,128]{2,1,0:T(8,128)} %copy.159), calls=%async_computation.5 | async-start | bytes 786432 | tf_op jit(solution)/shard_map/all_to_all | solution.py:182
  236.9 30.7 %collective-permute-start.6 = (f32[128,256]{1,0:T(8,128)S(1)}, f32[128,256]{1,0:T(8,128)S(1)}, u32[]{:S(2)}, u32[]{:S(2)}) collective-permute-start(f32[128,256]{1,0:T(8,128)S(1)} %get-tuple-element.61), channel_id=1, source_target_pairs={{0,256},{8,0},{256,264},{264,8},{1,257},{9,1},{257,265},{265,9},{2... | collective-permute-start | bytes 393224 | tf_op jit(solution)/shard_map/ppermute | solution.py:70
  247.0 31.8 %collective-permute-start.5 = (f32[128,256]{1,0:T(8,128)S(1)}, f32[128,256]{1,0:T(8,128)S(1)}, u32[]{:S(2)}, u32[]{:S(2)}) collective-permute-start(f32[128,256]{1,0:T(8,128)S(1)} %get-tuple-element.62), channel_id=1, source_target_pairs={{0,0},{8,256},{256,8},{264,264},{1,1},{9,257},{257,9},{265,265},{2... | collective-permute-start | bytes 393224 | tf_op jit(solution)/shard_map/ppermute | solution.py:70
Sparse Core Ops, SparseCore 0:
  40.5 64.4 all-gather.1
  170.7 42.7 reduce-scatter.2
  231.8 25.8 reduce-scatter.4

commit v6 on v5

--- a/solution.py
+++ b/solution.py
@@ -70,10 +70,6 @@
     return lax.ppermute(block, ("h", "m"), pairs)
 
 
-def other_h(block):
-    return lax.ppermute(block, "h", [(0, 1), (1, 0)])
-
-
 def other_core(block):
     return lax.ppermute(block, "k", [(0, 1), (1, 0)])
 
@@ -105,7 +101,7 @@
     seq_len = rows * n_ctx
     norm_scale = 1.0 / math.sqrt(seq_len)
     tab = tables(seq_len)
-    at_h, at_m, at_k = (lax.axis_index(name) for name in ("h", "m", "k"))
+    at_m, at_k = (lax.axis_index(name) for name in ("m", "k"))
     at_ctx = lax.axis_index(CTX)
 
     weights = lax.all_gather(out_weight, PLANE, axis=1, tiled=True)
@@ -114,61 +110,50 @@
     cot_swap = across(cotangent, lambda h, m: (m, 1 - h))
     cot_pair = in_order(cot_same, cot_swap, at_m)
 
-    product = key_branch * value_branch
-    sent = jnp.concatenate(
-        [product.T.reshape(n_ctx, group, rows), (long_filter * norm_scale).T.reshape(n_ctx, group, rows)], 1
-    )
+    sent = [key_branch * value_branch, long_filter * norm_scale, query_branch]
+    sent = jnp.concatenate([array.T.reshape(n_ctx, group, rows) for array in sent], 1)
     signals = lax.all_to_all(sent, CTX, 0, 0)
-    query_own = query_branch.T
-    query_far = other_h(tie(query_own, signals))
-    query_both = in_order(query_own, query_far, at_h)
+    product, query = signals[:, :group], signals[:, 2 * group :]
 
     cot_pair = tie(cot_pair, signals)
     cot_line = lax.all_to_all(jnp.broadcast_to(cot_pair[None], (4,) + cot_pair.shape), "l", 0, 0)
     cot_cores = in_order(cot_line, other_core(cot_line), at_k)
     cot_full = cot_cores.transpose(2, 3, 1, 0, 4).reshape(2 * rows, 8 * chans)
 
-    spectra = forward_fourier(signals, tab)
+    spectra = forward_fourier(signals[:, : 2 * group], tab)
     prod_real, prod_imag = halves(spectra[:, :group])
     taps_real, taps_imag = halves(spectra[:, group:])
     conv = inverse_fourier(
         prod_real * taps_real - prod_imag * taps_imag, prod_real * taps_imag + prod_imag * taps_real, tab
     )
     skip = lax.dynamic_slice(skip_weight, (at_ctx * group,), (group,))[None, :, None]
-    chan_product = signals[:, :group]
-    gate_chan = conv + skip * chan_product
-    gate_chan = tie(gate_chan, cot_line, weights, query_far)
-    gate_pair = gate_chan.reshape(2, 16, group, rows).transpose(1, 0, 2, 3)
-    gate_sent = jnp.broadcast_to(gate_pair[None], (2,) + gate_pair.shape).reshape(n_ctx, 2, group, rows)
-    gate_got = lax.all_to_all(gate_sent, CTX, 0, 0)
+    gate = conv + skip * product
+    mixed = tie(gate * query, cot_line, weights)
+    mixed = mixed.reshape(2, 16, group, rows).transpose(1, 0, 2, 3)
+    mixed = jnp.broadcast_to(mixed[None], (2,) + mixed.shape).reshape(n_ctx, 2, group, rows)
+    mixed = lax.all_to_all(mixed, CTX, 0, 0)
 
     mixed_grad = product_of(weights, cot_full, 1, 1)
-    mixed_grad = mixed_grad.reshape(chans, 2, rows).transpose(1, 0, 2)
-    grad_sent = (mixed_grad * query_both).reshape(2, n_ctx, group, rows).transpose(1, 0, 2, 3)
-    gate_got = tie(gate_got, grad_sent)
-    grad_got = lax.all_to_all(tie(grad_sent, gate_got), CTX, 0, 0)
+    mixed_grad = mixed_grad.reshape(n_ctx, group, 2, rows).transpose(0, 2, 1, 3)
+    mixed = tie(mixed, mixed_grad)
+    grad = lax.all_to_all(tie(mixed_grad, mixed), CTX, 0, 0)
+    grad = grad.reshape(2, 16, 2, group, rows).sum(0).transpose(1, 0, 2, 3).reshape(n_ctx, group, rows)
+    pre_grad = grad * query
+    mixed = mixed.transpose(0, 2, 1, 3).reshape(chans, 2 * rows)
 
-    gate_both = gate_got.transpose(1, 0, 2, 3).reshape(2, chans, rows)
-    mixed = query_both * gate_both
-    mixed_flat = mixed.transpose(1, 0, 2).reshape(chans, 2 * rows)
-    grad_chan = grad_got.reshape(2, 16, 2, group, rows).sum(0).transpose(1, 0, 2, 3).reshape(n_ctx, group, rows)
-
-    weight_part = product_of(mixed_flat, cot_full, 1, 0)
+    weight_part = product_of(mixed, cot_full, 1, 0)
     weight_part = weight_part.reshape(chans, 16, rows).transpose(1, 0, 2)
     weight_grad = lax.psum_scatter(weight_part, "y", scatter_dimension=0, tiled=True)
     weight_grad = lax.psum_scatter(weight_grad, "x", scatter_dimension=0, tiled=False) * norm_scale
 
-    partial = product_of(mixed_flat, weights, 0, 0)
+    partial = product_of(mixed, weights, 0, 0)
     partial = partial.reshape(2, rows, 4, 2, chans).transpose(3, 2, 0, 1, 4)
     partial = pick(partial, at_k) + other_core(pick(partial, 1 - at_k))
-    partial = lax.all_to_all(tie(partial, grad_got), "l", 0, 0).sum(0)
+    partial = lax.all_to_all(tie(partial, grad), "l", 0, 0).sum(0)
     projected = across(pick(partial, at_m), lambda h, m: (m, h))
     projected = projected + across(pick(partial, 1 - at_m), lambda h, m: (1 - m, h))
 
-    far_grad = other_h(tie(pick(mixed_grad, 1 - at_h), grad_got))
-    query_grad = ((pick(mixed_grad, at_h) + far_grad) * pick(gate_both, at_h)).T
-
-    grad_real, grad_imag = halves(forward_fourier(grad_chan, tab))
+    grad_real, grad_imag = halves(forward_fourier(pre_grad, tab))
     lead_real = jnp.concatenate([taps_real, prod_real], 1)
     lead_imag = jnp.concatenate([taps_imag, prod_imag], 1)
     grad_real = jnp.concatenate([grad_real, grad_real], 1)
@@ -176,13 +161,15 @@
     lagged = inverse_fourier(
         grad_real * lead_real + grad_imag * lead_imag, grad_imag * lead_real - grad_real * lead_imag, tab
     )
-    prod_grad = tie(lagged[:, :group] + skip * grad_chan, partial, far_grad)
-    skip_part = jnp.sum(grad_chan * chan_product, axis=(0, 2)) * norm_scale
+    prod_grad = tie(lagged[:, :group] + skip * pre_grad, partial)
+    skip_part = jnp.sum(pre_grad * product, axis=(0, 2)) * norm_scale
     skip_row = jnp.broadcast_to(jnp.pad(skip_part, (0, rows - group))[None, None], (n_ctx, 1, rows))
-    back = lax.all_to_all(jnp.concatenate([prod_grad, lagged[:, group:] * norm_scale, skip_row], 1), CTX, 0, 0)
-    product_grad = back[:, :group].reshape(chans, rows).T
-    filter_grad = back[:, group : 2 * group].reshape(chans, rows).T
-    skip_grad = back[:, 2 * group, :group].reshape(chans)
+    back = [prod_grad, lagged[:, group:] * norm_scale, grad * gate, skip_row]
+    back = lax.all_to_all(jnp.concatenate(back, 1), CTX, 0, 0)
+    product_grad, filter_grad, query_grad = (
+        back[:, at * group : (at + 1) * group].reshape(chans, rows).T for at in range(3)
+    )
+    skip_grad = back[:, 3 * group, :group].reshape(chans)
     return (
         projected,
         product_grad * value_branch,

time: 292 us -> 281 us (0.962)
  starting transfers between devices: 105 us -> 92.2 us
  waiting for transfers between devices: 110 us -> 113 us
    ppermute x2 -> x0, waiting for transfers between devices: 15.6 us -> none  [other_h(): return lax.ppermute(block, 'h', [(0, 1), (1, 0)])]
    ppermute x2 -> x0, starting transfers between devices: 9.47 us -> none  [other_h(): return lax.ppermute(block, 'h', [(0, 1), (1, 0)])]
    all_to_all x4, waiting for transfers between devices: 26.3 us -> 34.8 us  [the longest x1 21.5 us: local(): partial = lax.all_to_all(tie(partial, grad), 'l', 0, 0).sum(0)]
    ppermute x4, waiting for transfers between devices: 38.3 us -> 46.5 us  [across(): return lax.ppermute(block, ('h', 'm'), pairs)]
    all_to_all x1, waiting for transfers between devices: 3.08 us -> 8.17 us  [local(): signals = lax.all_to_all(sent, CTX, 0, 0)]
    all_to_all x1, waiting for transfers between devices: 26.5 us -> 22.4 us  [local(): lax.all_to_all(jnp.broadcast_to(cot_pair[None], (4,) + cot_pair.shape), '...]
    dot_general x2 -> x4, local copies, waits for them, and re-layouts: 4.77 us -> 5.97 us  [product_of(): lax.dot_general(left, right, (((left_dim,), (right_dim,)), ((), ())), pre...]
    unnamed x56 -> x50, local copies, waits for them, and re-layouts: 7.58 us -> 8.73 us
  transfers between devices with their start and end apart: 17 -> 15, of which waited for: 10 -> 8; matrix products, arithmetic and copies ran while one was open for 14% -> 14% of each run, Pallas kernels for 0% -> 0%
where the time goes in v6:
time: 281 us; the launch traced here: 280 us
  waiting for transfers between devices  113 us (40%)
  starting transfers between devices  92.2 us (33%)
  local copies, waits for them, and re-layouts  31 us (11%)
  between operations  19 us (7%)
  matrix products  14.2 us (5%)
  other arithmetic  10 us (4%)
    ppermute x4, waiting for transfers between devices, across(): return lax.ppermute(block, ('h', 'm'), pairs)  46.5 us
    ppermute x4, starting transfers between devices, across(): return lax.ppermute(block, ('h', 'm'), pairs)  28.1 us
    all_to_all x1, waiting for transfers between devices, local(): lax.all_to_all(jnp.broadcast_to(cot_pair[None], (4,) + cot_pair.shape), '...  22.4 us
    all_to_all x1, waiting for transfers between devices, local(): partial = lax.all_to_all(tie(partial, grad), 'l', 0, 0).sum(0)  21.5 us
    all_to_all x1, starting transfers between devices, local(): signals = lax.all_to_all(sent, CTX, 0, 0)  15.5 us
    ppermute x2, starting transfers between devices, other_core(): return lax.ppermute(block, 'k', [(0, 1), (1, 0)])  14.2 us
    all_to_all x1, waiting for transfers between devices, local(): grad = lax.all_to_all(tie(mixed_grad, mixed), CTX, 0, 0)  11.2 us
    dot_general x3, matrix products, product_of(): lax.dot_general(left, right, (((left_dim,), (right_dim,)), ((), ())), pre...  9.24 us
  transfers between devices with their start and end apart: 15, of which 8 were waited for; matrix products, arithmetic and copies ran while one was open for 14% of the time, Pallas kernels for 0%

profile of v6, /device:TPU:129, one launch (start us, length us, event | category | flops | bytes accessed | tf_op | source)
XLA Modules:
  0.0 279.7 jit_solution(18182279129955491557)
XLA Ops:
  7.2 1.0 copy.61
  8.2 1.0 copy.62
  9.2 1.0 copy.64
  10.2 1.0 copy.63
  11.3 0.8 pad_maximum_fusion.3
  12.1 15.5 %all-to-all-start = ((f32[32,24,128]{2,1,0:T(8,128)}), f32[32,24,128]{2,1,0:T(8,128)S(1)}, u32[]{:S(2)}, u32[]{:S(2)}) async-start(f32[32,24,128]{2,1,0:T(8,128)} %pad_maximum_fusion.3), calls=%async_computation | async-start | bytes 786432 | tf_op jit(solution)/shard_map/all_to_all | solution.py:115
  28.3 11.9 %collective-permute-start.1 = (f32[128,256]{1,0:T(8,128)S(1)}, f32[128,256]{1,0:T(8,128)S(1)}, u32[]{:S(2)}, u32[]{:S(2)}) collective-permute-start(f32[128,256]{1,0:T(8,128)S(1)} %copy-done.19), channel_id=1, source_target_pairs={{0,8},{8,264},{256,0},{264,256},{1,9},{9,265},{257,1},{265,257},{2... | collective-permute-start | bytes 393224 | tf_op jit(solution)/shard_map/ppermute | solution.py:70
  40.2 1.9 collective-permute-start
  42.1 8.2 %all-to-all-done = f32[32,24,128]{2,1,0:T(8,128)S(1)} async-done(((f32[32,24,128]{2,1,0:T(8,128)}), f32[32,24,128]{2,1,0:T(8,128)S(1)}, u32[]{:S(2)}, u32[]{:S(2)}) %all-to-all-start) | async-done | bytes 393248 | tf_op jit(solution)/shard_map/all_to_all | solution.py:115
  51.5 14.2 %collective-permute-done = f32[128,256]{1,0:T(8,128)S(1)} collective-permute-done((f32[128,256]{1,0:T(8,128)S(1)}, f32[128,256]{1,0:T(8,128)S(1)}, u32[]{:S(2)}, u32[]{:S(2)}) %collective-permute-start) | collective-permute-done | bytes 131104 | tf_op jit(solution)/shard_map/ppermute | solution.py:70
  65.7 1.1 broadcast_in_dim.6
  66.8 6.1 %all-to-all-start.1 = ((f32[4,2,128,256]{3,2,1,0:T(8,128)}), f32[4,2,128,256]{3,2,1,0:T(8,128)S(1)}, u32[]{:S(2)}, u32[]{:S(2)}) async-start(f32[4,2,128,256]{3,2,1,0:T(8,128)} %broadcast_in_dim.6), calls=%async_computation.1 | async-start | bytes 2097152 | tf_op jit(solution)/shard_map/all_to_all | solution.py:119
  74.5 0.8 fusion.35
  75.8 22.4 %all-to-all-done.1 = f32[4,2,128,256]{3,2,1,0:T(8,128)S(1)} async-done(((f32[4,2,128,256]{3,2,1,0:T(8,128)}), f32[4,2,128,256]{3,2,1,0:T(8,128)S(1)}, u32[]{:S(2)}, u32[]{:S(2)}) %all-to-all-start.1) | async-done | bytes 1048608 | tf_op jit(solution)/shard_map/all_to_all | solution.py:119
  98.2 3.3 %collective-permute-start.2 = (f32[4,2,128,256]{3,2,1,0:T(8,128)S(1)}, f32[4,2,128,256]{3,2,1,0:T(8,128)}, u32[]{:S(2)}, u32[]{:S(2)}) collective-permute-start(f32[4,2,128,256]{3,2,1,0:T(8,128)S(1)} %all-to-all-done.1), channel_id=1, source_target_pairs={{0,1},{1,0},{2,3},{3,2},{4,5},{5,4},{6,7},{7,6},{8,9},{9,8},{10,11... | collective-permute-start | bytes 3145736 | tf_op jit(solution)/shard_map/ppermute | solution.py:74
  101.5 1.2 slice.139
  104.5 1.0 add_add_fusion
  106.3 7.1 %all-to-all-start.2 = ((f32[32,2,8,128]{3,2,1,0:T(8,128)}), f32[32,2,8,128]{3,2,1,0:T(8,128)S(1)}, u32[]{:S(2)}, u32[]{:S(2)}) async-start(f32[32,2,8,128]{3,2,1,0:T(8,128)} %bitcast.17), calls=%async_computation.2 | async-start | bytes 524288 | tf_op jit(solution)/shard_map/all_to_all | solution.py:134
  113.4 2.9 %copy.75 = f32[2048,256]{1,0:T(8,128)} copy(f32[2048,256]{0,1:T(8,128)} %bitcast.118) | data formatting | bytes 4194304 | tf_op jit(solution)/shard_map/dot_general | solution.py:92
  116.3 1.8 fusion
  118.2 3.0 %copy.72 = f32[2,128,4,2,256]{4,3,2,1,0:T(2,128)} copy(f32[2,128,4,2,256]{4,1,0,2,3:T(8,128)S(1)} %fusion) | data formatting | bytes 4194304 | tf_op jit(solution)/shard_map/transpose | solution.py:121
  121.2 2.9 %reshape.120 = f32[256,2048]{1,0:T(8,128)S(1)} reshape(f32[2,128,4,2,256]{4,3,2,1,0:T(2,128)} %copy.72) | data formatting | bytes 4194304 | tf_op jit(solution)/shard_map/reshape | solution.py:121
  124.1 2.6 convolution_bitcast_fusion.1
  128.1 2.1 all-to-all-done.2
  132.1 1.1 copy.74
  133.2 2.6 fusion.39
  135.8 1.3 copy-done
  137.1 1.1 dynamic-slice_bitcast_fusion
  138.3 10.9 %collective-permute-start.3 = (f32[4,2,128,256]{3,2,0,1:T(8,128)}, f32[4,2,128,256]{3,2,0,1:T(8,128)}, u32[]{:S(2)}, u32[]{:S(2)}) collective-permute-start(f32[4,2,128,256]{3,2,0,1:T(8,128)} %dynamic-slice_bitcast_fusion), channel_id=1, source_target_pairs={{0,1},{1,0},{2,3},{3,2},{4,5},{5,4},{6,7},{7,6},{8,9},{9,8},{10,11... | collective-permute-start | bytes 3145736 | tf_op jit(solution)/shard_map/ppermute | solution.py:74
  149.2 0.8 broadcast_add_fusion
  150.0 7.5 %all-to-all-start.3 = ((f32[32,2,8,128]{3,2,1,0:T(8,128)}), f32[32,2,8,128]{3,2,1,0:T(8,128)S(1)}, u32[]{:S(2)}, u32[]{:S(2)}) async-start(f32[32,2,8,128]{3,2,1,0:T(8,128)} %broadcast_add_fusion), calls=%async_computation.3 | async-start | bytes 524288 | tf_op jit(solution)/shard_map/all_to_all | solution.py:139
  157.7 1.9 copy.96
  159.5 4.0 %convolution_bitcast_fusion = f32[16,256,128]{2,1,0:T(8,128)} fusion(f32[16,128,256]{2,1,0:T(8,128)} %bitcast.120, f32[32,2,8,128]{3,2,1,0:T(8,128)S(1)} %broadcast_add_fusion.1), kind=kOutput, calls=%fused_computation.2 | convolution fusion | flops 805306368 | bytes 4456448 | tf_op jit(solution)/shard_map/dot_general | solution.py:92
  163.5 11.2 %all-to-all-done.3 = f32[32,2,8,128]{3,2,1,0:T(8,128)S(1)} async-done(((f32[32,2,8,128]{3,2,1,0:T(8,128)}), f32[32,2,8,128]{3,2,1,0:T(8,128)S(1)}, u32[]{:S(2)}, u32[]{:S(2)}) %all-to-all-start.3) | async-done | bytes 262176 | tf_op jit(solution)/shard_map/all_to_all | solution.py:139
  176.0 1.4 fusion.1
  177.4 1.1 copy.78
  178.5 9.1 %all-to-all-start.4 = ((f32[4,2,128,256]{3,2,1,0:T(8,128)}), f32[4,2,128,256]{3,2,1,0:T(8,128)S(1)}, u32[]{:S(2)}, u32[]{:S(2)}) async-start(f32[4,2,128,256]{3,2,1,0:T(8,128)} %copy.78), calls=%async_computation.4 | async-start | bytes 2097152 | tf_op jit(solution)/shard_map/all_to_all | solution.py:152
  189.8 0.9 fusion.2
  191.3 21.5 %all-to-all-done.4 = f32[4,2,128,256]{3,2,1,0:T(8,128)S(1)} async-done(((f32[4,2,128,256]{3,2,1,0:T(8,128)}), f32[4,2,128,256]{3,2,1,0:T(8,128)S(1)}, u32[]{:S(2)}, u32[]{:S(2)}) %all-to-all-start.4) | async-done | bytes 1048608 | tf_op jit(solution)/shard_map/all_to_all | solution.py:152
  214.2 1.0 copy.85
  215.3 4.4 %all-to-all-start.5 = ((f32[32,25,128]{2,1,0:T(8,128)}), f32[32,25,128]{2,1,0:T(8,128)S(1)}, u32[]{:S(2)}, u32[]{:S(2)}) async-start(f32[32,25,128]{2,1,0:T(8,128)} %copy.85), calls=%async_computation.5 | async-start | bytes 1048576 | tf_op jit(solution)/shard_map/all_to_all | solution.py:168
  220.4 7.5 %collective-permute-start.5 = (f32[128,256]{1,0:T(8,128)S(1)}, f32[128,256]{1,0:T(8,128)S(1)}, u32[]{:S(2)}, u32[]{:S(2)}) collective-permute-start(f32[128,256]{1,0:T(8,128)S(1)} %get-tuple-element.51), channel_id=1, source_target_pairs={{0,256},{8,0},{256,264},{264,8},{1,257},{9,1},{257,265},{265,9},{2... | collective-permute-start | bytes 393224 | tf_op jit(solution)/shard_map/ppermute | solution.py:70
  228.0 6.8 %collective-permute-start.4 = (f32[128,256]{1,0:T(8,128)S(1)}, f32[128,256]{1,0:T(8,128)S(1)}, u32[]{:S(2)}, u32[]{:S(2)}) collective-permute-start(f32[128,256]{1,0:T(8,128)S(1)} %get-tuple-element.52), channel_id=1, source_target_pairs={{0,0},{8,256},{256,8},{264,264},{1,1},{9,257},{257,9},{265,265},{2... | collective-permute-start | bytes 393224 | tf_op jit(solution)/shard_map/ppermute | solution.py:70
  234.8 18.2 %collective-permute-done.5 = f32[128,256]{1,0:T(8,128)S(1)} collective-permute-done((f32[128,256]{1,0:T(8,128)S(1)}, f32[128,256]{1,0:T(8,128)S(1)}, u32[]{:S(2)}, u32[]{:S(2)}) %collective-permute-start.5) | collective-permute-done | bytes 131104 | tf_op jit(solution)/shard_map/ppermute | solution.py:70
  253.0 14.1 %collective-permute-done.4 = f32[128,256]{1,0:T(8,128)S(1)} collective-permute-done((f32[128,256]{1,0:T(8,128)S(1)}, f32[128,256]{1,0:T(8,128)S(1)}, u32[]{:S(2)}, u32[]{:S(2)}) %collective-permute-start.4) | collective-permute-done | bytes 131104 | tf_op jit(solution)/shard_map/ppermute | solution.py:70
  267.8 1.6 multiply_bitcast_fusion
  269.4 0.8 copy.90
  270.9 0.8 copy.92
  (103 shorter events, 14.5 us)
Async XLA Ops:
  7.2 21.1 %copy-start.19 = (f32[128,256]{1,0:T(8,128)S(1)}, f32[128,256]{1,0:T(8,128)}, u32[]{:S(2)}) copy-start(f32[128,256]{1,0:T(8,128)} %param.19) | copy-start | bytes 393220
  12.1 38.2 %all-to-all-start = ((f32[32,24,128]{2,1,0:T(8,128)}), f32[32,24,128]{2,1,0:T(8,128)S(1)}, u32[]{:S(2)}, u32[]{:S(2)}) async-start(f32[32,24,128]{2,1,0:T(8,128)} %pad_maximum_fusion.3), calls=%async_computation | async-start | bytes 786432 | tf_op jit(solution)/shard_map/all_to_all | solution.py:115
  27.5 45.3 %copy-start.20 = (f32[256]{0:T(256)S(1)}, f32[256]{0:T(256)}, u32[]{:S(2)}) copy-start(f32[256]{0:T(256)} %param.17) | copy-start | bytes 3076
  27.6 73.9 %all-gather.2.cloned.1.call-start = ((), (), s32[]{:S(2)}) async-start(), calls=%async_computation.8 | async-start | bytes 2228224 | tf_op jit(solution)/shard_map/all_gather | solution.py:107
  28.3 23.1 %collective-permute-start.1 = (f32[128,256]{1,0:T(8,128)S(1)}, f32[128,256]{1,0:T(8,128)S(1)}, u32[]{:S(2)}, u32[]{:S(2)}) collective-permute-start(f32[128,256]{1,0:T(8,128)S(1)} %copy-done.19), channel_id=1, source_target_pairs={{0,8},{8,264},{256,0},{264,256},{1,9},{9,265},{257,1},{265,257},{2... | collective-permute-start | bytes 393224 | tf_op jit(solution)/shard_map/ppermute | solution.py:70
  40.2 25.5 %collective-permute-start = (f32[128,256]{1,0:T(8,128)S(1)}, f32[128,256]{1,0:T(8,128)S(1)}, u32[]{:S(2)}, u32[]{:S(2)}) collective-permute-start(f32[128,256]{1,0:T(8,128)S(1)} %copy-done.19), channel_id=1, source_target_pairs={{0,0},{8,256},{256,8},{264,264},{1,1},{9,257},{257,9},{265,265},{2... | collective-permute-start | bytes 393224 | tf_op jit(solution)/shard_map/ppermute | solution.py:70
  65.7 7.3 %copy-start.17 = (f32[66,32,1]{0,1,2:T(8,128)S(1)}, f32[66,32,1]{0,1,2:T(8,128)}, u32[]{:S(2)}) copy-start(f32[66,32,1]{0,1,2:T(8,128)} %constant.88) | copy-start | bytes 25348
  65.7 7.9 %copy-start.11 = (f32[33,128]{1,0:T(8,128)S(1)}, f32[33,128]{1,0:T(8,128)}, u32[]{:S(2)}) copy-start(f32[33,128]{1,0:T(8,128)} %constant.81.clone) | copy-start | bytes 50692
  65.7 7.9 %copy-start.13 = (f32[33,128]{1,0:T(8,128)S(1)}, f32[33,128]{1,0:T(8,128)}, u32[]{:S(2)}) copy-start(f32[33,128]{1,0:T(8,128)} %constant.80.clone) | copy-start | bytes 50692
  66.8 31.4 %all-to-all-start.1 = ((f32[4,2,128,256]{3,2,1,0:T(8,128)}), f32[4,2,128,256]{3,2,1,0:T(8,128)S(1)}, u32[]{:S(2)}, u32[]{:S(2)}) async-start(f32[4,2,128,256]{3,2,1,0:T(8,128)} %broadcast_in_dim.6), calls=%async_computation.1 | async-start | bytes 2097152 | tf_op jit(solution)/shard_map/all_to_all | solution.py:119
  72.8 1.0 copy-start.4
  73.7 1.6 copy-start.2
  74.5 30.0 %copy-start.15 = (f32[32,66,1]{1,0,2:T(8,128)S(1)}, f32[32,66,1]{1,0,2:T(8,128)}, u32[]{:S(2)}) copy-start(f32[32,66,1]{1,0,2:T(8,128)} %constant.87) | copy-start | bytes 25348
  98.2 18.2 %collective-permute-start.2 = (f32[4,2,128,256]{3,2,1,0:T(8,128)S(1)}, f32[4,2,128,256]{3,2,1,0:T(8,128)}, u32[]{:S(2)}, u32[]{:S(2)}) collective-permute-start(f32[4,2,128,256]{3,2,1,0:T(8,128)S(1)} %all-to-all-done.1), channel_id=1, source_target_pairs={{0,1},{1,0},{2,3},{3,2},{4,5},{5,4},{6,7},{7,6},{8,9},{9,8},{10,11... | collective-permute-start | bytes 3145736 | tf_op jit(solution)/shard_map/ppermute | solution.py:74
  106.3 23.8 %all-to-all-start.2 = ((f32[32,2,8,128]{3,2,1,0:T(8,128)}), f32[32,2,8,128]{3,2,1,0:T(8,128)S(1)}, u32[]{:S(2)}, u32[]{:S(2)}) async-start(f32[32,2,8,128]{3,2,1,0:T(8,128)} %bitcast.17), calls=%async_computation.2 | async-start | bytes 524288 | tf_op jit(solution)/shard_map/all_to_all | solution.py:134
  135.8 1.3 copy-start
  138.3 37.7 %collective-permute-start.3 = (f32[4,2,128,256]{3,2,0,1:T(8,128)}, f32[4,2,128,256]{3,2,0,1:T(8,128)}, u32[]{:S(2)}, u32[]{:S(2)}) collective-permute-start(f32[4,2,128,256]{3,2,0,1:T(8,128)} %dynamic-slice_bitcast_fusion), channel_id=1, source_target_pairs={{0,1},{1,0},{2,3},{3,2},{4,5},{5,4},{6,7},{7,6},{8,9},{9,8},{10,11... | collective-permute-start | bytes 3145736 | tf_op jit(solution)/shard_map/ppermute | solution.py:74
  150.0 24.7 %all-to-all-start.3 = ((f32[32,2,8,128]{3,2,1,0:T(8,128)}), f32[32,2,8,128]{3,2,1,0:T(8,128)S(1)}, u32[]{:S(2)}, u32[]{:S(2)}) async-start(f32[32,2,8,128]{3,2,1,0:T(8,128)} %broadcast_add_fusion), calls=%async_computation.3 | async-start | bytes 524288 | tf_op jit(solution)/shard_map/all_to_all | solution.py:139
  157.4 62.3 %reduce-scatter.3.cloned.1.call-start = ((), (), s32[]{:S(2)}) async-start(), calls=%async_computation.9 | async-start | bytes 2621440 | tf_op jit(solution)/shard_map/reduce_scatter | solution.py:146
  163.5 12.5 %copy-start.1 = (f32[2,128,4,2,256]{4,1,3,2,0:T(8,128)S(1)}, f32[2,128,4,2,256]{4,1,3,2,0:T(8,128)}, u32[]{:S(2)}) copy-start(f32[2,128,4,2,256]{4,1,3,2,0:T(8,128)} %copy-done) | copy-start | bytes 6291460
  177.3 10.3 %copy-start.10 = (f32[32,8,128]{2,0,1:T(8,128)S(1)}, f32[32,8,128]{2,0,1:T(8,128)}, u32[]{:S(2)}) copy-start(f32[32,8,128]{2,0,1:T(8,128)} %get-tuple-element.55) | copy-start | bytes 393220
  177.4 11.0 %copy-start.18 = (f32[66,32,1]{0,1,2:T(8,128)S(1)}, f32[66,32,1]{0,1,2:T(8,128)}, u32[]{:S(2)}) copy-start(f32[66,32,1]{0,1,2:T(8,128)} %constant.88) | copy-start | bytes 25348
  178.5 10.4 %copy-start.12 = (f32[33,128]{1,0:T(8,128)S(1)}, f32[33,128]{1,0:T(8,128)}, u32[]{:S(2)}) copy-start(f32[33,128]{1,0:T(8,128)} %constant.81.clone) | copy-start | bytes 50692
  178.5 10.4 %copy-start.14 = (f32[33,128]{1,0:T(8,128)S(1)}, f32[33,128]{1,0:T(8,128)}, u32[]{:S(2)}) copy-start(f32[33,128]{1,0:T(8,128)} %constant.80.clone) | copy-start | bytes 50692
  178.5 10.5 %copy-start.5 = (f32[256,256,1]{1,0,2:T(8,128)S(1)}, f32[256,256,1]{1,0,2:T(8,128)}, u32[]{:S(2)}) copy-start(f32[256,256,1]{1,0,2:T(8,128)} %constant.89) | copy-start | bytes 786436
  178.5 34.3 %all-to-all-start.4 = ((f32[4,2,128,256]{3,2,1,0:T(8,128)}), f32[4,2,128,256]{3,2,1,0:T(8,128)S(1)}, u32[]{:S(2)}, u32[]{:S(2)}) async-start(f32[4,2,128,256]{3,2,1,0:T(8,128)} %copy.78), calls=%async_computation.4 | async-start | bytes 2097152 | tf_op jit(solution)/shard_map/all_to_all | solution.py:152
  187.6 1.8 copy-start.6
  187.6 1.8 copy-start.7
  187.6 1.8 copy-start.8
  188.8 1.0 copy-start.3
  189.5 1.4 copy-start.16
  190.7 23.4 %copy-start.9 = (f32[32,8,128]{2,0,1:T(8,128)S(1)}, f32[32,8,128]{2,0,1:T(8,128)}, u32[]{:S(2)}) copy-start(f32[32,8,128]{2,0,1:T(8,128)} %get-tuple-element.53) | copy-start | bytes 393220
  215.3 54.1 %all-to-all-start.5 = ((f32[32,25,128]{2,1,0:T(8,128)}), f32[32,25,128]{2,1,0:T(8,128)S(1)}, u32[]{:S(2)}, u32[]{:S(2)}) async-start(f32[32,25,128]{2,1,0:T(8,128)} %copy.85), calls=%async_computation.5 | async-start | bytes 1048576 | tf_op jit(solution)/shard_map/all_to_all | solution.py:168
  219.7 48.1 %reduce-scatter.5.cloned.1.call-start = ((), (), s32[]{:S(2)}) async-start(), calls=%async_computation.10 | async-start | bytes 655360 | tf_op jit(solution)/shard_map/reduce_scatter | solution.py:147
  220.4 32.6 %collective-permute-start.5 = (f32[128,256]{1,0:T(8,128)S(1)}, f32[128,256]{1,0:T(8,128)S(1)}, u32[]{:S(2)}, u32[]{:S(2)}) collective-permute-start(f32[128,256]{1,0:T(8,128)S(1)} %get-tuple-element.51), channel_id=1, source_target_pairs={{0,256},{8,0},{256,264},{264,8},{1,257},{9,1},{257,265},{265,9},{2... | collective-permute-start | bytes 393224 | tf_op jit(solution)/shard_map/ppermute | solution.py:70
  228.0 39.1 %collective-permute-start.4 = (f32[128,256]{1,0:T(8,128)S(1)}, f32[128,256]{1,0:T(8,128)S(1)}, u32[]{:S(2)}, u32[]{:S(2)}) collective-permute-start(f32[128,256]{1,0:T(8,128)S(1)} %get-tuple-element.52), channel_id=1, source_target_pairs={{0,0},{8,256},{256,8},{264,264},{1,1},{9,257},{257,9},{265,265},{2... | collective-permute-start | bytes 393224 | tf_op jit(solution)/shard_map/ppermute | solution.py:70
Sparse Core Ops, SparseCore 0:
  31.4 66.6 all-gather.1
  163.6 42.7 reduce-scatter.2
  223.6 35.1 reduce-scatter.4

commit v7 on v6

--- a/solution.py
+++ b/solution.py
@@ -104,7 +104,7 @@
     at_m, at_k = (lax.axis_index(name) for name in ("m", "k"))
     at_ctx = lax.axis_index(CTX)
 
-    weights = lax.all_gather(out_weight, PLANE, axis=1, tiled=True)
+    weights = lax.all_to_all(jnp.broadcast_to(out_weight[None], (16,) + out_weight.shape), PLANE, 0, 0)
 
     cot_same = across(cotangent, lambda h, m: (m, h))
     cot_swap = across(cotangent, lambda h, m: (m, 1 - h))
@@ -112,7 +112,8 @@
 
     sent = [key_branch * value_branch, long_filter * norm_scale, query_branch]
     sent = jnp.concatenate([array.T.reshape(n_ctx, group, rows) for array in sent], 1)
-    signals = lax.all_to_all(sent, CTX, 0, 0)
+    signals = lax.all_to_all(tie(sent, weights, cot_same, cot_swap), CTX, 0, 0)
+    weights = weights.transpose(1, 0, 2).reshape(chans, -1)
     product, query = signals[:, :group], signals[:, 2 * group :]
 
     cot_pair = tie(cot_pair, signals)
@@ -128,10 +129,9 @@
     )
     skip = lax.dynamic_slice(skip_weight, (at_ctx * group,), (group,))[None, :, None]
     gate = conv + skip * product
-    mixed = tie(gate * query, cot_line, weights)
-    mixed = mixed.reshape(2, 16, group, rows).transpose(1, 0, 2, 3)
+    mixed = (gate * query).reshape(2, 16, group, rows).transpose(1, 0, 2, 3)
     mixed = jnp.broadcast_to(mixed[None], (2,) + mixed.shape).reshape(n_ctx, 2, group, rows)
-    mixed = lax.all_to_all(mixed, CTX, 0, 0)
+    mixed = lax.all_to_all(tie(mixed, cot_line), CTX, 0, 0)
 
     mixed_grad = product_of(weights, cot_full, 1, 1)
     mixed_grad = mixed_grad.reshape(n_ctx, group, 2, rows).transpose(0, 2, 1, 3)
@@ -143,13 +143,15 @@
 
     weight_part = product_of(mixed, cot_full, 1, 0)
     weight_part = weight_part.reshape(chans, 16, rows).transpose(1, 0, 2)
-    weight_grad = lax.psum_scatter(weight_part, "y", scatter_dimension=0, tiled=True)
-    weight_grad = lax.psum_scatter(weight_grad, "x", scatter_dimension=0, tiled=False) * norm_scale
+    weight_part = lax.psum_scatter(weight_part, "y", scatter_dimension=0, tiled=True)
+    weight_grad = lax.psum_scatter(weight_part, "x", scatter_dimension=0, tiled=False) * norm_scale
 
     partial = product_of(mixed, weights, 0, 0)
     partial = partial.reshape(2, rows, 4, 2, chans).transpose(3, 2, 0, 1, 4)
-    partial = pick(partial, at_k) + other_core(pick(partial, 1 - at_k))
+    partial_far = pick(partial, 1 - at_k)
+    partial = pick(partial, at_k) + jnp.stack([other_core(partial_far[at]) for at in range(4)])
     partial = lax.all_to_all(tie(partial, grad), "l", 0, 0).sum(0)
+    partial = tie(partial, weight_part)
     projected = across(pick(partial, at_m), lambda h, m: (m, h))
     projected = projected + across(pick(partial, 1 - at_m), lambda h, m: (1 - m, h))
 
@@ -163,7 +165,7 @@
     )
     prod_grad = tie(lagged[:, :group] + skip * pre_grad, partial)
     skip_part = jnp.sum(pre_grad * product, axis=(0, 2)) * norm_scale
-    skip_row = jnp.broadcast_to(jnp.pad(skip_part, (0, rows - group))[None, None], (n_ctx, 1, rows))
+    skip_row = jnp.broadcast_to(jnp.pad(skip_part, (0, rows - group))[None, None], (n_ctx, group, rows))
     back = [prod_grad, lagged[:, group:] * norm_scale, grad * gate, skip_row]
     back = lax.all_to_all(jnp.concatenate(back, 1), CTX, 0, 0)
     product_grad, filter_grad, query_grad = (

time: 281 us -> 299 us (1.064)
  waiting for transfers between devices: 113 us -> 128 us
  starting transfers between devices: 92.2 us -> 95.7 us
    all_to_all x2 -> x3, waiting for transfers between devices: 10.3 us -> 34 us  [the longest x1 21.6 us: local(): signals = lax.all_to_all(tie(sent, weights, cot_same, cot_swap), CTX, 0, 0)]
    all_to_all x1, starting transfers between devices: 4.4 us -> 12.7 us  [local(): back = lax.all_to_all(jnp.concatenate(back, 1), CTX, 0, 0)]
    all_to_all x1, waiting for transfers between devices: 11.2 us -> 4.87 us  [local(): grad = lax.all_to_all(tie(mixed_grad, mixed), CTX, 0, 0)]
    all_to_all x1, starting transfers between devices: 9.13 us -> 3.66 us  [local(): partial = lax.all_to_all(tie(partial, grad), 'l', 0, 0).sum(0)]
    unnamed x50 -> x72, local copies, waits for them, and re-layouts: 8.73 us -> 3.88 us
    all_to_all x1, starting transfers between devices: 6.06 us -> 10.4 us  [local(): lax.all_to_all(jnp.broadcast_to(cot_pair[None], (4,) + cot_pair.shape), '...]
    ppermute x4, starting transfers between devices: 28.1 us -> 24 us  [across(): return lax.ppermute(block, ('h', 'm'), pairs)]
    all_to_all x2 -> x3, starting transfers between devices: 22.6 us -> 24.8 us  [the longest x1 13 us: local(): signals = lax.all_to_all(tie(sent, weights, cot_same, cot_swap), CTX, 0, 0)]
  transfers between devices with their start and end apart: 15 -> 18, of which waited for: 8 -> 9; matrix products, arithmetic and copies ran while one was open for 14% -> 13% of each run, Pallas kernels for 0% -> 0%
where the time goes in v7:
time: 299 us; the launch traced here: 298 us
  waiting for transfers between devices  128 us (43%)
  starting transfers between devices  95.7 us (32%)
  local copies, waits for them, and re-layouts  30 us (10%)
  between operations  21.5 us (7%)
  matrix products  12 us (4%)
  other arithmetic  10.4 us (3%)
    ppermute x4, waiting for transfers between devices, across(): return lax.ppermute(block, ('h', 'm'), pairs)  45.6 us
    ppermute x4, starting transfers between devices, across(): return lax.ppermute(block, ('h', 'm'), pairs)  24 us
    all_to_all x1, waiting for transfers between devices, local(): partial = lax.all_to_all(tie(partial, grad), 'l', 0, 0).sum(0)  22 us
    all_to_all x1, waiting for transfers between devices, local(): signals = lax.all_to_all(tie(sent, weights, cot_same, cot_swap), CTX, 0, 0)  21.6 us
    all_to_all x1, waiting for transfers between devices, local(): lax.all_to_all(jnp.broadcast_to(cot_pair[None], (4,) + cot_pair.shape), '...  20.7 us
    all_to_all x1, starting transfers between devices, local(): signals = lax.all_to_all(tie(sent, weights, cot_same, cot_swap), CTX, 0, 0)  13 us
    all_to_all x1, starting transfers between devices, local(): back = lax.all_to_all(jnp.concatenate(back, 1), CTX, 0, 0)  12.7 us
    ppermute x5, starting transfers between devices, other_core(): return lax.ppermute(block, 'k', [(0, 1), (1, 0)])  12.3 us
  transfers between devices with their start and end apart: 18, of which 9 were waited for; matrix products, arithmetic and copies ran while one was open for 13% of the time, Pallas kernels for 0%

profile of v7, /device:TPU:129, one launch (start us, length us, event | category | flops | bytes accessed | tf_op | source)
XLA Modules:
  0.0 297.6 jit_solution(1844351261715586488)
XLA Ops:
  7.2 2.5 broadcast_in_dim.8
  9.6 6.9 %all-to-all-start = ((f32[16,256,128]{2,1,0:T(8,128)}), f32[16,256,128]{2,1,0:T(8,128)S(1)}, u32[]{:S(2)}, u32[]{:S(2)}) async-start(f32[16,256,128]{2,1,0:T(8,128)} %broadcast_in_dim.8), calls=%async_computation | async-start | bytes 4194304 | tf_op jit(solution)/shard_map/all_to_all | solution.py:107
  16.6 10.6 %collective-permute-start.1 = (f32[128,256]{1,0:T(8,128)S(1)}, f32[128,256]{1,0:T(8,128)S(1)}, u32[]{:S(2)}, u32[]{:S(2)}) collective-permute-start(f32[128,256]{1,0:T(8,128)S(1)} %copy-done.30), channel_id=1, source_target_pairs={{0,8},{8,264},{256,0},{264,256},{1,9},{9,265},{257,1},{265,257},{2... | collective-permute-start | bytes 393224 | tf_op jit(solution)/shard_map/ppermute | solution.py:70
  27.2 1.9 collective-permute-start
  29.6 8.4 %collective-permute-done.1 = f32[128,256]{1,0:T(8,128)S(1)} collective-permute-done((f32[128,256]{1,0:T(8,128)S(1)}, f32[128,256]{1,0:T(8,128)S(1)}, u32[]{:S(2)}, u32[]{:S(2)}) %collective-permute-start.1) | collective-permute-done | bytes 131104 | tf_op jit(solution)/shard_map/ppermute | solution.py:70
  39.2 3.2 %collective-permute-done = f32[128,256]{1,0:T(8,128)S(1)} collective-permute-done((f32[128,256]{1,0:T(8,128)S(1)}, f32[128,256]{1,0:T(8,128)S(1)}, u32[]{:S(2)}, u32[]{:S(2)}) %collective-permute-start) | collective-permute-done | bytes 131104 | tf_op jit(solution)/shard_map/ppermute | solution.py:70
  43.6 3.5 %all-to-all-done = f32[16,256,128]{2,1,0:T(8,128)S(1)} async-done(((f32[16,256,128]{2,1,0:T(8,128)}), f32[16,256,128]{2,1,0:T(8,128)S(1)}, u32[]{:S(2)}, u32[]{:S(2)}) %all-to-all-start) | async-done | bytes 2097184 | tf_op jit(solution)/shard_map/all_to_all | solution.py:107
  48.3 0.8 fusion.11
  49.1 13.0 %all-to-all-start.1 = ((f32[32,24,128]{2,1,0:T(8,128)}), f32[32,24,128]{2,1,0:T(8,128)S(1)}, u32[]{:S(2)}, u32[]{:S(2)}) async-start(f32[32,24,128]{2,1,0:T(8,128)} %fusion.11), calls=%async_computation.1 | async-start | bytes 786432 | tf_op jit(solution)/shard_map/all_to_all | solution.py:115
  62.1 21.6 %all-to-all-done.1 = f32[32,24,128]{2,1,0:T(8,128)S(1)} async-done(((f32[32,24,128]{2,1,0:T(8,128)}), f32[32,24,128]{2,1,0:T(8,128)S(1)}, u32[]{:S(2)}, u32[]{:S(2)}) %all-to-all-start.1) | async-done | bytes 393248 | tf_op jit(solution)/shard_map/all_to_all | solution.py:115
  84.9 1.1 broadcast_in_dim.9
  86.0 10.4 %all-to-all-start.2 = ((f32[4,2,128,256]{3,2,1,0:T(8,128)}), f32[4,2,128,256]{3,2,1,0:T(8,128)S(1)}, u32[]{:S(2)}, u32[]{:S(2)}) async-start(f32[4,2,128,256]{3,2,1,0:T(8,128)} %broadcast_in_dim.9), calls=%async_computation.2 | async-start | bytes 2097152 | tf_op jit(solution)/shard_map/all_to_all | solution.py:120
  96.4 0.8 dynamic_slice.17
  97.9 0.8 multiply_add_fusion.1
  99.6 0.9 fusion.37
  100.9 20.7 %all-to-all-done.2 = f32[4,2,128,256]{3,2,1,0:T(8,128)S(1)} async-done(((f32[4,2,128,256]{3,2,1,0:T(8,128)}), f32[4,2,128,256]{3,2,1,0:T(8,128)S(1)}, u32[]{:S(2)}, u32[]{:S(2)}) %all-to-all-start.2) | async-done | bytes 1048608 | tf_op jit(solution)/shard_map/all_to_all | solution.py:120
  121.6 3.4 %collective-permute-start.2 = (f32[4,2,128,256]{3,2,1,0:T(8,128)S(1)}, f32[4,2,128,256]{3,2,1,0:T(8,128)}, u32[]{:S(2)}, u32[]{:S(2)}) collective-permute-start(f32[4,2,128,256]{3,2,1,0:T(8,128)S(1)} %all-to-all-done.2), channel_id=1, source_target_pairs={{0,1},{1,0},{2,3},{3,2},{4,5},{5,4},{6,7},{7,6},{8,9},{9,8},{10,11... | collective-permute-start | bytes 3145736 | tf_op jit(solution)/shard_map/ppermute | solution.py:74
  127.5 4.9 %all-to-all-start.3 = ((f32[32,2,8,128]{3,2,1,0:T(8,128)}), f32[32,2,8,128]{3,2,1,0:T(8,128)S(1)}, u32[]{:S(2)}, u32[]{:S(2)}) async-start(f32[32,2,8,128]{3,2,1,0:T(8,128)} %bitcast.19), calls=%async_computation.3 | async-start | bytes 524288 | tf_op jit(solution)/shard_map/all_to_all | solution.py:134
  132.4 1.9 copy.116
  134.3 1.8 fusion
  136.1 3.0 %copy.115 = f32[2,128,4,2,256]{4,3,2,1,0:T(2,128)} copy(f32[2,128,4,2,256]{4,1,0,2,3:T(8,128)S(1)} %fusion) | data formatting | bytes 4194304 | tf_op jit(solution)/shard_map/transpose | solution.py:122
  139.1 3.9 %reshape.134 = f32[256,2048]{1,0:T(8,128)} reshape(f32[2,128,4,2,256]{4,3,2,1,0:T(2,128)} %copy.115) | data formatting | bytes 4194304 | tf_op jit(solution)/shard_map/reshape | solution.py:122
  143.0 2.7 convolution_bitcast_fusion.1
  146.9 9.0 %all-to-all-done.3 = f32[32,2,8,128]{3,2,1,0:T(8,128)S(1)} async-done(((f32[32,2,8,128]{3,2,1,0:T(8,128)}), f32[32,2,8,128]{3,2,1,0:T(8,128)S(1)}, u32[]{:S(2)}, u32[]{:S(2)}) %all-to-all-start.3) | async-done | bytes 262176 | tf_op jit(solution)/shard_map/all_to_all | solution.py:134
  157.8 7.5 %all-to-all-start.4 = ((f32[32,2,8,128]{3,2,1,0:T(8,128)}), f32[32,2,8,128]{3,2,1,0:T(8,128)S(1)}, u32[]{:S(2)}, u32[]{:S(2)}) async-start(f32[32,2,8,128]{3,2,1,0:T(8,128)} %broadcast_add_fusion), calls=%async_computation.4 | async-start | bytes 524288 | tf_op jit(solution)/shard_map/all_to_all | solution.py:139
  165.6 2.9 copy.141
  168.5 4.0 %convolution_bitcast_fusion = f32[16,256,128]{2,1,0:T(8,128)} fusion(f32[16,128,256]{2,1,0:T(8,128)} %bitcast.145, f32[32,2,8,128]{3,2,1,0:T(8,128)S(1)} %broadcast_add_fusion.1), kind=kOutput, calls=%fused_computation.2 | convolution fusion | flops 805306368 | bytes 4456448 | tf_op jit(solution)/shard_map/dot_general | solution.py:92
  172.7 1.1 fusion.41
  173.9 0.8 slice_bitcast_fusion.3
  174.7 2.7 collective-permute-start.3
  177.5 1.9 collective-permute-start.4
  179.4 2.4 collective-permute-start.5
  181.8 1.9 collective-permute-start.6
  183.8 4.9 %all-to-all-done.4 = f32[32,2,8,128]{3,2,1,0:T(8,128)S(1)} async-done(((f32[32,2,8,128]{3,2,1,0:T(8,128)}), f32[32,2,8,128]{3,2,1,0:T(8,128)S(1)}, u32[]{:S(2)}, u32[]{:S(2)}) %all-to-all-start.4) | async-done | bytes 262176 | tf_op jit(solution)/shard_map/all_to_all | solution.py:139
  189.9 2.1 fusion.1
  192.1 3.7 %all-to-all-start.5 = ((f32[4,2,128,256]{3,2,1,0:T(8,128)}), f32[4,2,128,256]{3,2,1,0:T(8,128)S(1)}, u32[]{:S(2)}, u32[]{:S(2)}) async-start(f32[4,2,128,256]{3,2,1,0:T(8,128)} %fusion.1), calls=%async_computation.5 | async-start | bytes 2097152 | tf_op jit(solution)/shard_map/all_to_all | solution.py:153
  197.5 0.9 fusion.2
  199.0 22.0 %all-to-all-done.5 = f32[4,2,128,256]{3,2,1,0:T(8,128)S(1)} async-done(((f32[4,2,128,256]{3,2,1,0:T(8,128)}), f32[4,2,128,256]{3,2,1,0:T(8,128)S(1)}, u32[]{:S(2)}, u32[]{:S(2)}) %all-to-all-start.5) | async-done | bytes 1048608 | tf_op jit(solution)/shard_map/all_to_all | solution.py:153
  221.1 1.2 slice.181
  224.5 1.1 copy.131
  225.6 12.7 %all-to-all-start.6 = ((f32[32,32,128]{2,1,0:T(8,128)}), f32[32,32,128]{2,1,0:T(8,128)S(1)}, u32[]{:S(2)}, u32[]{:S(2)}) async-start(f32[32,32,128]{2,1,0:T(8,128)} %copy.131), calls=%async_computation.7 | async-start | bytes 1048576 | tf_op jit(solution)/shard_map/all_to_all | solution.py:170
  239.3 9.6 %collective-permute-start.7 = (f32[128,256]{1,0:T(8,128)S(1)}, f32[128,256]{1,0:T(8,128)S(1)}, u32[]{:S(2)}, u32[]{:S(2)}) collective-permute-start(f32[128,256]{1,0:T(8,128)S(1)} %bitcast.157), channel_id=1, source_target_pairs={{0,0},{8,256},{256,8},{264,264},{1,1},{9,257},{257,9},{265,265},{2... | collective-permute-start | bytes 393224 | tf_op jit(solution)/shard_map/ppermute | solution.py:70
  248.9 1.9 collective-permute-start.8
  250.8 33.9 %collective-permute-done.7 = f32[128,256]{1,0:T(8,128)S(1)} collective-permute-done((f32[128,256]{1,0:T(8,128)S(1)}, f32[128,256]{1,0:T(8,128)S(1)}, u32[]{:S(2)}, u32[]{:S(2)}) %collective-permute-start.7) | collective-permute-done | bytes 131104 | tf_op jit(solution)/shard_map/ppermute | solution.py:70
  285.4 1.6 multiply_bitcast_fusion
  287.0 0.8 copy.134
  287.8 0.8 copy.135
  288.5 0.8 copy.136
  (135 shorter events, 15.4 us)
Async XLA Ops:
  9.6 6.9 %copy-start.30 = (f32[128,256]{1,0:T(8,128)S(1)}, f32[128,256]{1,0:T(8,128)}, u32[]{:S(2)}) copy-start(f32[128,256]{1,0:T(8,128)} %param.19) | copy-start | bytes 393220
  9.6 19.5 %copy-start.21 = (f32[128,256]{1,0:T(8,128)S(1)}, f32[128,256]{1,0:T(8,128)}, u32[]{:S(2)}) copy-start(f32[128,256]{1,0:T(8,128)} %param.13) | copy-start | bytes 393220
  9.6 19.6 %copy-start.22 = (f32[128,256]{1,0:T(8,128)S(1)}, f32[128,256]{1,0:T(8,128)}, u32[]{:S(2)}) copy-start(f32[128,256]{1,0:T(8,128)} %param.14) | copy-start | bytes 393220
  9.6 19.7 %copy-start.23 = (f32[128,256]{1,0:T(8,128)S(1)}, f32[128,256]{1,0:T(8,128)}, u32[]{:S(2)}) copy-start(f32[128,256]{1,0:T(8,128)} %param.16) | copy-start | bytes 393220
  9.6 19.8 %copy-start.24 = (f32[128,256]{1,0:T(8,128)S(1)}, f32[128,256]{1,0:T(8,128)}, u32[]{:S(2)}) copy-start(f32[128,256]{1,0:T(8,128)} %param.15) | copy-start | bytes 393220
  9.6 37.4 %all-to-all-start = ((f32[16,256,128]{2,1,0:T(8,128)}), f32[16,256,128]{2,1,0:T(8,128)S(1)}, u32[]{:S(2)}, u32[]{:S(2)}) async-start(f32[16,256,128]{2,1,0:T(8,128)} %broadcast_in_dim.8), calls=%async_computation | async-start | bytes 4194304 | tf_op jit(solution)/shard_map/all_to_all | solution.py:107
  16.6 21.5 %collective-permute-start.1 = (f32[128,256]{1,0:T(8,128)S(1)}, f32[128,256]{1,0:T(8,128)S(1)}, u32[]{:S(2)}, u32[]{:S(2)}) collective-permute-start(f32[128,256]{1,0:T(8,128)S(1)} %copy-done.30), channel_id=1, source_target_pairs={{0,8},{8,264},{256,0},{264,256},{1,9},{9,265},{257,1},{265,257},{2... | collective-permute-start | bytes 393224 | tf_op jit(solution)/shard_map/ppermute | solution.py:70
  27.2 15.2 %collective-permute-start = (f32[128,256]{1,0:T(8,128)S(1)}, f32[128,256]{1,0:T(8,128)S(1)}, u32[]{:S(2)}, u32[]{:S(2)}) collective-permute-start(f32[128,256]{1,0:T(8,128)S(1)} %copy-done.30), channel_id=1, source_target_pairs={{0,0},{8,256},{256,8},{264,264},{1,1},{9,257},{257,9},{265,265},{2... | collective-permute-start | bytes 393224 | tf_op jit(solution)/shard_map/ppermute | solution.py:70
  29.3 56.7 %copy-start.1 = (f32[128,256]{0,1:T(8,128)}, f32[128,256]{0,1:T(8,128)S(1)}, u32[]{:S(2)}) copy-start(f32[128,256]{0,1:T(8,128)S(1)} %copy.103) | copy-start | bytes 393220
  29.4 56.6 %copy-start.3 = (f32[128,256]{0,1:T(8,128)}, f32[128,256]{0,1:T(8,128)S(1)}, u32[]{:S(2)}) copy-start(f32[128,256]{0,1:T(8,128)S(1)} %copy.104) | copy-start | bytes 393220
  47.0 39.0 %copy-start = (f32[16,256,128]{2,1,0:T(8,128)}, f32[16,256,128]{2,1,0:T(8,128)S(1)}, u32[]{:S(2)}) copy-start(f32[16,256,128]{2,1,0:T(8,128)S(1)} %all-to-all-done) | copy-start | bytes 6291460
  49.1 34.6 %all-to-all-start.1 = ((f32[32,24,128]{2,1,0:T(8,128)}), f32[32,24,128]{2,1,0:T(8,128)S(1)}, u32[]{:S(2)}, u32[]{:S(2)}) async-start(f32[32,24,128]{2,1,0:T(8,128)} %fusion.11), calls=%async_computation.1 | async-start | bytes 786432 | tf_op jit(solution)/shard_map/all_to_all | solution.py:115
  84.9 12.3 %copy-start.26 = (f32[66,32,1]{0,1,2:T(8,128)S(1)}, f32[66,32,1]{0,1,2:T(8,128)}, u32[]{:S(2)}) copy-start(f32[66,32,1]{0,1,2:T(8,128)} %constant.91) | copy-start | bytes 25348
  86.0 35.6 %all-to-all-start.2 = ((f32[4,2,128,256]{3,2,1,0:T(8,128)}), f32[4,2,128,256]{3,2,1,0:T(8,128)S(1)}, u32[]{:S(2)}, u32[]{:S(2)}) async-start(f32[4,2,128,256]{3,2,1,0:T(8,128)} %broadcast_in_dim.9), calls=%async_computation.2 | async-start | bytes 2097152 | tf_op jit(solution)/shard_map/all_to_all | solution.py:120
  96.4 2.4 copy-start.11
  97.2 29.1 %copy-start.28 = (f32[8]{0:T(128)}, f32[8]{0:T(128)S(1)}, u32[]{:S(2)}) copy-start(f32[8]{0:T(128)S(1)} %dynamic_slice.17) | copy-start | bytes 100
  98.8 1.7 copy-start.9
  98.8 2.1 copy-start.17
  98.8 2.1 copy-start.19
  99.6 26.7 %copy-start.25 = (f32[32,66,1]{1,0,2:T(8,128)S(1)}, f32[32,66,1]{1,0,2:T(8,128)}, u32[]{:S(2)}) copy-start(f32[32,66,1]{1,0,2:T(8,128)} %constant.90) | copy-start | bytes 25348
  121.6 12.7 %collective-permute-start.2 = (f32[4,2,128,256]{3,2,1,0:T(8,128)S(1)}, f32[4,2,128,256]{3,2,1,0:T(8,128)}, u32[]{:S(2)}, u32[]{:S(2)}) collective-permute-start(f32[4,2,128,256]{3,2,1,0:T(8,128)S(1)} %all-to-all-done.2), channel_id=1, source_target_pairs={{0,1},{1,0},{2,3},{3,2},{4,5},{5,4},{6,7},{7,6},{8,9},{9,8},{10,11... | collective-permute-start | bytes 3145736 | tf_op jit(solution)/shard_map/ppermute | solution.py:74
  125.1 1.6 copy-start.5
  125.1 1.6 copy-start.7
  127.5 28.4 %all-to-all-start.3 = ((f32[32,2,8,128]{3,2,1,0:T(8,128)}), f32[32,2,8,128]{3,2,1,0:T(8,128)S(1)}, u32[]{:S(2)}, u32[]{:S(2)}) async-start(f32[32,2,8,128]{3,2,1,0:T(8,128)} %bitcast.19), calls=%async_computation.3 | async-start | bytes 524288 | tf_op jit(solution)/shard_map/all_to_all | solution.py:134
  157.8 30.8 %all-to-all-start.4 = ((f32[32,2,8,128]{3,2,1,0:T(8,128)}), f32[32,2,8,128]{3,2,1,0:T(8,128)S(1)}, u32[]{:S(2)}, u32[]{:S(2)}) async-start(f32[32,2,8,128]{3,2,1,0:T(8,128)} %broadcast_add_fusion), calls=%async_computation.4 | async-start | bytes 524288 | tf_op jit(solution)/shard_map/all_to_all | solution.py:139
  165.4 55.7 %reduce-scatter.3.cloned.1.call-start = ((), (), s32[]{:S(2)}) async-start(), calls=%async_computation.9 | async-start | bytes 2621440 | tf_op jit(solution)/shard_map/reduce_scatter | solution.py:146
  174.7 15.1 %collective-permute-start.3 = (f32[2,128,256]{2,1,0:T(8,128)}, f32[2,128,256]{2,1,0:T(8,128)S(1)}, u32[]{:S(2)}, u32[]{:S(2)}) collective-permute-start(f32[2,128,256]{2,1,0:T(8,128)} %get-tuple-element.32), channel_id=1, source_target_pairs={{0,1},{1,0},{2,3},{3,2},{4,5},{5,4},{6,7},{7,6},{8,9},{9,8},{10,11... | collective-permute-start | bytes 786440 | tf_op jit(solution)/shard_map/ppermute | solution.py:74
  177.5 12.4 %collective-permute-start.4 = (f32[2,128,256]{2,1,0:T(8,128)S(1)}, f32[2,128,256]{2,1,0:T(8,128)S(1)}, u32[]{:S(2)}, u32[]{:S(2)}) collective-permute-start(f32[2,128,256]{2,1,0:T(8,128)S(1)} %get-tuple-element.33), channel_id=1, source_target_pairs={{0,1},{1,0},{2,3},{3,2},{4,5},{5,4},{6,7},{7,6},{8,9},{9,8},{10,11... | collective-permute-start | bytes 786440 | tf_op jit(solution)/shard_map/ppermute | solution.py:74
  179.4 10.5 %collective-permute-start.5 = (f32[2,128,256]{2,1,0:T(8,128)S(1)}, f32[2,128,256]{2,1,0:T(8,128)S(1)}, u32[]{:S(2)}, u32[]{:S(2)}) collective-permute-start(f32[2,128,256]{2,1,0:T(8,128)S(1)} %get-tuple-element.35), channel_id=1, source_target_pairs={{0,1},{1,0},{2,3},{3,2},{4,5},{5,4},{6,7},{7,6},{8,9},{9,8},{10,11... | collective-permute-start | bytes 786440 | tf_op jit(solution)/shard_map/ppermute | solution.py:74
  181.8 8.1 %collective-permute-start.6 = (f32[2,128,256]{2,1,0:T(8,128)S(1)}, f32[2,128,256]{2,1,0:T(8,128)}, u32[]{:S(2)}, u32[]{:S(2)}) collective-permute-start(f32[2,128,256]{2,1,0:T(8,128)S(1)} %get-tuple-element.34), channel_id=1, source_target_pairs={{0,1},{1,0},{2,3},{3,2},{4,5},{5,4},{6,7},{7,6},{8,9},{9,8},{10,11... | collective-permute-start | bytes 786440 | tf_op jit(solution)/shard_map/ppermute | solution.py:74
  189.9 5.9 %copy-start.6 = (f32[32,8,128]{2,1,0:T(8,128)S(1)}, f32[32,8,128]{2,1,0:T(8,128)}, u32[]{:S(2)}) copy-start(f32[32,8,128]{2,1,0:T(8,128)} %copy-done.5) | copy-start | bytes 393220
  189.9 5.9 %copy-start.8 = (f32[32,8,128]{2,1,0:T(8,128)S(1)}, f32[32,8,128]{2,1,0:T(8,128)}, u32[]{:S(2)}) copy-start(f32[32,8,128]{2,1,0:T(8,128)} %copy-done.7) | copy-start | bytes 393220
  192.1 3.9 %copy-start.27 = (f32[66,32,1]{0,1,2:T(8,128)S(1)}, f32[66,32,1]{0,1,2:T(8,128)}, u32[]{:S(2)}) copy-start(f32[66,32,1]{0,1,2:T(8,128)} %constant.91) | copy-start | bytes 25348
  192.1 4.4 %copy-start.18 = (f32[33,128]{1,0:T(8,128)S(1)}, f32[33,128]{1,0:T(8,128)}, u32[]{:S(2)}) copy-start(f32[33,128]{1,0:T(8,128)} %constant.83.clone) | copy-start | bytes 50692
  192.1 4.4 %copy-start.20 = (f32[33,128]{1,0:T(8,128)S(1)}, f32[33,128]{1,0:T(8,128)}, u32[]{:S(2)}) copy-start(f32[33,128]{1,0:T(8,128)} %constant.84.clone) | copy-start | bytes 50692
  192.1 4.5 %copy-start.12 = (f32[256,256,1]{1,0,2:T(8,128)S(1)}, f32[256,256,1]{1,0,2:T(8,128)}, u32[]{:S(2)}) copy-start(f32[256,256,1]{1,0,2:T(8,128)} %constant.92) | copy-start | bytes 786436
  192.1 28.9 %all-to-all-start.5 = ((f32[4,2,128,256]{3,2,1,0:T(8,128)}), f32[4,2,128,256]{3,2,1,0:T(8,128)S(1)}, u32[]{:S(2)}, u32[]{:S(2)}) async-start(f32[4,2,128,256]{3,2,1,0:T(8,128)} %fusion.1), calls=%async_computation.5 | async-start | bytes 2097152 | tf_op jit(solution)/shard_map/all_to_all | solution.py:153
  195.7 1.3 copy-start.13
  195.8 1.3 copy-start.14
  195.8 1.3 copy-start.15
  195.8 1.3 copy-start.16
  198.4 25.8 %copy-start.29 = (f32[8]{0:T(128)S(1)}, f32[8]{0:T(128)}, u32[]{:S(2)}) copy-start(f32[8]{0:T(128)} %copy-done.28) | copy-start | bytes 100
  224.4 62.5 %copy-start.2 = (f32[128,256]{0,1:T(8,128)S(1)}, f32[128,256]{0,1:T(8,128)}, u32[]{:S(2)}) copy-start(f32[128,256]{0,1:T(8,128)} %copy-done.1) | copy-start | bytes 393220
  224.4 62.5 %copy-start.4 = (f32[128,256]{0,1:T(8,128)S(1)}, f32[128,256]{0,1:T(8,128)}, u32[]{:S(2)}) copy-start(f32[128,256]{0,1:T(8,128)} %copy-done.3) | copy-start | bytes 393220
  225.6 61.4 %all-to-all-start.6 = ((f32[32,32,128]{2,1,0:T(8,128)}), f32[32,32,128]{2,1,0:T(8,128)S(1)}, u32[]{:S(2)}, u32[]{:S(2)}) async-start(f32[32,32,128]{2,1,0:T(8,128)} %copy.131), calls=%async_computation.7 | async-start | bytes 1048576 | tf_op jit(solution)/shard_map/all_to_all | solution.py:170
  238.3 47.1 %reduce-scatter.5.cloned.1.call-start = ((), (), s32[]{:S(2)}) async-start(), calls=%async_computation.10 | async-start | bytes 655360 | tf_op jit(solution)/shard_map/reduce_scatter | solution.py:147
  239.3 45.4 %collective-permute-start.7 = (f32[128,256]{1,0:T(8,128)S(1)}, f32[128,256]{1,0:T(8,128)S(1)}, u32[]{:S(2)}, u32[]{:S(2)}) collective-permute-start(f32[128,256]{1,0:T(8,128)S(1)} %bitcast.157), channel_id=1, source_target_pairs={{0,0},{8,256},{256,8},{264,264},{1,1},{9,257},{257,9},{265,265},{2... | collective-permute-start | bytes 393224 | tf_op jit(solution)/shard_map/ppermute | solution.py:70
  248.9 35.8 %collective-permute-start.8 = (f32[128,256]{1,0:T(8,128)S(1)}, f32[128,256]{1,0:T(8,128)S(1)}, u32[]{:S(2)}, u32[]{:S(2)}) collective-permute-start(f32[128,256]{1,0:T(8,128)S(1)} %bitcast.158), channel_id=1, source_target_pairs={{0,256},{8,0},{256,264},{264,8},{1,257},{9,1},{257,265},{265,9},{2... | collective-permute-start | bytes 393224 | tf_op jit(solution)/shard_map/ppermute | solution.py:70
  (1 other events, 1.0 us)
Sparse Core Ops, SparseCore 0:
  172.6 41.4 reduce-scatter.2
  242.2 32.3 reduce-scatter.4

commit v8 on v6

v8 whole, which is shorter than its diff:
```python
import math

import jax
import jax.numpy as jnp
import numpy as np
from jax import lax
from jax.experimental import pallas as pl
from jax.experimental.pallas import tpu as pltpu
from jax.sharding import Mesh
from jax.sharding import PartitionSpec as P

AXES = ("h", "y", "x", "m", "l", "k")
SIZES = (2, 4, 4, 2, 4, 2)
CTX = ("h", "y", "x")
PLANE = ("y", "x")
side = 128
exact = lax.Precision.HIGHEST
ANY = pl.BlockSpec(memory_space=pl.ANY)
VMEM = pl.BlockSpec(memory_space=pltpu.VMEM)


def tables(seq_len):
    full = 2 * seq_len
    blocks = full // side
    kept = blocks // 2 + 1
    rows = np.arange(kept)
    first = 2.0 * np.pi * np.outer(rows, np.arange(seq_len // side)) / blocks
    turn = 2.0 * np.pi * np.outer(rows, np.arange(side)) / full
    inner = 2.0 * np.pi * np.outer(np.arange(side), np.arange(side)) / side
    weight = np.where((rows == 0) | (rows == blocks // 2), 1.0, 2.0)[:, None] / full
    cos, sin = np.cos(inner), np.sin(inner)
    as32 = lambda a: jnp.asarray(a.astype(np.float32))
    return dict(
        first=as32(np.concatenate([np.cos(first), -np.sin(first)], 0)),
        turn_cos=as32(np.cos(turn))[:, None, :],
        turn_sin=as32(np.sin(turn))[:, None, :],
        inner=as32(np.block([[cos, -sin], [sin, cos]])),
        outer=as32(np.block([[cos, sin], [-sin, cos]])),
        last=as32(np.concatenate([weight * np.cos(first), -weight * np.sin(first)], 0).T),
        kept=kept,
    )


def forward_fourier(signal, tab):
    both = jnp.einsum("kn,ncm->kcm", tab["first"], signal, precision=exact)
    real, imag = both[: tab["kept"]], both[tab["kept"] :]
    turned = jnp.concatenate(
        [real * tab["turn_cos"] + imag * tab["turn_sin"], imag * tab["turn_cos"] - real * tab["turn_sin"]], 2
    )
    return jnp.einsum("kcm,mj->kcj", turned, tab["inner"], precision=exact)


def inverse_fourier(real, imag, tab):
    back = jnp.einsum("kcm,mj->kcj", jnp.concatenate([real, imag], 2), tab["outer"], precision=exact)
    real, imag = back[..., :side], back[..., side:]
    turned = jnp.concatenate(
        [real * tab["turn_cos"] - imag * tab["turn_sin"], imag * tab["turn_cos"] + real * tab["turn_sin"]], 0
    )
    return jnp.einsum("nk,kcm->ncm", tab["last"], turned, precision=exact)


def halves(spectrum):
    return spectrum[..., :side], spectrum[..., side:]


def split(array):
    high = array.astype(jnp.bfloat16)
    return high, (array - high.astype(jnp.float32)).astype(jnp.bfloat16)


def dot3(left, right, left_dim, right_dim):
    def one(a, b):
        return lax.dot_general(a, b, (((left_dim,), (right_dim,)), ((), ())), preferred_element_type=jnp.float32)

    return one(left[0], right[0]) + (one(left[0], right[1]) + one(left[1], right[0]))


def params(mib=24):
    return pltpu.CompilerParams(vmem_limit_bytes=mib << 20)


def cost(flops=0, size=0):
    return pl.CostEstimate(flops=flops, bytes_accessed=size, transcendentals=0)


def prepare_kernel(scale, group, key, value, taps, query, *refs):
    out = refs[-1]
    arrays = (key[...] * value[...], taps[...] * scale, query[...])
    for at, array in enumerate(arrays):
        out[:, at * group : (at + 1) * group, :] = array.T.reshape(out.shape[0], group, out.shape[2])


def prepare(key, value, taps, query, first, scale, n_ctx):
    rows, chans = key.shape
    group = chans // n_ctx
    return pl.pallas_call(
        lambda *refs: prepare_kernel(scale, group, *refs),
        out_shape=jax.ShapeDtypeStruct((n_ctx, 3 * group, rows), jnp.float32),
        in_specs=[VMEM] * 4 + [ANY] * len(first),
        out_specs=VMEM,
        compiler_params=params(),
        cost_estimate=cost(0, 1 << 20),
    )(key, value, taps, query, *first)


def double_kernel(mixed, *refs):
    out = refs[-1]
    half = mixed.shape[0] // 2
    for to in range(2):
        for at in range(2):
            out[to * half : (to + 1) * half, at] = mixed[at * half : (at + 1) * half]


def double(mixed, first):
    blocks, group, rows = mixed.shape
    return pl.pallas_call(
        double_kernel,
        out_shape=jax.ShapeDtypeStruct((blocks, 2, group, rows), jnp.float32),
        in_specs=[VMEM] + [ANY] * len(first),
        out_specs=VMEM,
        compiler_params=params(),
        cost_estimate=cost(0, 1 << 18),
    )(mixed, *first)


def gradient_kernel(at_k, near_w, far_w, near, far, out, total):
    step = pl.program_id(0)
    rows = near.shape[2]

    def term(weight, cot):
        flat = cot[...].reshape(2 * rows, cot.shape[3])
        return dot3(split(weight[...]), split(flat), 1, 1)

    both = term(near_w, near) + term(far_w, far)

    @pl.when(step == 0)
    def _():
        total[...] = both

    @pl.when(step > 0)
    def _():
        total[...] += both

    @pl.when(step == pl.num_programs(0) - 1)
    def _():
        for at in range(2):
            out[:, at] = total[:, at * rows : (at + 1) * rows].reshape(out.shape[0], out.shape[2], rows)


def gradient(weights, near, far, at_k, n_ctx):
    lines, _, rows, wide = near.shape
    chans = weights.shape[0]
    block = pl.BlockSpec((1, 2, rows, wide), lambda l, k: (l, 0, 0, 0))
    return pl.pallas_call(
        gradient_kernel,
        out_shape=jax.ShapeDtypeStruct((n_ctx, 2, chans // n_ctx, rows), jnp.float32),
        grid_spec=pltpu.PrefetchScalarGridSpec(
            num_scalar_prefetch=1,
            grid=(lines,),
            in_specs=[
                pl.BlockSpec((chans, wide), lambda l, k: (0, 2 * l + k[0])),
                pl.BlockSpec((chans, wide), lambda l, k: (0, 2 * l + 1 - k[0])),
                block,
                block,
            ],
            out_specs=pl.BlockSpec((n_ctx, 2, chans // n_ctx, rows), lambda l, k: (0, 0, 0, 0)),
            scratch_shapes=[pltpu.VMEM((chans, 2 * rows), jnp.float32)],
        ),
        compiler_params=params(),
        cost_estimate=cost(3 * 2 * chans * 2 * rows * 2 * lines * wide, 5 << 20),
    )(at_k, weights, weights, near, far)


def partial_kernel(at_k, mixed, weight, *refs):
    out, high, low = refs[-3:]
    rows = mixed.shape[3]
    chans = weight.shape[0]

    @pl.when(pl.program_id(0) == 0)
    def _():
        for at in range(2):
            turned = split(mixed[:, at].reshape(chans, rows).T)
            high[at * rows : (at + 1) * rows], low[at * rows : (at + 1) * rows] = turned

    value = dot3((high[...], low[...]), split(weight[...]), 1, 0).reshape(out.shape)
    if len(refs) > 3:
        value = value + refs[0][...]
    out[...] = value


def partial_sums(mixed, weights, at_k, far, more=None, first=()):
    chans = weights.shape[0]
    rows = mixed.shape[3]
    lines = weights.shape[1] // (2 * chans)
    flip = 1 if far else 0
    block = pl.BlockSpec((1, 2, rows, chans), lambda l, k: (l, 0, 0, 0))
    return pl.pallas_call(
        partial_kernel,
        out_shape=jax.ShapeDtypeStruct((lines, 2, rows, chans), jnp.float32),
        grid_spec=pltpu.PrefetchScalarGridSpec(
            num_scalar_prefetch=1,
            grid=(lines,),
            in_specs=[
                pl.BlockSpec(mixed.shape, lambda l, k: (0, 0, 0, 0)),
                pl.BlockSpec((chans, chans), lambda l, k: (0, 2 * l + (k[0] + flip) % 2)),
            ]
            + ([block] if more is not None else [])
            + [ANY] * len(first),
            out_specs=block,
            scratch_shapes=[pltpu.VMEM((2 * rows, chans), jnp.bfloat16)] * 2,
        ),
        compiler_params=params(),
        cost_estimate=cost(3 * 2 * chans * 2 * rows * lines * chans, 3 << 20),
    )(at_k, mixed, weights, *([more] if more is not None else []), *first)


def outer_kernel(at_k, mixed, near, far, out, high, low):
    rows = mixed.shape[3]
    chans = out.shape[1]

    @pl.when(pl.program_id(0) == 0)
    def _():
        for at in range(2):
            turned = split(mixed[:, at].reshape(chans, rows))
            high[:, at * rows : (at + 1) * rows], low[:, at * rows : (at + 1) * rows] = turned

    for cot, core in ((near, at_k[0]), (far, 1 - at_k[0])):
        flat = cot[...].reshape(2 * rows, cot.shape[3])
        value = dot3((high[...], low[...]), split(flat), 1, 0)
        for at in range(2):
            out[2 * core + at] = value[:, at * rows : (at + 1) * rows]


def outer(mixed, near, far, at_k):
    lines, _, rows, wide = near.shape
    chans = mixed.shape[0] * mixed.shape[2]
    block = pl.BlockSpec((1, 2, rows, wide), lambda l, k: (l, 0, 0, 0))
    return pl.pallas_call(
        outer_kernel,
        out_shape=jax.ShapeDtypeStruct((4 * lines, chans, rows), jnp.float32),
        grid_spec=pltpu.PrefetchScalarGridSpec(
            num_scalar_prefetch=1,
            grid=(lines,),
            in_specs=[pl.BlockSpec(mixed.shape, lambda l, k: (0, 0, 0, 0)), block, block],
            out_specs=pl.BlockSpec((4, chans, rows), lambda l, k: (l, 0, 0)),
            scratch_shapes=[pltpu.VMEM((chans, 2 * rows), jnp.bfloat16)] * 2,
        ),
        compiler_params=params(),
        cost_estimate=cost(3 * 2 * chans * 2 * rows * 2 * lines * wide, 5 << 20),
    )(at_k, mixed, near, far)


def returned_kernel(scale, group, lagged, pre_grad, signals, grad, gate, skip, *refs):
    out = refs[-1]
    pre = pre_grad[...]
    out[:, :group] = lagged[:, :group] + skip[...][None] * pre
    out[:, group : 2 * group] = lagged[:, group:] * scale
    out[:, 2 * group : 3 * group] = grad[...] * gate[...]
    skip_grad = jnp.sum(jnp.sum(pre * signals[:, :group], axis=0), axis=1, keepdims=True) * scale
    out[:, 3 * group :] = jnp.broadcast_to(skip_grad[None], out.shape[:1] + (group,) + out.shape[2:])


def returned(lagged, pre_grad, signals, grad, gate, skip, first, scale):
    blocks, group, rows = pre_grad.shape
    return pl.pallas_call(
        lambda *refs: returned_kernel(scale, group, *refs),
        out_shape=jax.ShapeDtypeStruct((blocks, 4 * group, rows), jnp.float32),
        in_specs=[VMEM] * 6 + [ANY] * len(first),
        out_specs=VMEM,
        compiler_params=params(),
        cost_estimate=cost(0, 1 << 20),
    )(lagged, pre_grad, signals, grad, gate, skip, *first)


def finish_kernel(group, back, key, value, key_grad, value_grad, query_grad, filter_grad, skip_grad):
    rows, chans = key.shape

    def turned(at):
        return back[:, at * group : (at + 1) * group, :].reshape(chans, rows).T

    product_grad = turned(0)
    key_grad[...] = product_grad * value[...]
    value_grad[...] = product_grad * key[...]
    filter_grad[...] = turned(1)
    query_grad[...] = turned(2)
    skip_grad[...] = turned(3)[:1]


def finish(back, key, value, group):
    whole = jax.ShapeDtypeStruct(key.shape, jnp.float32)
    return pl.pallas_call(
        lambda *refs: finish_kernel(group, *refs),
        out_shape=[whole] * 4 + [jax.ShapeDtypeStruct((1, key.shape[1]), jnp.float32)],
        in_specs=[VMEM] * 3,
        out_specs=[VMEM] * 5,
        compiler_params=params(),
        cost_estimate=cost(0, 1 << 20),
    )(back, key, value)


def across(block, target):
    pairs = []
    for h in range(2):
        for m in range(2):
            to_h, to_m = target(h, m)
            pairs.append((h * 2 + m, to_h * 2 + to_m))
    return lax.ppermute(block, ("h", "m"), pairs)


def other_core(block):
    return lax.ppermute(block, "k", [(0, 1), (1, 0)])


def in_order(own, other, at):
    return jnp.where(at == 0, jnp.stack([own, other]), jnp.stack([other, own]))


def tie(value, *first):
    for array in first:
        value = value + 0.0 * array[(0,) * array.ndim]
    return value


def pick(pair, at):
    return lax.dynamic_index_in_dim(pair, at, 0, False)


def local(key_branch, value_branch, query_branch, long_filter, skip_weight, out_weight, cotangent):
    rows, chans = key_branch.shape
    n_ctx = 32
    group = chans // n_ctx
    seq_len = rows * n_ctx
    norm_scale = 1.0 / math.sqrt(seq_len)
    tab = tables(seq_len)
    at_m = lax.axis_index("m")
    at_k = lax.axis_index("k").astype(jnp.int32).reshape(1)
    at_ctx = lax.axis_index(CTX)

    weights = lax.all_gather(out_weight, PLANE, axis=1, tiled=True)

    cot_same = across(cotangent, lambda h, m: (m, h))
    cot_swap = across(cotangent, lambda h, m: (m, 1 - h))
    cot_pair = in_order(cot_same, cot_swap, at_m)

    sent = prepare(key_branch, value_branch, long_filter, query_branch, (), norm_scale, n_ctx)
    signals = lax.all_to_all(sent, CTX, 0, 0)
    product, query = signals[:, :group], signals[:, 2 * group :]

    cot_pair = tie(cot_pair, signals)
    near = lax.all_to_all(jnp.broadcast_to(cot_pair[None], (4,) + cot_pair.shape), "l", 0, 0)
    far = other_core(near)

    tab["first"] = tie(tab["first"], weights)
    spectra = forward_fourier(signals[:, : 2 * group], tab)
    prod_real, prod_imag = halves(spectra[:, :group])
    taps_real, taps_imag = halves(spectra[:, group:])
    conv = inverse_fourier(
        prod_real * taps_real - prod_imag * taps_imag, prod_real * taps_imag + prod_imag * taps_real, tab
    )
    skip = jnp.broadcast_to(lax.dynamic_slice(skip_weight, (at_ctx * group,), (group,))[:, None], (group, rows))
    gate = conv + skip[None] * product
    mixed = lax.all_to_all(double(gate * query, (near,)), CTX, 0, 0)

    mixed_grad = gradient(weights, near, far, at_k, n_ctx)
    grad_got = lax.all_to_all(mixed_grad + 0.0 * mixed, CTX, 0, 0)
    grad = grad_got.reshape(2, 16, 2, group, rows).sum(0).transpose(1, 0, 2, 3).reshape(n_ctx, group, rows)
    pre_grad = grad * query

    weight_part = outer(mixed, near, far, at_k)
    weight_part = lax.psum_scatter(weight_part, "y", scatter_dimension=0, tiled=True)
    weight_grad = lax.psum_scatter(weight_part, "x", scatter_dimension=0, tiled=False) * norm_scale

    partial_far = partial_sums(mixed, weights, at_k, True)
    partial_far = jnp.concatenate([other_core(partial_far[at : at + 2]) for at in range(0, 4, 2)])
    partial = partial_sums(mixed, weights, at_k, False, partial_far, (grad_got,))
    line_got = lax.all_to_all(partial, "l", 0, 0)
    partial = tie(line_got.sum(0), weight_part)
    projected = across(pick(partial, at_m), lambda h, m: (m, h))
    projected = projected + across(pick(partial, 1 - at_m), lambda h, m: (1 - m, h))

    grad_real, grad_imag = halves(forward_fourier(pre_grad, tab))
    lead_real = jnp.concatenate([taps_real, prod_real], 1)
    lead_imag = jnp.concatenate([taps_imag, prod_imag], 1)
    grad_real = jnp.concatenate([grad_real, grad_real], 1)
    grad_imag = jnp.concatenate([grad_imag, grad_imag], 1)
    lagged = inverse_fourier(
        grad_real * lead_real + grad_imag * lead_imag, grad_imag * lead_real - grad_real * lead_imag, tab
    )
    back = returned(lagged, pre_grad, signals, grad, gate, skip, (line_got,), norm_scale)
    back = lax.all_to_all(back, CTX, 0, 0)
    key_grad, value_grad, query_grad, filter_grad, skip_grad = finish(back, key_branch, value_branch, group)
    return (projected, key_grad, value_grad, query_grad, filter_grad, skip_grad.reshape(chans), weight_grad)


def solution(mesh):
    grid = Mesh(mesh.devices.reshape(SIZES), AXES)
    wide = P(("h", "y", "x"), ("m", "l", "k"))
    tall = P(("m", "l", "k"), ("h", "y", "x"))
    flat = P(("m", "l", "k"))
    return jax.shard_map(
        local,
        mesh=grid,
        in_specs=(wide, wide, wide, wide, flat, tall, wide),
        out_specs=(wide, wide, wide, wide, wide, flat, tall),
        check_vma=False,
    )
```

time: 281 us -> 264 us (0.940)
  local copies, waits for them, and re-layouts: 31 us -> 13.7 us
  Pallas kernels: 0 us -> 12.4 us
  matrix products: 14.2 us -> 4.92 us
  waiting for transfers between devices: 113 us -> 121 us
  starting transfers between devices: 92.2 us -> 84.8 us
    pallas_call x0 -> x8, Pallas kernels: none -> 12.4 us  [the longest x1 3.48 us: gradient(): pl.pallas_call(gradient_kernel, out_shape=jax.ShapeDtypeStruct((n_ctx, 2,...]
    all_to_all x1, waiting for transfers between devices: 22.4 us -> 11.5 us  [local(): lax.all_to_all(jnp.broadcast_to(cot_pair[None], (4,) + cot_pair.shape), '...]
    dot_general x3 -> x0, matrix products: 9.24 us -> none  [product_of(): lax.dot_general(left, right, (((left_dim,), (right_dim,)), ((), ())), pre...]
    all_to_all x4, waiting for transfers between devices: 34.8 us -> 43.8 us  [the longest x1 21.1 us: local(): line_got = lax.all_to_all(partial, 'l', 0, 0)]
    all_gather x1, waiting for transfers between devices: 0.02 us -> 7.25 us  [local(): weights = lax.all_gather(out_weight, PLANE, axis=1, tiled=True)]
    all_to_all x4, starting transfers between devices: 28.1 us -> 34.9 us  [the longest x1 13.4 us: local(): back = lax.all_to_all(back, CTX, 0, 0)]
    ppermute x2 -> x3, starting transfers between devices: 14.2 us -> 8.04 us  [other_core(): return lax.ppermute(block, 'k', [(0, 1), (1, 0)])]
    dot_general x4 -> x1, local copies, waits for them, and re-layouts: 5.97 us -> 0.16 us  [inverse_fourier(): return jnp.einsum('nk,kcm->ncm', tab['last'], turned, precision=exact)]
  transfers between devices with their start and end apart: 15 -> 16, of which waited for: 8 -> 8; matrix products, arithmetic and copies ran while one was open for 14% -> 7% of each run, Pallas kernels for 0% -> 4%
where the time goes in v8:
time: 264 us; the launch traced here: 262 us
  waiting for transfers between devices  121 us (46%)
  starting transfers between devices  84.8 us (32%)
  between operations  16.4 us (6%)
  local copies, waits for them, and re-layouts  13.7 us (5%)
  Pallas kernels  12.4 us (5%)
  other arithmetic  9.34 us (4%)
  matrix products  4.92 us (2%)
    ppermute x4, waiting for transfers between devices, across(): return lax.ppermute(block, ('h', 'm'), pairs)  45.4 us
    ppermute x4, starting transfers between devices, across(): return lax.ppermute(block, ('h', 'm'), pairs)  22.7 us
    all_to_all x1, waiting for transfers between devices, local(): line_got = lax.all_to_all(partial, 'l', 0, 0)  21.1 us
    all_to_all x1, waiting for transfers between devices, local(): mixed = lax.all_to_all(double(gate * query, (near,)), CTX, 0, 0)  19.3 us
    all_to_all x1, starting transfers between devices, local(): signals = lax.all_to_all(sent, CTX, 0, 0)  15.5 us
    all_to_all x1, starting transfers between devices, local(): back = lax.all_to_all(back, CTX, 0, 0)  13.4 us
    all_to_all x1, waiting for transfers between devices, local(): signals = lax.all_to_all(sent, CTX, 0, 0)  11.6 us
    all_to_all x1, waiting for transfers between devices, local(): lax.all_to_all(jnp.broadcast_to(cot_pair[None], (4,) + cot_pair.shape), '...  11.5 us
  transfers between devices with their start and end apart: 16, of which 8 were waited for; matrix products, arithmetic and copies ran while one was open for 7% of the time, Pallas kernels for 4%

profile of v8, /device:TPU:129, one launch (start us, length us, event | category | flops | bytes accessed | tf_op | source)
XLA Modules:
  0.0 262.4 jit_solution(8743148679856506097)
XLA Ops:
  7.9 0.9 copy-done.7
  8.8 0.9 copy-done.9
  9.7 0.9 copy-done.12
  10.6 0.9 copy-done.13
  11.5 0.9 shard_map.180
  12.4 15.5 %all-to-all-start = ((f32[32,24,128]{2,1,0:T(8,128)}), f32[32,24,128]{2,1,0:T(8,128)S(1)}, u32[]{:S(2)}, u32[]{:S(2)}) async-start(f32[32,24,128]{2,1,0:T(8,128)} %shard_map.180), calls=%async_computation | async-start | bytes 786432 | tf_op jit(solution)/shard_map/all_to_all | solution.py:346
  28.0 10.0 %collective-permute-start = (f32[128,256]{1,0:T(8,128)}, f32[128,256]{1,0:T(8,128)S(1)}, u32[]{:S(2)}, u32[]{:S(2)}) collective-permute-start(f32[128,256]{1,0:T(8,128)} %param.19), channel_id=1, source_target_pairs={{0,0},{8,256},{256,8},{264,264},{1,1},{9,257},{257,9},{265,265},{2... | collective-permute-start | bytes 393224 | tf_op jit(solution)/shard_map/ppermute | solution.py:307
  38.0 3.4 %collective-permute-start.1 = (f32[128,256]{1,0:T(8,128)}, f32[128,256]{1,0:T(8,128)S(1)}, u32[]{:S(2)}, u32[]{:S(2)}) collective-permute-start(f32[128,256]{1,0:T(8,128)} %param.19), channel_id=1, source_target_pairs={{0,8},{8,264},{256,0},{264,256},{1,9},{9,265},{257,1},{265,257},{2... | collective-permute-start | bytes 393224 | tf_op jit(solution)/shard_map/ppermute | solution.py:307
  41.4 11.6 %all-to-all-done.refs_2_ = f32[32,24,128]{2,1,0:T(8,128)S(1)} async-done(((f32[32,24,128]{2,1,0:T(8,128)}), f32[32,24,128]{2,1,0:T(8,128)S(1)}, u32[]{:S(2)}, u32[]{:S(2)}) %all-to-all-start) | async-done | bytes 393248 | tf_op jit(solution)/shard_map/all_to_all | solution.py:346
  54.2 12.0 %collective-permute-done = f32[128,256]{1,0:T(8,128)S(1)} collective-permute-done((f32[128,256]{1,0:T(8,128)}, f32[128,256]{1,0:T(8,128)S(1)}, u32[]{:S(2)}, u32[]{:S(2)}) %collective-permute-start) | collective-permute-done | bytes 131104 | tf_op jit(solution)/shard_map/ppermute | solution.py:307
  66.2 1.1 broadcast_in_dim.4
  67.3 3.5 %all-to-all-start.1 = ((f32[4,2,128,256]{3,2,1,0:T(8,128)}), f32[4,2,128,256]{3,2,1,0:T(8,128)S(1)}, u32[]{:S(2)}, u32[]{:S(2)}) async-start(f32[4,2,128,256]{3,2,1,0:T(8,128)} %broadcast_in_dim.4), calls=%async_computation.1 | async-start | bytes 2097152 | tf_op jit(solution)/shard_map/all_to_all | solution.py:350
  71.5 7.2 %all-gather.2.cloned.1.call-done.weight.near_w.far_w = f32[256,2048]{1,0:T(8,128)} async-done(((f32[256,128]{1,0:T(8,128)}), f32[256,2048]{1,0:T(8,128)}) %all-gather.2.cloned.1.call-update) | async-done | bytes 2097168 | tf_op jit(solution)/shard_map/all_gather | solution.py:339
  78.7 1.2 slice.94
  81.5 0.7 fusion.6
  82.2 0.8 fusion.41
  83.5 1.0 fusion.8
  84.5 11.5 %all-to-all-done.1.refs_0_.near = f32[4,2,128,256]{3,2,1,0:T(8,128)S(1)} async-done(((f32[4,2,128,256]{3,2,1,0:T(8,128)}), f32[4,2,128,256]{3,2,1,0:T(8,128)S(1)}, u32[]{:S(2)}, u32[]{:S(2)}) %all-to-all-start.1) | async-done | bytes 1048608 | tf_op jit(solution)/shard_map/all_to_all | solution.py:350
  96.0 3.4 %collective-permute-start.4 = (f32[4,2,128,256]{3,2,1,0:T(8,128)S(1)}, f32[4,2,128,256]{3,2,1,0:T(8,128)}, u32[]{:S(2)}, u32[]{:S(2)}) collective-permute-start(f32[4,2,128,256]{3,2,1,0:T(8,128)S(1)} %all-to-all-done.1.refs_0_.near), channel_id=1, source_target_pairs={{0,1},{1,0},{2,3},{3,2},{4,5},{5,4},{6,7},{7,6},{8,9},{9,8},{10,11... | collective-permute-start | bytes 3145736 | tf_op jit(solution)/shard_map/ppermute | solution.py:311
  99.4 1.7 slice_multiply_fusion.2
  101.8 11.5 %all-to-all-start.2 = ((f32[32,2,8,128]{3,2,1,0:T(8,128)}), f32[32,2,8,128]{3,2,1,0:T(8,128)S(1)}, u32[]{:S(2)}, u32[]{:S(2)}) async-start(f32[32,2,8,128]{3,2,1,0:T(8,128)} %copy-done.5), calls=%async_computation.2 | async-start | bytes 524288 | tf_op jit(solution)/shard_map/all_to_all | solution.py:362
  113.3 3.5 %shard_map.183 = f32[32,2,8,128]{3,2,1,0:T(8,128)S(1)} custom-call(s32[1]{0:T(128)} %bitcast.at_k, f32[256,2048]{1,0:T(8,128)S(1)} %copy-done, f32[256,2048]{1,0:T(8,128)S(1)} %copy-done, f32[4,2,128,256]{3,2,1,0:T(8,128)S(1)} %all-to-all-done.1.refs_0_.near, f32[4,2,128,256]{3,2,1,0:T(8,128)} %collective-permute-done.4.far), custom_call_target="tpu_custom_call" | custom-call | flops 805306368 | bytes 5242880 | tf_op jit(solution)/shard_map/pallas_call | solution.py:154
  116.8 0.7 copy-done.6
  117.5 19.3 %all-to-all-done.2.mixed = f32[32,2,8,128]{3,2,1,0:T(8,128)S(1)} async-done(((f32[32,2,8,128]{3,2,1,0:T(8,128)}), f32[32,2,8,128]{3,2,1,0:T(8,128)S(1)}, u32[]{:S(2)}, u32[]{:S(2)}) %all-to-all-start.2) | async-done | bytes 262176 | tf_op jit(solution)/shard_map/all_to_all | solution.py:362
  136.8 1.7 multiply_add_fusion.2
  138.5 6.3 %all-to-all-start.3 = ((f32[32,2,8,128]{3,2,1,0:T(8,128)}), f32[32,2,8,128]{3,2,1,0:T(8,128)}, u32[]{:S(2)}, u32[]{:S(2)}) async-start(f32[32,2,8,128]{3,2,1,0:T(8,128)} %multiply_add_fusion.2), calls=%async_computation.3 | async-start | bytes 524288 | tf_op jit(solution)/shard_map/all_to_all | solution.py:365
  144.9 1.4 shard_map.182
  146.3 1.1 fusion.40
  147.4 2.8 %collective-permute-start.2 = (f32[2,2,128,256]{3,2,1,0:T(8,128)}, f32[2,2,128,256]{3,2,1,0:T(8,128)}, u32[]{:S(2)}, u32[]{:S(2)}) collective-permute-start(f32[2,2,128,256]{3,2,1,0:T(8,128)} %get-tuple-element.19), channel_id=1, source_target_pairs={{0,1},{1,0},{2,3},{3,2},{4,5},{5,4},{6,7},{7,6},{8,9},{9,8},{10,11... | collective-permute-start | bytes 1572872 | tf_op jit(solution)/shard_map/ppermute | solution.py:311
  150.2 1.9 collective-permute-start.3
  152.1 3.2 %shard_map.185 = f32[16,256,128]{2,1,0:T(8,128)S(1)} custom-call(s32[1]{0:T(128)} %bitcast.at_k, f32[32,2,8,128]{3,2,1,0:T(8,128)S(1)} %all-to-all-done.2.mixed, f32[4,2,128,256]{3,2,1,0:T(8,128)S(1)} %all-to-all-done.1.refs_0_.near, f32[4,2,128,256]{3,2,1,0:T(8,128)} %collective-permute-done.4.far), custom_call_target="tpu_custom_call" | custom-call | flops 805306368 | bytes 5242880 | tf_op jit(solution)/shard_map/pallas_call | solution.py:238
  155.3 1.4 copy-done.1
  156.7 1.3 pad_maximum_fusion.refs_0_
  158.0 3.4 %all-to-all-done.3.refs_1_ = f32[32,2,8,128]{3,2,1,0:T(8,128)} async-done(((f32[32,2,8,128]{3,2,1,0:T(8,128)}), f32[32,2,8,128]{3,2,1,0:T(8,128)}, u32[]{:S(2)}, u32[]{:S(2)}) %all-to-all-start.3) | async-done | bytes 262176 | tf_op jit(solution)/shard_map/all_to_all | solution.py:365
  161.4 1.4 shard_map.184
  162.9 1.0 copy-done.4
  163.9 3.7 %all-to-all-start.4 = ((f32[4,2,128,256]{3,2,1,0:T(8,128)}), f32[4,2,128,256]{3,2,1,0:T(8,128)S(1)}, u32[]{:S(2)}, u32[]{:S(2)}) async-start(f32[4,2,128,256]{3,2,1,0:T(8,128)} %copy-done.4), calls=%async_computation.4 | async-start | bytes 2097152 | tf_op jit(solution)/shard_map/all_to_all | solution.py:376
  167.6 1.1 reduce_sum.19
  170.2 0.9 fusion
  171.8 21.1 %all-to-all-done.4.refs_6_ = f32[4,2,128,256]{3,2,1,0:T(8,128)S(1)} async-done(((f32[4,2,128,256]{3,2,1,0:T(8,128)}), f32[4,2,128,256]{3,2,1,0:T(8,128)S(1)}, u32[]{:S(2)}, u32[]{:S(2)}) %all-to-all-start.4) | async-done | bytes 1048608 | tf_op jit(solution)/shard_map/all_to_all | solution.py:376
  192.9 1.0 shard_map.186
  193.9 13.4 %all-to-all-start.5 = ((f32[32,32,128]{2,1,0:T(8,128)}), f32[32,32,128]{2,1,0:T(8,128)S(1)}, u32[]{:S(2)}, u32[]{:S(2)}) async-start(f32[32,32,128]{2,1,0:T(8,128)} %shard_map.186), calls=%async_computation.6 | async-start | bytes 1048576 | tf_op jit(solution)/shard_map/all_to_all | solution.py:390
  208.2 1.2 slice.109
  210.1 7.4 %collective-permute-start.5 = (f32[128,256]{1,0:T(8,128)S(1)}, f32[128,256]{1,0:T(8,128)S(1)}, u32[]{:S(2)}, u32[]{:S(2)}) collective-permute-start(f32[128,256]{1,0:T(8,128)S(1)} %get-tuple-element.42), channel_id=1, source_target_pairs={{0,0},{8,256},{256,8},{264,264},{1,1},{9,257},{257,9},{265,265},{2... | collective-permute-start | bytes 393224 | tf_op jit(solution)/shard_map/ppermute | solution.py:307
  217.5 1.9 collective-permute-start.6
  219.4 33.4 %collective-permute-done.5 = f32[128,256]{1,0:T(8,128)S(1)} collective-permute-done((f32[128,256]{1,0:T(8,128)S(1)}, f32[128,256]{1,0:T(8,128)S(1)}, u32[]{:S(2)}, u32[]{:S(2)}) %collective-permute-start.5) | collective-permute-done | bytes 131104 | tf_op jit(solution)/shard_map/ppermute | solution.py:307
  253.4 1.6 multiply_bitcast_fusion
  255.0 0.9 shard_map.187
  (101 shorter events, 7.7 us)
Async XLA Ops:
  7.2 71.5 %all-gather.2.cloned.1.call-start = ((), (), s32[]{:S(2)}) async-start(), calls=%async_computation.8 | async-start | bytes 2228224 | tf_op jit(solution)/shard_map/all_gather | solution.py:339
  7.9 0.9 copy-start.7
  8.8 0.9 copy-start.9
  9.7 0.9 copy-start.12
  10.6 0.9 copy-start.13
  12.4 40.5 %all-to-all-start = ((f32[32,24,128]{2,1,0:T(8,128)}), f32[32,24,128]{2,1,0:T(8,128)S(1)}, u32[]{:S(2)}, u32[]{:S(2)}) async-start(f32[32,24,128]{2,1,0:T(8,128)} %shard_map.180), calls=%async_computation | async-start | bytes 786432 | tf_op jit(solution)/shard_map/all_to_all | solution.py:346
  27.9 42.9 %copy-start.32 = (f32[256]{0:T(256)S(1)}, f32[256]{0:T(256)}, u32[]{:S(2)}) copy-start(f32[256]{0:T(256)} %param.17) | copy-start | bytes 3076
  28.0 38.2 %collective-permute-start = (f32[128,256]{1,0:T(8,128)}, f32[128,256]{1,0:T(8,128)S(1)}, u32[]{:S(2)}, u32[]{:S(2)}) collective-permute-start(f32[128,256]{1,0:T(8,128)} %param.19), channel_id=1, source_target_pairs={{0,0},{8,256},{256,8},{264,264},{1,1},{9,257},{257,9},{265,265},{2... | collective-permute-start | bytes 393224 | tf_op jit(solution)/shard_map/ppermute | solution.py:307
  38.0 28.1 %collective-permute-start.1 = (f32[128,256]{1,0:T(8,128)}, f32[128,256]{1,0:T(8,128)S(1)}, u32[]{:S(2)}, u32[]{:S(2)}) collective-permute-start(f32[128,256]{1,0:T(8,128)} %param.19), channel_id=1, source_target_pairs={{0,8},{8,264},{256,0},{264,256},{1,9},{9,265},{257,1},{265,257},{2... | collective-permute-start | bytes 393224 | tf_op jit(solution)/shard_map/ppermute | solution.py:307
  53.0 46.4 %copy-start.2 = (f32[32,24,128]{2,1,0:T(8,128)}, f32[32,24,128]{2,1,0:T(8,128)S(1)}, u32[]{:S(2)}) copy-start(f32[32,24,128]{2,1,0:T(8,128)S(1)} %all-to-all-done.refs_2_) | copy-start | bytes 1179652
  66.2 14.4 %copy-start.29 = (f32[66,32]{0,1:T(8,128)S(1)}, f32[66,32]{0,1:T(8,128)}, u32[]{:S(2)}) copy-start(f32[66,32]{0,1:T(8,128)} %constant.64.clone) | copy-start | bytes 25348
  66.2 15.1 %copy-start.22 = (f32[33,128]{1,0:T(8,128)S(1)}, f32[33,128]{1,0:T(8,128)}, u32[]{:S(2)}) copy-start(f32[33,128]{1,0:T(8,128)} %constant.65.clone) | copy-start | bytes 50692
  66.2 15.1 %copy-start.25 = (f32[33,128]{1,0:T(8,128)S(1)}, f32[33,128]{1,0:T(8,128)}, u32[]{:S(2)}) copy-start(f32[33,128]{1,0:T(8,128)} %constant.66.clone) | copy-start | bytes 50692
  67.3 28.7 %all-to-all-start.1 = ((f32[4,2,128,256]{3,2,1,0:T(8,128)}), f32[4,2,128,256]{3,2,1,0:T(8,128)S(1)}, u32[]{:S(2)}, u32[]{:S(2)}) async-start(f32[4,2,128,256]{3,2,1,0:T(8,128)} %broadcast_in_dim.4), calls=%async_computation.1 | async-start | bytes 2097152 | tf_op jit(solution)/shard_map/all_to_all | solution.py:350
  70.8 10.6 %copy-start.16 = (f32[256,256,1]{1,0,2:T(8,128)S(1)}, f32[256,256,1]{1,0,2:T(8,128)}, u32[]{:S(2)}) copy-start(f32[256,256,1]{1,0,2:T(8,128)} %constant.71) | copy-start | bytes 786436
  81.4 1.6 copy-start.14
  81.4 2.0 copy-start.23
  81.4 2.0 copy-start.26
  81.5 2.0 copy-start.28
  83.4 29.9 %copy-start = (f32[256,2048]{1,0:T(8,128)S(1)}, f32[256,2048]{1,0:T(8,128)}, u32[]{:S(2)}) copy-start(f32[256,2048]{1,0:T(8,128)} %all-gather.2.cloned.1.call-done.weight.near_w.far_w) | copy-start | bytes 6291460
  96.0 17.3 %collective-permute-start.4 = (f32[4,2,128,256]{3,2,1,0:T(8,128)S(1)}, f32[4,2,128,256]{3,2,1,0:T(8,128)}, u32[]{:S(2)}, u32[]{:S(2)}) collective-permute-start(f32[4,2,128,256]{3,2,1,0:T(8,128)S(1)} %all-to-all-done.1.refs_0_.near), channel_id=1, source_target_pairs={{0,1},{1,0},{2,3},{3,2},{4,5},{5,4},{6,7},{7,6},{8,9},{9,8},{10,11... | collective-permute-start | bytes 3145736 | tf_op jit(solution)/shard_map/ppermute | solution.py:311
  101.8 35.1 %all-to-all-start.2 = ((f32[32,2,8,128]{3,2,1,0:T(8,128)}), f32[32,2,8,128]{3,2,1,0:T(8,128)S(1)}, u32[]{:S(2)}, u32[]{:S(2)}) async-start(f32[32,2,8,128]{3,2,1,0:T(8,128)} %copy-done.5), calls=%async_computation.2 | async-start | bytes 524288 | tf_op jit(solution)/shard_map/all_to_all | solution.py:362
  116.8 0.7 copy-start.6
  138.5 22.9 %all-to-all-start.3 = ((f32[32,2,8,128]{3,2,1,0:T(8,128)}), f32[32,2,8,128]{3,2,1,0:T(8,128)}, u32[]{:S(2)}, u32[]{:S(2)}) async-start(f32[32,2,8,128]{3,2,1,0:T(8,128)} %multiply_add_fusion.2), calls=%async_computation.3 | async-start | bytes 524288 | tf_op jit(solution)/shard_map/all_to_all | solution.py:365
  144.8 62.6 %reduce-scatter.3.cloned.1.call-start = ((), (), s32[]{:S(2)}) async-start(), calls=%async_computation.9 | async-start | bytes 2621440 | tf_op jit(solution)/shard_map/reduce_scatter | solution.py:370
  147.4 9.3 %collective-permute-start.2 = (f32[2,2,128,256]{3,2,1,0:T(8,128)}, f32[2,2,128,256]{3,2,1,0:T(8,128)}, u32[]{:S(2)}, u32[]{:S(2)}) collective-permute-start(f32[2,2,128,256]{3,2,1,0:T(8,128)} %get-tuple-element.19), channel_id=1, source_target_pairs={{0,1},{1,0},{2,3},{3,2},{4,5},{5,4},{6,7},{7,6},{8,9},{9,8},{10,11... | collective-permute-start | bytes 1572872 | tf_op jit(solution)/shard_map/ppermute | solution.py:311
  150.2 6.5 %collective-permute-start.3 = (f32[2,2,128,256]{3,2,1,0:T(8,128)}, f32[2,2,128,256]{3,2,1,0:T(8,128)}, u32[]{:S(2)}, u32[]{:S(2)}) collective-permute-start(f32[2,2,128,256]{3,2,1,0:T(8,128)} %get-tuple-element.20), channel_id=1, source_target_pairs={{0,1},{1,0},{2,3},{3,2},{4,5},{5,4},{6,7},{7,6},{8,9},{9,8},{10,11... | collective-permute-start | bytes 1572872 | tf_op jit(solution)/shard_map/ppermute | solution.py:311
  155.3 1.4 copy-start.1
  162.9 1.0 copy-start.4
  163.9 4.8 %copy-start.3 = (f32[32,24,128]{2,1,0:T(8,128)S(1)}, f32[32,24,128]{2,1,0:T(8,128)}, u32[]{:S(2)}) copy-start(f32[32,24,128]{2,1,0:T(8,128)} %copy-done.2) | copy-start | bytes 1179652
  163.9 4.8 %copy-start.30 = (f32[66,32]{0,1:T(8,128)S(1)}, f32[66,32]{0,1:T(8,128)}, u32[]{:S(2)}) copy-start(f32[66,32]{0,1:T(8,128)} %constant.64.clone) | copy-start | bytes 25348
  163.9 5.3 %copy-start.24 = (f32[33,128]{1,0:T(8,128)S(1)}, f32[33,128]{1,0:T(8,128)}, u32[]{:S(2)}) copy-start(f32[33,128]{1,0:T(8,128)} %constant.65.clone) | copy-start | bytes 50692
  163.9 5.3 %copy-start.27 = (f32[33,128]{1,0:T(8,128)S(1)}, f32[33,128]{1,0:T(8,128)}, u32[]{:S(2)}) copy-start(f32[33,128]{1,0:T(8,128)} %constant.66.clone) | copy-start | bytes 50692
  163.9 5.4 %copy-start.17 = (f32[256,256,1]{1,0,2:T(8,128)S(1)}, f32[256,256,1]{1,0,2:T(8,128)}, u32[]{:S(2)}) copy-start(f32[256,256,1]{1,0,2:T(8,128)} %constant.71) | copy-start | bytes 786436
  163.9 29.0 %all-to-all-start.4 = ((f32[4,2,128,256]{3,2,1,0:T(8,128)}), f32[4,2,128,256]{3,2,1,0:T(8,128)S(1)}, u32[]{:S(2)}, u32[]{:S(2)}) async-start(f32[4,2,128,256]{3,2,1,0:T(8,128)} %copy-done.4), calls=%async_computation.4 | async-start | bytes 2097152 | tf_op jit(solution)/shard_map/all_to_all | solution.py:376
  167.5 2.2 copy-start.18
  167.6 2.2 copy-start.19
  167.6 2.2 copy-start.20
  167.6 2.2 copy-start.21
  169.2 1.0 copy-start.15
  170.2 22.7 %copy-start.31 = (f32[8]{0:T(128)S(1)}, f32[8]{0:T(128)}, u32[]{:S(2)}) copy-start(f32[8]{0:T(128)} %dynamic_slice.10) | copy-start | bytes 100
  170.2 22.7 %copy-start.11 = (f32[32,8,128]{2,1,0:T(8,128)S(1)}, f32[32,8,128]{2,1,0:T(8,128)}, u32[]{:S(2)}) copy-start(f32[32,8,128]{2,1,0:T(8,128)} %get-tuple-element.18.refs_4_) | copy-start | bytes 393220
  193.9 61.1 %copy-start.8 = (f32[128,256]{1,0:T(8,128)S(1)}, f32[128,256]{1,0:T(8,128)}, u32[]{:S(2)}) copy-start(f32[128,256]{1,0:T(8,128)} %refs_1_.3) | copy-start | bytes 393220
  193.9 61.1 %copy-start.10 = (f32[128,256]{1,0:T(8,128)S(1)}, f32[128,256]{1,0:T(8,128)}, u32[]{:S(2)}) copy-start(f32[128,256]{1,0:T(8,128)} %refs_2_.3) | copy-start | bytes 393220
  193.9 61.1 %all-to-all-start.5 = ((f32[32,32,128]{2,1,0:T(8,128)}), f32[32,32,128]{2,1,0:T(8,128)S(1)}, u32[]{:S(2)}, u32[]{:S(2)}) async-start(f32[32,32,128]{2,1,0:T(8,128)} %shard_map.186), calls=%async_computation.6 | async-start | bytes 1048576 | tf_op jit(solution)/shard_map/all_to_all | solution.py:390
  207.3 46.1 %reduce-scatter.5.cloned.1.call-start = ((), (), s32[]{:S(2)}) async-start(), calls=%async_computation.10 | async-start | bytes 655360 | tf_op jit(solution)/shard_map/reduce_scatter | solution.py:371
  210.1 42.7 %collective-permute-start.5 = (f32[128,256]{1,0:T(8,128)S(1)}, f32[128,256]{1,0:T(8,128)S(1)}, u32[]{:S(2)}, u32[]{:S(2)}) collective-permute-start(f32[128,256]{1,0:T(8,128)S(1)} %get-tuple-element.42), channel_id=1, source_target_pairs={{0,0},{8,256},{256,8},{264,264},{1,1},{9,257},{257,9},{265,265},{2... | collective-permute-start | bytes 393224 | tf_op jit(solution)/shard_map/ppermute | solution.py:307
  217.5 35.3 %collective-permute-start.6 = (f32[128,256]{1,0:T(8,128)S(1)}, f32[128,256]{1,0:T(8,128)S(1)}, u32[]{:S(2)}, u32[]{:S(2)}) collective-permute-start(f32[128,256]{1,0:T(8,128)S(1)} %get-tuple-element.41), channel_id=1, source_target_pairs={{0,256},{8,0},{256,264},{264,8},{1,257},{9,1},{257,265},{265,9},{2... | collective-permute-start | bytes 393224 | tf_op jit(solution)/shard_map/ppermute | solution.py:307
  (1 other events, 0.7 us)
Sparse Core Ops, SparseCore 0:
  11.0 67.6 all-gather.1
  156.8 39.9 reduce-scatter.2
  211.2 30.6 reduce-scatter.4

commit v9 on v8

--- a/solution.py
+++ b/solution.py
@@ -123,6 +123,39 @@
     )(mixed, *first)
 
 
+def line_kernel(at_m, same, swap, *refs):
+    out = refs[-1]
+    for to in range(out.shape[0]):
+        out[to, at_m[0]] = same[...]
+        out[to, 1 - at_m[0]] = swap[...]
+
+
+def line_blocks(same, swap, at_m, lines, first):
+    return pl.pallas_call(
+        line_kernel,
+        out_shape=jax.ShapeDtypeStruct((lines, 2) + same.shape, jnp.float32),
+        in_specs=[pl.BlockSpec(memory_space=pltpu.SMEM)] + [VMEM] * 2 + [ANY] * len(first),
+        out_specs=VMEM,
+        compiler_params=params(),
+        cost_estimate=cost(0, 1 << 20),
+    )(at_m, same, swap, *first)
+
+
+def pass_kernel(value, *refs):
+    refs[-1][...] = value[...]
+
+
+def after(value, first):
+    return pl.pallas_call(
+        pass_kernel,
+        out_shape=jax.ShapeDtypeStruct(value.shape, jnp.float32),
+        in_specs=[VMEM] + [ANY] * len(first),
+        out_specs=VMEM,
+        compiler_params=params(),
+        cost_estimate=cost(0, 1 << 18),
+    )(value, *first)
+
+
 def gradient_kernel(at_k, near_w, far_w, near, far, out, total):
     step = pl.program_id(0)
     rows = near.shape[2]
@@ -311,16 +344,6 @@
     return lax.ppermute(block, "k", [(0, 1), (1, 0)])
 
 
-def in_order(own, other, at):
-    return jnp.where(at == 0, jnp.stack([own, other]), jnp.stack([other, own]))
-
-
-def tie(value, *first):
-    for array in first:
-        value = value + 0.0 * array[(0,) * array.ndim]
-    return value
-
-
 def pick(pair, at):
     return lax.dynamic_index_in_dim(pair, at, 0, False)
 
@@ -332,25 +355,18 @@
     seq_len = rows * n_ctx
     norm_scale = 1.0 / math.sqrt(seq_len)
     tab = tables(seq_len)
-    at_m = lax.axis_index("m")
-    at_k = lax.axis_index("k").astype(jnp.int32).reshape(1)
+    at_m, at_k = (lax.axis_index(name).astype(jnp.int32).reshape(1) for name in ("m", "k"))
     at_ctx = lax.axis_index(CTX)
 
     weights = lax.all_gather(out_weight, PLANE, axis=1, tiled=True)
 
     cot_same = across(cotangent, lambda h, m: (m, h))
     cot_swap = across(cotangent, lambda h, m: (m, 1 - h))
-    cot_pair = in_order(cot_same, cot_swap, at_m)
 
     sent = prepare(key_branch, value_branch, long_filter, query_branch, (), norm_scale, n_ctx)
     signals = lax.all_to_all(sent, CTX, 0, 0)
     product, query = signals[:, :group], signals[:, 2 * group :]
 
-    cot_pair = tie(cot_pair, signals)
-    near = lax.all_to_all(jnp.broadcast_to(cot_pair[None], (4,) + cot_pair.shape), "l", 0, 0)
-    far = other_core(near)
-
-    tab["first"] = tie(tab["first"], weights)
     spectra = forward_fourier(signals[:, : 2 * group], tab)
     prod_real, prod_imag = halves(spectra[:, :group])
     taps_real, taps_imag = halves(spectra[:, group:])
@@ -359,24 +375,28 @@
     )
     skip = jnp.broadcast_to(lax.dynamic_slice(skip_weight, (at_ctx * group,), (group,))[:, None], (group, rows))
     gate = conv + skip[None] * product
-    mixed = lax.all_to_all(double(gate * query, (near,)), CTX, 0, 0)
-
-    mixed_grad = gradient(weights, near, far, at_k, n_ctx)
-    grad_got = lax.all_to_all(mixed_grad + 0.0 * mixed, CTX, 0, 0)
-    grad = grad_got.reshape(2, 16, 2, group, rows).sum(0).transpose(1, 0, 2, 3).reshape(n_ctx, group, rows)
-    pre_grad = grad * query
+    mixed = lax.all_to_all(double(gate * query, ()), CTX, 0, 0)
+
+    near = line_blocks(cot_same, cot_swap, at_m, 4, (mixed,))
+    near = lax.all_to_all(near, "l", 0, 0)
+    far = other_core(near)
+
+    partial = partial_sums(mixed, weights, at_k, True)
+    partial = jnp.concatenate([other_core(partial[at : at + 2]) for at in range(0, 4, 2)])
+    partial = partial_sums(mixed, weights, at_k, False, partial, (near,))
+    line_got = lax.all_to_all(partial, "l", 0, 0)
+    partial = line_got.sum(0)
+    projected = across(pick(partial, at_m[0]), lambda h, m: (m, h))
+    projected = projected + across(pick(partial, 1 - at_m[0]), lambda h, m: (1 - m, h))
 
     weight_part = outer(mixed, near, far, at_k)
     weight_part = lax.psum_scatter(weight_part, "y", scatter_dimension=0, tiled=True)
     weight_grad = lax.psum_scatter(weight_part, "x", scatter_dimension=0, tiled=False) * norm_scale
 
-    partial_far = partial_sums(mixed, weights, at_k, True)
-    partial_far = jnp.concatenate([other_core(partial_far[at : at + 2]) for at in range(0, 4, 2)])
-    partial = partial_sums(mixed, weights, at_k, False, partial_far, (grad_got,))
-    line_got = lax.all_to_all(partial, "l", 0, 0)
-    partial = tie(line_got.sum(0), weight_part)
-    projected = across(pick(partial, at_m), lambda h, m: (m, h))
-    projected = projected + across(pick(partial, 1 - at_m), lambda h, m: (1 - m, h))
+    mixed_grad = gradient(weights, near, far, at_k, n_ctx)
+    grad_got = lax.all_to_all(after(mixed_grad, (line_got,)), CTX, 0, 0)
+    grad = grad_got.reshape(2, 16, 2, group, rows).sum(0).transpose(1, 0, 2, 3).reshape(n_ctx, group, rows)
+    pre_grad = grad * query
 
     grad_real, grad_imag = halves(forward_fourier(pre_grad, tab))
     lead_real = jnp.concatenate([taps_real, prod_real], 1)
@@ -386,7 +406,7 @@
     lagged = inverse_fourier(
         grad_real * lead_real + grad_imag * lead_imag, grad_imag * lead_real - grad_real * lead_imag, tab
     )
-    back = returned(lagged, pre_grad, signals, grad, gate, skip, (line_got,), norm_scale)
+    back = returned(lagged, pre_grad, signals, grad, gate, skip, (projected, weight_part), norm_scale)
     back = lax.all_to_all(back, CTX, 0, 0)
     key_grad, value_grad, query_grad, filter_grad, skip_grad = finish(back, key_branch, value_branch, group)
     return (projected, key_grad, value_grad, query_grad, filter_grad, skip_grad.reshape(chans), weight_grad)

time: 264 us -> 265 us (level)
  the two profiles are of different devices: /device:TPU:129 before, /device:TPU:1 now
where the time goes in v9:
time: 265 us; the launch traced here: 264 us
  starting transfers between devices  108 us (41%)
  waiting for transfers between devices  105 us (40%)
  between operations  16.2 us (6%)
  local copies, waits for them, and re-layouts  13.6 us (5%)
  Pallas kernels  11.8 us (4%)
  other arithmetic  5.44 us (2%)
  matrix products  4.26 us (2%)
    reduce_scatter x1, waiting for transfers between devices, local(): lax.psum_scatter(weight_part, 'x', scatter_dimension=0, tiled=False)  33.2 us
    ppermute x4, starting transfers between devices, across(): return lax.ppermute(block, ('h', 'm'), pairs)  28 us
    ppermute x4, waiting for transfers between devices, across(): return lax.ppermute(block, ('h', 'm'), pairs)  23.1 us
    all_to_all x1, starting transfers between devices, local(): near = lax.all_to_all(near, 'l', 0, 0)  23 us
    all_to_all x1, starting transfers between devices, local(): signals = lax.all_to_all(sent, CTX, 0, 0)  21.1 us
    all_to_all x1, waiting for transfers between devices, local(): signals = lax.all_to_all(sent, CTX, 0, 0)  16.7 us
    all_to_all x1, waiting for transfers between devices, local(): near = lax.all_to_all(near, 'l', 0, 0)  14 us
    unnamed x70, local copies, waits for them, and re-layouts  12.5 us
  transfers between devices with their start and end apart: 16, of which 8 were waited for; matrix products, arithmetic and copies ran while one was open for 4% of the time, Pallas kernels for 3%

profile of v9, /device:TPU:1, one launch (start us, length us, event | category | flops | bytes accessed | tf_op | source)
XLA Modules:
  0.0 264.4 jit_solution(3512482952870919514)
XLA Ops:
  8.0 0.9 copy-done.11
  8.9 0.9 copy-done.13
  9.8 0.9 copy-done.15
  10.7 0.9 copy-done.16
  11.6 0.9 shard_map.180
  12.6 21.1 %all-to-all-start = ((f32[32,24,128]{2,1,0:T(8,128)}), f32[32,24,128]{2,1,0:T(8,128)S(1)}, u32[]{:S(2)}, u32[]{:S(2)}) async-start(f32[32,24,128]{2,1,0:T(8,128)} %shard_map.180), calls=%async_computation | async-start | bytes 786432 | tf_op jit(solution)/shard_map/all_to_all | solution.py:367
  34.4 0.8 dynamic_slice.10
  35.2 16.7 %all-to-all-done.refs_2_ = f32[32,24,128]{2,1,0:T(8,128)S(1)} async-done(((f32[32,24,128]{2,1,0:T(8,128)}), f32[32,24,128]{2,1,0:T(8,128)S(1)}, u32[]{:S(2)}, u32[]{:S(2)}) %all-to-all-start) | async-done | bytes 393248 | tf_op jit(solution)/shard_map/all_to_all | solution.py:367
  52.8 0.7 fusion.6
  53.5 0.8 fusion.34
  55.3 0.7 shard_map.181
  56.0 4.0 %all-to-all-start.1 = ((f32[32,2,8,128]{3,2,1,0:T(8,128)}), f32[32,2,8,128]{3,2,1,0:T(8,128)S(1)}, u32[]{:S(2)}, u32[]{:S(2)}) async-start(f32[32,2,8,128]{3,2,1,0:T(8,128)} %shard_map.181), calls=%async_computation.1 | async-start | bytes 524288 | tf_op jit(solution)/shard_map/all_to_all | solution.py:378
  60.7 13.4 %collective-permute-start.3 = (f32[128,256]{1,0:T(8,128)S(1)}, f32[128,256]{1,0:T(8,128)S(1)}, u32[]{:S(2)}, u32[]{:S(2)}) collective-permute-start(f32[128,256]{1,0:T(8,128)S(1)} %copy-done.34), channel_id=1, source_target_pairs={{0,8},{8,264},{256,0},{264,256},{1,9},{9,265},{257,1},{265,257},{2... | collective-permute-start | bytes 393224 | tf_op jit(solution)/shard_map/ppermute | solution.py:340
  74.1 9.9 %collective-permute-done.3.swap = f32[128,256]{1,0:T(8,128)S(1)} collective-permute-done((f32[128,256]{1,0:T(8,128)S(1)}, f32[128,256]{1,0:T(8,128)S(1)}, u32[]{:S(2)}, u32[]{:S(2)}) %collective-permute-start.3) | collective-permute-done | bytes 131104 | tf_op jit(solution)/shard_map/ppermute | solution.py:340
  84.0 1.0 shard_map.183
  85.1 23.0 %all-to-all-start.2 = ((f32[4,2,128,256]{3,2,1,0:T(8,128)}), f32[4,2,128,256]{3,2,1,0:T(8,128)S(1)}, u32[]{:S(2)}, u32[]{:S(2)}) async-start(f32[4,2,128,256]{3,2,1,0:T(8,128)} %shard_map.183), calls=%async_computation.2 | async-start | bytes 2097152 | tf_op jit(solution)/shard_map/all_to_all | solution.py:381
  108.0 1.6 copy-done
  109.6 1.4 shard_map.182
  111.1 3.2 %collective-permute-start.1 = (f32[2,2,128,256]{3,2,1,0:T(8,128)S(1)}, f32[2,2,128,256]{3,2,1,0:T(8,128)S(1)}, u32[]{:S(2)}, u32[]{:S(2)}) collective-permute-start(f32[2,2,128,256]{3,2,1,0:T(8,128)S(1)} %get-tuple-element.20), channel_id=1, source_target_pairs={{0,1},{1,0},{2,3},{3,2},{4,5},{5,4},{6,7},{7,6},{8,9},{9,8},{10,11... | collective-permute-start | bytes 1572872 | tf_op jit(solution)/shard_map/ppermute | solution.py:344
  114.3 1.9 collective-permute-start
  116.2 1.9 collective-permute-done
  118.1 1.1 pad_maximum_fusion.refs_0_
  119.2 14.0 %all-to-all-done.2.refs_1_.near = f32[4,2,128,256]{3,2,1,0:T(8,128)S(1)} async-done(((f32[4,2,128,256]{3,2,1,0:T(8,128)}), f32[4,2,128,256]{3,2,1,0:T(8,128)S(1)}, u32[]{:S(2)}, u32[]{:S(2)}) %all-to-all-start.2) | async-done | bytes 1048608 | tf_op jit(solution)/shard_map/all_to_all | solution.py:381
  133.2 1.2 copy-done.8
  134.5 1.4 shard_map.184
  135.9 1.0 copy-done.7
  136.9 4.3 %all-to-all-start.3 = ((f32[4,2,128,256]{3,2,1,0:T(8,128)}), f32[4,2,128,256]{3,2,1,0:T(8,128)}, u32[]{:S(2)}, u32[]{:S(2)}) async-start(f32[4,2,128,256]{3,2,1,0:T(8,128)} %copy-done.7), calls=%async_computation.3 | async-start | bytes 2097152 | tf_op jit(solution)/shard_map/all_to_all | solution.py:387
  141.2 3.4 %collective-permute-start.6 = (f32[4,2,128,256]{3,2,1,0:T(8,128)S(1)}, f32[4,2,128,256]{3,2,1,0:T(8,128)S(1)}, u32[]{:S(2)}, u32[]{:S(2)}) collective-permute-start(f32[4,2,128,256]{3,2,1,0:T(8,128)S(1)} %all-to-all-done.2.refs_1_.near), channel_id=1, source_target_pairs={{0,1},{1,0},{2,3},{3,2},{4,5},{5,4},{6,7},{7,6},{8,9},{9,8},{10,11... | collective-permute-start | bytes 3145736 | tf_op jit(solution)/shard_map/ppermute | solution.py:344
  144.6 2.3 collective-permute-done.6.far
  146.8 1.7 shard_map.187
  148.5 1.3 copy-done.2
  149.9 1.0 copy-done.5
  150.9 1.2 copy-done.6
  152.1 2.0 shard_map.185.value
  154.2 12.2 %all-to-all-done.3.refs_0_ = f32[4,2,128,256]{3,2,1,0:T(8,128)} async-done(((f32[4,2,128,256]{3,2,1,0:T(8,128)}), f32[4,2,128,256]{3,2,1,0:T(8,128)}, u32[]{:S(2)}, u32[]{:S(2)}) %all-to-all-start.3) | async-done | bytes 1048608 | tf_op jit(solution)/shard_map/all_to_all | solution.py:387
  166.4 0.7 shard_map.186
  167.1 7.0 %all-to-all-start.4 = ((f32[32,2,8,128]{3,2,1,0:T(8,128)}), f32[32,2,8,128]{3,2,1,0:T(8,128)S(1)}, u32[]{:S(2)}, u32[]{:S(2)}) async-start(f32[32,2,8,128]{3,2,1,0:T(8,128)} %shard_map.186), calls=%async_computation.4 | async-start | bytes 524288 | tf_op jit(solution)/shard_map/all_to_all | solution.py:397
  174.2 1.3 reduce_sum.18
  175.6 0.8 collective-permute-start.4
  176.4 13.1 %collective-permute-start.5 = (f32[128,256]{1,0:T(8,128)S(1)}, f32[128,256]{1,0:T(8,128)S(1)}, u32[]{:S(2)}, u32[]{:S(2)}) collective-permute-start(f32[128,256]{1,0:T(8,128)S(1)} %get-tuple-element.41), channel_id=1, source_target_pairs={{0,256},{8,0},{256,264},{264,8},{1,257},{9,1},{257,265},{265,9},{2... | collective-permute-start | bytes 393224 | tf_op jit(solution)/shard_map/ppermute | solution.py:340
  189.6 13.2 %collective-permute-done.5 = f32[128,256]{1,0:T(8,128)S(1)} collective-permute-done((f32[128,256]{1,0:T(8,128)S(1)}, f32[128,256]{1,0:T(8,128)S(1)}, u32[]{:S(2)}, u32[]{:S(2)}) %collective-permute-start.5) | collective-permute-done | bytes 131104 | tf_op jit(solution)/shard_map/ppermute | solution.py:340
  204.5 0.9 fusion
  206.3 1.0 copy-done.9
  207.3 1.0 shard_map.188
  208.3 12.4 %all-to-all-start.5 = ((f32[32,32,128]{2,1,0:T(8,128)}), f32[32,32,128]{2,1,0:T(8,128)S(1)}, u32[]{:S(2)}, u32[]{:S(2)}) async-start(f32[32,32,128]{2,1,0:T(8,128)} %shard_map.188), calls=%async_computation.6 | async-start | bytes 1048576 | tf_op jit(solution)/shard_map/all_to_all | solution.py:410
  221.3 33.2 %reduce-scatter.5.cloned.1.call-done = f32[1,256,128]{2,1,0:T(8,128)} async-done(((f32[4,256,128]{2,1,0:T(8,128)}), f32[1,256,128]{2,1,0:T(8,128)}) %reduce-scatter.5.cloned.1.call-update) | async-done | bytes 131088 | tf_op jit(solution)/shard_map/reduce_scatter | solution.py:394
  254.5 1.6 multiply_bitcast_fusion
  256.1 0.9 shard_map.189
  (100 shorter events, 6.2 us)
Async XLA Ops:
  8.0 43.9 %copy-start.30 = (f32[66,32,1]{0,1,2:T(8,128)S(1)}, f32[66,32,1]{0,1,2:T(8,128)}, u32[]{:S(2)}) copy-start(f32[66,32,1]{0,1,2:T(8,128)} %constant.65) | copy-start | bytes 25348
  8.0 0.9 copy-start.11
  11.6 41.0 %copy-start.25 = (f32[33,128]{1,0:T(8,128)S(1)}, f32[33,128]{1,0:T(8,128)}, u32[]{:S(2)}) copy-start(f32[33,128]{1,0:T(8,128)} %constant.60.clone) | copy-start | bytes 50692
  11.6 41.0 %copy-start.27 = (f32[33,128]{1,0:T(8,128)S(1)}, f32[33,128]{1,0:T(8,128)}, u32[]{:S(2)}) copy-start(f32[33,128]{1,0:T(8,128)} %constant.59.clone) | copy-start | bytes 50692
  12.6 39.4 %all-to-all-start = ((f32[32,24,128]{2,1,0:T(8,128)}), f32[32,24,128]{2,1,0:T(8,128)S(1)}, u32[]{:S(2)}, u32[]{:S(2)}) async-start(f32[32,24,128]{2,1,0:T(8,128)} %shard_map.180), calls=%async_computation | async-start | bytes 786432 | tf_op jit(solution)/shard_map/all_to_all | solution.py:367
  33.7 19.1 %copy-start.19 = (f32[256,256,1]{1,0,2:T(8,128)S(1)}, f32[256,256,1]{1,0,2:T(8,128)}, u32[]{:S(2)}) copy-start(f32[256,256,1]{1,0,2:T(8,128)} %constant.66) | copy-start | bytes 786436
  33.7 74.3 %all-gather.2.cloned.1.call-start = ((), (), s32[]{:S(2)}) async-start(), calls=%async_computation.8 | async-start | bytes 2228224 | tf_op jit(solution)/shard_map/all_gather | solution.py:361
  35.2 20.0 %copy-start.32 = (f32[8]{0:T(128)}, f32[8]{0:T(128)S(1)}, u32[]{:S(2)}) copy-start(f32[8]{0:T(128)S(1)} %dynamic_slice.10) | copy-start | bytes 100
  51.9 3.3 %copy-start.3 = (f32[32,24,128]{2,1,0:T(8,128)}, f32[32,24,128]{2,1,0:T(8,128)S(1)}, u32[]{:S(2)}) copy-start(f32[32,24,128]{2,1,0:T(8,128)S(1)} %all-to-all-done.refs_2_) | copy-start | bytes 1179652
  52.8 1.6 copy-start.17
  52.8 2.0 copy-start.29
  54.4 5.7 %copy-start.34 = (f32[128,256]{1,0:T(8,128)S(1)}, f32[128,256]{1,0:T(8,128)}, u32[]{:S(2)}) copy-start(f32[128,256]{1,0:T(8,128)} %param.19) | copy-start | bytes 393220
  56.0 28.0 %all-to-all-start.1 = ((f32[32,2,8,128]{3,2,1,0:T(8,128)}), f32[32,2,8,128]{3,2,1,0:T(8,128)S(1)}, u32[]{:S(2)}, u32[]{:S(2)}) async-start(f32[32,2,8,128]{3,2,1,0:T(8,128)} %shard_map.181), calls=%async_computation.1 | async-start | bytes 524288 | tf_op jit(solution)/shard_map/all_to_all | solution.py:378
  60.0 14.1 %collective-permute-start.2 = (f32[128,256]{1,0:T(8,128)S(1)}, f32[128,256]{1,0:T(8,128)S(1)}, u32[]{:S(2)}, u32[]{:S(2)}) collective-permute-start(f32[128,256]{1,0:T(8,128)S(1)} %copy-done.34), channel_id=1, source_target_pairs={{0,0},{8,256},{256,8},{264,264},{1,1},{9,257},{257,9},{265,265},{2... | collective-permute-start | bytes 393224 | tf_op jit(solution)/shard_map/ppermute | solution.py:340
  60.7 23.3 %collective-permute-start.3 = (f32[128,256]{1,0:T(8,128)S(1)}, f32[128,256]{1,0:T(8,128)S(1)}, u32[]{:S(2)}, u32[]{:S(2)}) collective-permute-start(f32[128,256]{1,0:T(8,128)S(1)} %copy-done.34), channel_id=1, source_target_pairs={{0,8},{8,264},{256,0},{264,256},{1,9},{9,265},{257,1},{265,257},{2... | collective-permute-start | bytes 393224 | tf_op jit(solution)/shard_map/ppermute | solution.py:340
  85.1 48.2 %all-to-all-start.2 = ((f32[4,2,128,256]{3,2,1,0:T(8,128)}), f32[4,2,128,256]{3,2,1,0:T(8,128)S(1)}, u32[]{:S(2)}, u32[]{:S(2)}) async-start(f32[4,2,128,256]{3,2,1,0:T(8,128)} %shard_map.183), calls=%async_computation.2 | async-start | bytes 2097152 | tf_op jit(solution)/shard_map/all_to_all | solution.py:381
  108.0 1.6 copy-start
  111.0 22.2 %copy-start.1 = (f32[256,2048]{1,0:T(8,128)S(1)}, f32[256,2048]{1,0:T(8,128)}, u32[]{:S(2)}) copy-start(f32[256,2048]{1,0:T(8,128)} %all-gather.2.cloned.1.call-done.weight.near_w.far_w) | copy-start | bytes 6291460
  111.1 5.1 %collective-permute-start.1 = (f32[2,2,128,256]{3,2,1,0:T(8,128)S(1)}, f32[2,2,128,256]{3,2,1,0:T(8,128)S(1)}, u32[]{:S(2)}, u32[]{:S(2)}) collective-permute-start(f32[2,2,128,256]{3,2,1,0:T(8,128)S(1)} %get-tuple-element.20), channel_id=1, source_target_pairs={{0,1},{1,0},{2,3},{3,2},{4,5},{5,4},{6,7},{7,6},{8,9},{9,8},{10,11... | collective-permute-start | bytes 1572872 | tf_op jit(solution)/shard_map/ppermute | solution.py:344
  114.3 3.8 %collective-permute-start = (f32[2,2,128,256]{3,2,1,0:T(8,128)S(1)}, f32[2,2,128,256]{3,2,1,0:T(8,128)S(1)}, u32[]{:S(2)}, u32[]{:S(2)}) collective-permute-start(f32[2,2,128,256]{3,2,1,0:T(8,128)S(1)} %get-tuple-element.19), channel_id=1, source_target_pairs={{0,1},{1,0},{2,3},{3,2},{4,5},{5,4},{6,7},{7,6},{8,9},{9,8},{10,11... | collective-permute-start | bytes 1572872 | tf_op jit(solution)/shard_map/ppermute | solution.py:344
  133.2 1.2 copy-start.8
  135.9 1.0 copy-start.7
  136.9 29.5 %all-to-all-start.3 = ((f32[4,2,128,256]{3,2,1,0:T(8,128)}), f32[4,2,128,256]{3,2,1,0:T(8,128)}, u32[]{:S(2)}, u32[]{:S(2)}) async-start(f32[4,2,128,256]{3,2,1,0:T(8,128)} %copy-done.7), calls=%async_computation.3 | async-start | bytes 2097152 | tf_op jit(solution)/shard_map/all_to_all | solution.py:387
  141.1 65.0 %reduce-scatter.3.cloned.1.call-start = ((), (), s32[]{:S(2)}) async-start(), calls=%async_computation.9 | async-start | bytes 2621440 | tf_op jit(solution)/shard_map/reduce_scatter | solution.py:393
  141.2 5.6 %collective-permute-start.6 = (f32[4,2,128,256]{3,2,1,0:T(8,128)S(1)}, f32[4,2,128,256]{3,2,1,0:T(8,128)S(1)}, u32[]{:S(2)}, u32[]{:S(2)}) collective-permute-start(f32[4,2,128,256]{3,2,1,0:T(8,128)S(1)} %all-to-all-done.2.refs_1_.near), channel_id=1, source_target_pairs={{0,1},{1,0},{2,3},{3,2},{4,5},{5,4},{6,7},{7,6},{8,9},{9,8},{10,11... | collective-permute-start | bytes 3145736 | tf_op jit(solution)/shard_map/ppermute | solution.py:344
  148.5 1.4 copy-start.2
  149.9 1.0 copy-start.5
  150.9 1.2 copy-start.6
  167.1 35.8 %copy-start.4 = (f32[32,24,128]{2,1,0:T(8,128)S(1)}, f32[32,24,128]{2,1,0:T(8,128)}, u32[]{:S(2)}) copy-start(f32[32,24,128]{2,1,0:T(8,128)} %copy-done.3) | copy-start | bytes 1179652
  167.1 35.8 %copy-start.31 = (f32[66,32,1]{0,1,2:T(8,128)S(1)}, f32[66,32,1]{0,1,2:T(8,128)}, u32[]{:S(2)}) copy-start(f32[66,32,1]{0,1,2:T(8,128)} %constant.65) | copy-start | bytes 25348
  167.1 35.7 %all-to-all-start.4 = ((f32[32,2,8,128]{3,2,1,0:T(8,128)}), f32[32,2,8,128]{3,2,1,0:T(8,128)S(1)}, u32[]{:S(2)}, u32[]{:S(2)}) async-start(f32[32,2,8,128]{3,2,1,0:T(8,128)} %shard_map.186), calls=%async_computation.4 | async-start | bytes 524288 | tf_op jit(solution)/shard_map/all_to_all | solution.py:397
  174.2 29.3 %copy-start.26 = (f32[33,128]{1,0:T(8,128)S(1)}, f32[33,128]{1,0:T(8,128)}, u32[]{:S(2)}) copy-start(f32[33,128]{1,0:T(8,128)} %constant.60.clone) | copy-start | bytes 50692
  174.2 29.3 %copy-start.28 = (f32[33,128]{1,0:T(8,128)S(1)}, f32[33,128]{1,0:T(8,128)}, u32[]{:S(2)}) copy-start(f32[33,128]{1,0:T(8,128)} %constant.59.clone) | copy-start | bytes 50692
  175.6 28.0 %copy-start.20 = (f32[256,256,1]{1,0,2:T(8,128)S(1)}, f32[256,256,1]{1,0,2:T(8,128)}, u32[]{:S(2)}) copy-start(f32[256,256,1]{1,0,2:T(8,128)} %constant.66) | copy-start | bytes 786436
  175.6 13.9 %collective-permute-start.4 = (f32[128,256]{1,0:T(8,128)S(1)}, f32[128,256]{1,0:T(8,128)S(1)}, u32[]{:S(2)}, u32[]{:S(2)}) collective-permute-start(f32[128,256]{1,0:T(8,128)S(1)} %get-tuple-element.42), channel_id=1, source_target_pairs={{0,0},{8,256},{256,8},{264,264},{1,1},{9,257},{257,9},{265,265},{2... | collective-permute-start | bytes 393224 | tf_op jit(solution)/shard_map/ppermute | solution.py:340
  176.4 26.4 %collective-permute-start.5 = (f32[128,256]{1,0:T(8,128)S(1)}, f32[128,256]{1,0:T(8,128)S(1)}, u32[]{:S(2)}, u32[]{:S(2)}) collective-permute-start(f32[128,256]{1,0:T(8,128)S(1)} %get-tuple-element.41), channel_id=1, source_target_pairs={{0,256},{8,0},{256,264},{264,8},{1,257},{9,1},{257,265},{265,9},{2... | collective-permute-start | bytes 393224 | tf_op jit(solution)/shard_map/ppermute | solution.py:340
  202.8 3.4 %copy-start.10 = (f32[128,256]{1,0:T(8,128)}, f32[128,256]{1,0:T(8,128)S(1)}, u32[]{:S(2)}) copy-start(f32[128,256]{1,0:T(8,128)S(1)} %add.54.refs_6_) | copy-start | bytes 393220
  202.8 1.2 copy-start.21
  202.8 1.2 copy-start.22
  202.9 1.2 copy-start.23
  202.9 1.2 copy-start.24
  203.5 1.0 copy-start.18
  204.5 1.7 copy-start.33
  205.9 50.1 %copy-start.12 = (f32[128,256]{1,0:T(8,128)S(1)}, f32[128,256]{1,0:T(8,128)}, u32[]{:S(2)}) copy-start(f32[128,256]{1,0:T(8,128)} %refs_1_.3) | copy-start | bytes 393220
  206.0 50.1 %copy-start.14 = (f32[128,256]{1,0:T(8,128)S(1)}, f32[128,256]{1,0:T(8,128)}, u32[]{:S(2)}) copy-start(f32[128,256]{1,0:T(8,128)} %refs_2_.3) | copy-start | bytes 393220
  206.2 1.0 copy-start.9
  208.3 47.8 %all-to-all-start.5 = ((f32[32,32,128]{2,1,0:T(8,128)}), f32[32,32,128]{2,1,0:T(8,128)S(1)}, u32[]{:S(2)}, u32[]{:S(2)}) async-start(f32[32,32,128]{2,1,0:T(8,128)} %shard_map.188), calls=%async_computation.6 | async-start | bytes 1048576 | tf_op jit(solution)/shard_map/all_to_all | solution.py:410
  220.7 33.8 %reduce-scatter.5.cloned.1.call-start = ((), (), s32[]{:S(2)}) async-start(), calls=%async_computation.10 | async-start | bytes 655360 | tf_op jit(solution)/shard_map/reduce_scatter | solution.py:394
  (3 other events, 2.7 us)
Sparse Core Ops, SparseCore 0:
  37.5 63.9 all-gather.1
Sparse Core Ops, SparseCore 1:
  151.0 32.2 reduce-scatter.2
  224.2 30.2 reduce-scatter.4

commit v10 on v9

--- a/solution.py
+++ b/solution.py
@@ -331,17 +331,17 @@
     )(back, key, value)
 
 
-def across(block, target):
-    pairs = []
-    for h in range(2):
-        for m in range(2):
-            to_h, to_m = target(h, m)
-            pairs.append((h * 2 + m, to_h * 2 + to_m))
-    return lax.ppermute(block, ("h", "m"), pairs)
+def swap_hm(block):
+    return lax.ppermute(block, ("h", "m"), [(h * 2 + m, m * 2 + h) for h in range(2) for m in range(2)])
 
 
 def other_core(block):
     return lax.ppermute(block, "k", [(0, 1), (1, 0)])
+
+
+def fold(pair, at, axis, apart):
+    pairs = [(here, here ^ apart) for here in range(lax.axis_size(axis))]
+    return pick(pair, at) + lax.ppermute(pick(pair, 1 - at), axis, pairs)
 
 
 def pick(pair, at):
@@ -356,12 +356,13 @@
     norm_scale = 1.0 / math.sqrt(seq_len)
     tab = tables(seq_len)
     at_m, at_k = (lax.axis_index(name).astype(jnp.int32).reshape(1) for name in ("m", "k"))
+    at_x = lax.axis_index("x")
     at_ctx = lax.axis_index(CTX)
 
     weights = lax.all_gather(out_weight, PLANE, axis=1, tiled=True)
 
-    cot_same = across(cotangent, lambda h, m: (m, h))
-    cot_swap = across(cotangent, lambda h, m: (m, 1 - h))
+    cot_same = swap_hm(cotangent)
+    cot_swap = lax.ppermute(cot_same, "m", [(0, 1), (1, 0)])
 
     sent = prepare(key_branch, value_branch, long_filter, query_branch, (), norm_scale, n_ctx)
     signals = lax.all_to_all(sent, CTX, 0, 0)
@@ -386,12 +387,13 @@
     partial = partial_sums(mixed, weights, at_k, False, partial, (near,))
     line_got = lax.all_to_all(partial, "l", 0, 0)
     partial = line_got.sum(0)
-    projected = across(pick(partial, at_m[0]), lambda h, m: (m, h))
-    projected = projected + across(pick(partial, 1 - at_m[0]), lambda h, m: (1 - m, h))
+    projected = fold(partial, at_m[0], "m", 1)
+    projected = swap_hm(projected)
 
     weight_part = outer(mixed, near, far, at_k)
     weight_part = lax.psum_scatter(weight_part, "y", scatter_dimension=0, tiled=True)
-    weight_grad = lax.psum_scatter(weight_part, "x", scatter_dimension=0, tiled=False) * norm_scale
+    weight_grad = fold(weight_part.reshape((2, 2) + weight_part.shape[1:]), at_x // 2, "x", 2)
+    weight_grad = fold(weight_grad, at_x % 2, "x", 1) * norm_scale
 
     mixed_grad = gradient(weights, near, far, at_k, n_ctx)
     grad_got = lax.all_to_all(after(mixed_grad, (line_got,)), CTX, 0, 0)

time: 265 us -> 273 us (1.030)
  the two profiles are of different devices: /device:TPU:1 before, /device:TPU:32 now
where the time goes in v10:
time: 273 us; the launch traced here: 272 us
  starting transfers between devices  114 us (42%)
  waiting for transfers between devices  105 us (38%)
  between operations  16.3 us (6%)
  local copies, waits for them, and re-layouts  15.9 us (6%)
  Pallas kernels  11.8 us (4%)
  other arithmetic  4.59 us (2%)
  matrix products  4.25 us (2%)
    all_to_all x1, waiting for transfers between devices, local(): signals = lax.all_to_all(sent, CTX, 0, 0)  30.2 us
    ppermute x1, starting transfers between devices, local(): cot_swap = lax.ppermute(cot_same, 'm', [(0, 1), (1, 0)])  26.1 us
    ppermute x3, waiting for transfers between devices, fold(): return pick(pair, at) + lax.ppermute(pick(pair, 1 - at), axis, pairs)  21.8 us
    all_to_all x1, starting transfers between devices, local(): back = lax.all_to_all(back, CTX, 0, 0)  21.2 us
    all_to_all x1, starting transfers between devices, local(): signals = lax.all_to_all(sent, CTX, 0, 0)  19.7 us
    unnamed x75, local copies, waits for them, and re-layouts  14.7 us
    all_to_all x1, waiting for transfers between devices, local(): back = lax.all_to_all(back, CTX, 0, 0)  14.5 us
    ppermute x3, starting transfers between devices, fold(): return pick(pair, at) + lax.ppermute(pick(pair, 1 - at), axis, pairs)  13 us
  transfers between devices with their start and end apart: 17, of which 11 were waited for; matrix products, arithmetic and copies ran while one was open for 4% of the time, Pallas kernels for 3%

profile of v10, /device:TPU:32, one launch (start us, length us, event | category | flops | bytes accessed | tf_op | source)
XLA Modules:
  0.0 272.1 jit_solution(17527391472364980820)
XLA Ops:
  8.0 0.9 copy-done.13
  8.9 0.9 copy-done.15
  9.8 0.9 copy-done.17
  10.7 0.9 copy-done.18
  11.6 0.9 shard_map.180
  12.5 19.7 %all-to-all-start = ((f32[32,24,128]{2,1,0:T(8,128)}), f32[32,24,128]{2,1,0:T(8,128)S(1)}, u32[]{:S(2)}, u32[]{:S(2)}) async-start(f32[32,24,128]{2,1,0:T(8,128)} %shard_map.180), calls=%async_computation | async-start | bytes 786432 | tf_op jit(solution)/shard_map/all_to_all | solution.py:368
  33.7 30.2 %all-to-all-done.refs_2_ = f32[32,24,128]{2,1,0:T(8,128)S(1)} async-done(((f32[32,24,128]{2,1,0:T(8,128)}), f32[32,24,128]{2,1,0:T(8,128)S(1)}, u32[]{:S(2)}, u32[]{:S(2)}) %all-to-all-start) | async-done | bytes 393248 | tf_op jit(solution)/shard_map/all_to_all | solution.py:368
  65.6 0.8 fusion.35
  68.1 4.1 %all-to-all-start.1 = ((f32[32,2,8,128]{3,2,1,0:T(8,128)}), f32[32,2,8,128]{3,2,1,0:T(8,128)S(1)}, u32[]{:S(2)}, u32[]{:S(2)}) async-start(f32[32,2,8,128]{3,2,1,0:T(8,128)} %shard_map.181), calls=%async_computation.1 | async-start | bytes 524288 | tf_op jit(solution)/shard_map/all_to_all | solution.py:379
  72.8 26.1 %collective-permute-start.3 = (f32[128,256]{1,0:T(8,128)S(1)}, f32[128,256]{1,0:T(8,128)S(1)}, u32[]{:S(2)}, u32[]{:S(2)}) collective-permute-start(f32[128,256]{1,0:T(8,128)S(1)} %collective-permute-done.2.same), channel_id=1, source_target_pairs={{0,8},{8,0},{1,9},{9,1},{2,10},{10,2},{3,11},{11,3},{4,12},{12,4},... | collective-permute-start | bytes 393224 | tf_op jit(solution)/shard_map/ppermute | solution.py:365
  99.0 5.9 %collective-permute-done.3.swap = f32[128,256]{1,0:T(8,128)S(1)} collective-permute-done((f32[128,256]{1,0:T(8,128)S(1)}, f32[128,256]{1,0:T(8,128)S(1)}, u32[]{:S(2)}, u32[]{:S(2)}) %collective-permute-start.3) | collective-permute-done | bytes 131104 | tf_op jit(solution)/shard_map/ppermute | solution.py:365
  104.8 1.0 shard_map.183
  105.9 3.5 %all-to-all-start.2 = ((f32[4,2,128,256]{3,2,1,0:T(8,128)}), f32[4,2,128,256]{3,2,1,0:T(8,128)S(1)}, u32[]{:S(2)}, u32[]{:S(2)}) async-start(f32[4,2,128,256]{3,2,1,0:T(8,128)} %shard_map.183), calls=%async_computation.2 | async-start | bytes 2097152 | tf_op jit(solution)/shard_map/all_to_all | solution.py:382
  109.4 1.6 copy-done
  111.0 1.4 shard_map.182
  112.5 2.1 collective-permute-start.1
  114.6 2.4 collective-permute-start
  117.0 1.5 collective-permute-done
  118.5 1.1 pad_maximum_fusion.refs_0_
  119.6 13.0 %all-to-all-done.2.refs_1_.near = f32[4,2,128,256]{3,2,1,0:T(8,128)S(1)} async-done(((f32[4,2,128,256]{3,2,1,0:T(8,128)}), f32[4,2,128,256]{3,2,1,0:T(8,128)S(1)}, u32[]{:S(2)}, u32[]{:S(2)}) %all-to-all-start.2) | async-done | bytes 1048608 | tf_op jit(solution)/shard_map/all_to_all | solution.py:382
  132.5 1.2 copy-done.8
  133.8 1.4 shard_map.184
  135.2 1.0 copy-done.7
  136.2 6.7 %all-to-all-start.3 = ((f32[4,2,128,256]{3,2,1,0:T(8,128)}), f32[4,2,128,256]{3,2,1,0:T(8,128)}, u32[]{:S(2)}, u32[]{:S(2)}) async-start(f32[4,2,128,256]{3,2,1,0:T(8,128)} %copy-done.7), calls=%async_computation.3 | async-start | bytes 2097152 | tf_op jit(solution)/shard_map/all_to_all | solution.py:388
  142.9 1.9 collective-permute-start.6
  144.8 2.6 collective-permute-done.6.far
  147.4 1.7 shard_map.187
  149.1 1.3 copy-done.2
  150.5 1.0 copy-done.5
  151.5 1.2 copy-done.6
  152.7 2.0 shard_map.185.value
  155.5 9.4 %all-to-all-done.3.refs_0_ = f32[4,2,128,256]{3,2,1,0:T(8,128)} async-done(((f32[4,2,128,256]{3,2,1,0:T(8,128)}), f32[4,2,128,256]{3,2,1,0:T(8,128)}, u32[]{:S(2)}, u32[]{:S(2)}) %all-to-all-start.3) | async-done | bytes 1048608 | tf_op jit(solution)/shard_map/all_to_all | solution.py:388
  164.9 0.9 copy-done.12
  166.5 11.8 %all-to-all-start.4 = ((f32[32,2,8,128]{3,2,1,0:T(8,128)}), f32[32,2,8,128]{3,2,1,0:T(8,128)S(1)}, u32[]{:S(2)}, u32[]{:S(2)}) async-start(f32[32,2,8,128]{3,2,1,0:T(8,128)} %shard_map.186), calls=%async_computation.4 | async-start | bytes 524288 | tf_op jit(solution)/shard_map/all_to_all | solution.py:399
  178.4 1.4 reduce_sum.18
  179.8 5.2 %collective-permute-start.4 = (f32[128,256]{1,0:T(8,128)S(1)}, f32[128,256]{1,0:T(8,128)S(1)}, u32[]{:S(2)}, u32[]{:S(2)}) collective-permute-start(f32[128,256]{1,0:T(8,128)S(1)} %dynamic-slice_bitcast_fusion.2), channel_id=1, source_target_pairs={{0,8},{8,0},{1,9},{9,1},{2,10},{10,2},{3,11},{11,3},{4,12},{12,4},... | collective-permute-start | bytes 393224 | tf_op jit(solution)/shard_map/ppermute | solution.py:344
  184.9 11.2 %collective-permute-done.4 = f32[128,256]{1,0:T(8,128)S(1)} collective-permute-done((f32[128,256]{1,0:T(8,128)S(1)}, f32[128,256]{1,0:T(8,128)S(1)}, u32[]{:S(2)}, u32[]{:S(2)}) %collective-permute-start.4) | collective-permute-done | bytes 131104 | tf_op jit(solution)/shard_map/ppermute | solution.py:344
  197.0 5.7 %all-to-all-done.4 = f32[32,2,8,128]{3,2,1,0:T(8,128)S(1)} async-done(((f32[32,2,8,128]{3,2,1,0:T(8,128)}), f32[32,2,8,128]{3,2,1,0:T(8,128)S(1)}, u32[]{:S(2)}, u32[]{:S(2)}) %all-to-all-start.4) | async-done | bytes 262176 | tf_op jit(solution)/shard_map/all_to_all | solution.py:399
  204.3 0.9 fusion
  206.0 1.0 copy-done.9
  207.0 1.0 shard_map.188
  208.0 21.2 %all-to-all-start.5 = ((f32[32,32,128]{2,1,0:T(8,128)}), f32[32,32,128]{2,1,0:T(8,128)S(1)}, u32[]{:S(2)}, u32[]{:S(2)}) async-start(f32[32,32,128]{2,1,0:T(8,128)} %shard_map.188), calls=%async_computation.6 | async-start | bytes 1048576 | tf_op jit(solution)/shard_map/all_to_all | solution.py:412
  229.3 5.2 %collective-permute-start.7 = (f32[2,256,128]{2,1,0:T(8,128)S(1)}, f32[2,256,128]{2,1,0:T(8,128)S(1)}, u32[]{:S(2)}, u32[]{:S(2)}) collective-permute-start(f32[2,256,128]{2,1,0:T(8,128)S(1)} %dynamic-slice_bitcast_fusion), channel_id=1, source_target_pairs={{0,32},{16,48},{32,0},{48,16},{1,33},{17,49},{33,1},{49,17},{2,34}... | collective-permute-start | bytes 786440 | tf_op jit(solution)/shard_map/ppermute | solution.py:344
  234.5 6.5 %collective-permute-done.7 = f32[2,256,128]{2,1,0:T(8,128)S(1)} collective-permute-done((f32[2,256,128]{2,1,0:T(8,128)S(1)}, f32[2,256,128]{2,1,0:T(8,128)S(1)}, u32[]{:S(2)}, u32[]{:S(2)}) %collective-permute-start.7) | collective-permute-done | bytes 262176 | tf_op jit(solution)/shard_map/ppermute | solution.py:344
  241.1 2.6 collective-permute-start.8
  243.7 4.2 %collective-permute-done.8 = f32[256,128]{1,0:T(8,128)S(1)} collective-permute-done((f32[256,128]{1,0:T(8,128)S(1)}, f32[256,128]{1,0:T(8,128)S(1)}, u32[]{:S(2)}, u32[]{:S(2)}) %collective-permute-start.8) | collective-permute-done | bytes 131104 | tf_op jit(solution)/shard_map/ppermute | solution.py:344
  248.6 14.5 %all-to-all-done.5.refs_0_ = f32[32,32,128]{2,1,0:T(8,128)S(1)} async-done(((f32[32,32,128]{2,1,0:T(8,128)}), f32[32,32,128]{2,1,0:T(8,128)S(1)}, u32[]{:S(2)}, u32[]{:S(2)}) %all-to-all-start.5) | async-done | bytes 524320 | tf_op jit(solution)/shard_map/all_to_all | solution.py:412
  263.1 0.9 shard_map.189
  (109 shorter events, 11.3 us)
Async XLA Ops:
  8.0 56.7 %copy-start.27 = (f32[33,128]{1,0:T(8,128)S(1)}, f32[33,128]{1,0:T(8,128)}, u32[]{:S(2)}) copy-start(f32[33,128]{1,0:T(8,128)} %constant.95.clone) | copy-start | bytes 50692
  11.6 52.4 %copy-start.32 = (f32[66,32,1]{0,1,2:T(8,128)S(1)}, f32[66,32,1]{0,1,2:T(8,128)}, u32[]{:S(2)}) copy-start(f32[66,32,1]{0,1,2:T(8,128)} %constant.100) | copy-start | bytes 25348
  11.6 53.1 %copy-start.29 = (f32[33,128]{1,0:T(8,128)S(1)}, f32[33,128]{1,0:T(8,128)}, u32[]{:S(2)}) copy-start(f32[33,128]{1,0:T(8,128)} %constant.94.clone) | copy-start | bytes 50692
  12.5 51.4 %all-to-all-start = ((f32[32,24,128]{2,1,0:T(8,128)}), f32[32,24,128]{2,1,0:T(8,128)S(1)}, u32[]{:S(2)}, u32[]{:S(2)}) async-start(f32[32,24,128]{2,1,0:T(8,128)} %shard_map.180), calls=%async_computation | async-start | bytes 786432 | tf_op jit(solution)/shard_map/all_to_all | solution.py:368
  32.2 32.6 %copy-start.21 = (f32[256,256,1]{1,0,2:T(8,128)S(1)}, f32[256,256,1]{1,0,2:T(8,128)}, u32[]{:S(2)}) copy-start(f32[256,256,1]{1,0,2:T(8,128)} %constant.101) | copy-start | bytes 786436
  32.2 77.2 %all-gather.2.cloned.1.call-start = ((), (), s32[]{:S(2)}) async-start(), calls=%async_computation.7 | async-start | bytes 2228224 | tf_op jit(solution)/shard_map/all_gather | solution.py:362
  33.7 33.5 %copy-start.34 = (f32[8]{0:T(128)}, f32[8]{0:T(128)S(1)}, u32[]{:S(2)}) copy-start(f32[8]{0:T(128)S(1)} %dynamic_slice.24) | copy-start | bytes 100
  64.0 3.3 %copy-start.3 = (f32[32,24,128]{2,1,0:T(8,128)}, f32[32,24,128]{2,1,0:T(8,128)S(1)}, u32[]{:S(2)}) copy-start(f32[32,24,128]{2,1,0:T(8,128)S(1)} %all-to-all-done.refs_2_) | copy-start | bytes 1179652
  64.8 1.6 copy-start.19
  64.9 2.0 copy-start.31
  66.4 5.7 %copy-start.36 = (f32[128,256]{1,0:T(8,128)S(1)}, f32[128,256]{1,0:T(8,128)}, u32[]{:S(2)}) copy-start(f32[128,256]{1,0:T(8,128)} %param.19) | copy-start | bytes 393220
  68.1 36.7 %all-to-all-start.1 = ((f32[32,2,8,128]{3,2,1,0:T(8,128)}), f32[32,2,8,128]{3,2,1,0:T(8,128)S(1)}, u32[]{:S(2)}, u32[]{:S(2)}) async-start(f32[32,2,8,128]{3,2,1,0:T(8,128)} %shard_map.181), calls=%async_computation.1 | async-start | bytes 524288 | tf_op jit(solution)/shard_map/all_to_all | solution.py:379
  72.2 0.7 collective-permute-start.2
  72.8 32.0 %collective-permute-start.3 = (f32[128,256]{1,0:T(8,128)S(1)}, f32[128,256]{1,0:T(8,128)S(1)}, u32[]{:S(2)}, u32[]{:S(2)}) collective-permute-start(f32[128,256]{1,0:T(8,128)S(1)} %collective-permute-done.2.same), channel_id=1, source_target_pairs={{0,8},{8,0},{1,9},{9,1},{2,10},{10,2},{3,11},{11,3},{4,12},{12,4},... | collective-permute-start | bytes 393224 | tf_op jit(solution)/shard_map/ppermute | solution.py:365
  105.9 26.7 %all-to-all-start.2 = ((f32[4,2,128,256]{3,2,1,0:T(8,128)}), f32[4,2,128,256]{3,2,1,0:T(8,128)S(1)}, u32[]{:S(2)}, u32[]{:S(2)}) async-start(f32[4,2,128,256]{3,2,1,0:T(8,128)} %shard_map.183), calls=%async_computation.2 | async-start | bytes 2097152 | tf_op jit(solution)/shard_map/all_to_all | solution.py:382
  109.4 1.6 copy-start
  112.4 20.1 %copy-start.1 = (f32[256,2048]{1,0:T(8,128)S(1)}, f32[256,2048]{1,0:T(8,128)}, u32[]{:S(2)}) copy-start(f32[256,2048]{1,0:T(8,128)} %all-gather.2.cloned.1.call-done.weight.near_w.far_w) | copy-start | bytes 6291460
  112.5 4.5 %collective-permute-start.1 = (f32[2,2,128,256]{3,2,1,0:T(8,128)S(1)}, f32[2,2,128,256]{3,2,1,0:T(8,128)S(1)}, u32[]{:S(2)}, u32[]{:S(2)}) collective-permute-start(f32[2,2,128,256]{3,2,1,0:T(8,128)S(1)} %get-tuple-element.20), channel_id=1, source_target_pairs={{0,1},{1,0},{2,3},{3,2},{4,5},{5,4},{6,7},{7,6},{8,9},{9,8},{10,11... | collective-permute-start | bytes 1572872 | tf_op jit(solution)/shard_map/ppermute | solution.py:339
  114.6 3.9 %collective-permute-start = (f32[2,2,128,256]{3,2,1,0:T(8,128)S(1)}, f32[2,2,128,256]{3,2,1,0:T(8,128)S(1)}, u32[]{:S(2)}, u32[]{:S(2)}) collective-permute-start(f32[2,2,128,256]{3,2,1,0:T(8,128)S(1)} %get-tuple-element.19), channel_id=1, source_target_pairs={{0,1},{1,0},{2,3},{3,2},{4,5},{5,4},{6,7},{7,6},{8,9},{9,8},{10,11... | collective-permute-start | bytes 1572872 | tf_op jit(solution)/shard_map/ppermute | solution.py:339
  132.5 1.2 copy-start.8
  135.2 1.0 copy-start.7
  136.2 28.7 %all-to-all-start.3 = ((f32[4,2,128,256]{3,2,1,0:T(8,128)}), f32[4,2,128,256]{3,2,1,0:T(8,128)}, u32[]{:S(2)}, u32[]{:S(2)}) async-start(f32[4,2,128,256]{3,2,1,0:T(8,128)} %copy-done.7), calls=%async_computation.3 | async-start | bytes 2097152 | tf_op jit(solution)/shard_map/all_to_all | solution.py:388
  142.9 63.0 %reduce-scatter.2.cloned.1.call-start = ((), (), s32[]{:S(2)}) async-start(), calls=%async_computation.8 | async-start | bytes 2621440 | tf_op jit(solution)/shard_map/reduce_scatter | solution.py:394
  142.9 4.5 %collective-permute-start.6 = (f32[4,2,128,256]{3,2,1,0:T(8,128)S(1)}, f32[4,2,128,256]{3,2,1,0:T(8,128)S(1)}, u32[]{:S(2)}, u32[]{:S(2)}) collective-permute-start(f32[4,2,128,256]{3,2,1,0:T(8,128)S(1)} %all-to-all-done.2.refs_1_.near), channel_id=1, source_target_pairs={{0,1},{1,0},{2,3},{3,2},{4,5},{5,4},{6,7},{7,6},{8,9},{9,8},{10,11... | collective-permute-start | bytes 3145736 | tf_op jit(solution)/shard_map/ppermute | solution.py:339
  149.1 1.3 copy-start.2
  150.5 1.0 copy-start.5
  151.5 1.2 copy-start.6
  155.5 47.3 %copy-start.4 = (f32[32,24,128]{2,1,0:T(8,128)S(1)}, f32[32,24,128]{2,1,0:T(8,128)}, u32[]{:S(2)}) copy-start(f32[32,24,128]{2,1,0:T(8,128)} %copy-done.3) | copy-start | bytes 1179652
  166.5 36.3 %copy-start.33 = (f32[66,32,1]{0,1,2:T(8,128)S(1)}, f32[66,32,1]{0,1,2:T(8,128)}, u32[]{:S(2)}) copy-start(f32[66,32,1]{0,1,2:T(8,128)} %constant.100) | copy-start | bytes 25348
  166.5 36.2 %all-to-all-start.4 = ((f32[32,2,8,128]{3,2,1,0:T(8,128)}), f32[32,2,8,128]{3,2,1,0:T(8,128)S(1)}, u32[]{:S(2)}, u32[]{:S(2)}) async-start(f32[32,2,8,128]{3,2,1,0:T(8,128)} %shard_map.186), calls=%async_computation.4 | async-start | bytes 524288 | tf_op jit(solution)/shard_map/all_to_all | solution.py:399
  178.3 25.0 %copy-start.28 = (f32[33,128]{1,0:T(8,128)S(1)}, f32[33,128]{1,0:T(8,128)}, u32[]{:S(2)}) copy-start(f32[33,128]{1,0:T(8,128)} %constant.95.clone) | copy-start | bytes 50692
  178.3 24.9 %copy-start.30 = (f32[33,128]{1,0:T(8,128)S(1)}, f32[33,128]{1,0:T(8,128)}, u32[]{:S(2)}) copy-start(f32[33,128]{1,0:T(8,128)} %constant.94.clone) | copy-start | bytes 50692
  178.4 25.0 %copy-start.22 = (f32[256,256,1]{1,0,2:T(8,128)S(1)}, f32[256,256,1]{1,0,2:T(8,128)}, u32[]{:S(2)}) copy-start(f32[256,256,1]{1,0,2:T(8,128)} %constant.101) | copy-start | bytes 786436
  179.8 16.4 %collective-permute-start.4 = (f32[128,256]{1,0:T(8,128)S(1)}, f32[128,256]{1,0:T(8,128)S(1)}, u32[]{:S(2)}, u32[]{:S(2)}) collective-permute-start(f32[128,256]{1,0:T(8,128)S(1)} %dynamic-slice_bitcast_fusion.2), channel_id=1, source_target_pairs={{0,8},{8,0},{1,9},{9,1},{2,10},{10,2},{3,11},{11,3},{4,12},{12,4},... | collective-permute-start | bytes 393224 | tf_op jit(solution)/shard_map/ppermute | solution.py:344
  196.1 7.7 %copy-start.23 = (f32[33,8,128]{2,1,0:T(8,128)S(1)}, f32[33,8,128]{2,1,0:T(8,128)}, u32[]{:S(2)}) copy-start(f32[33,8,128]{2,1,0:T(8,128)} %get-tuple-element.27) | copy-start | bytes 405508
  196.1 7.7 %copy-start.24 = (f32[33,8,128]{2,1,0:T(8,128)S(1)}, f32[33,8,128]{2,1,0:T(8,128)}, u32[]{:S(2)}) copy-start(f32[33,8,128]{2,1,0:T(8,128)} %get-tuple-element.30) | copy-start | bytes 405508
  196.2 7.7 %copy-start.25 = (f32[33,8,128]{2,1,0:T(8,128)S(1)}, f32[33,8,128]{2,1,0:T(8,128)}, u32[]{:S(2)}) copy-start(f32[33,8,128]{2,1,0:T(8,128)} %get-tuple-element.31) | copy-start | bytes 405508
  196.2 7.7 %copy-start.26 = (f32[33,8,128]{2,1,0:T(8,128)S(1)}, f32[33,8,128]{2,1,0:T(8,128)}, u32[]{:S(2)}) copy-start(f32[33,8,128]{2,1,0:T(8,128)} %get-tuple-element.32) | copy-start | bytes 405508
  196.2 9.7 %collective-permute-start.5 = (f32[128,256]{1,0:T(8,128)S(1)}, f32[128,256]{1,0:T(8,128)S(1)}, u32[]{:S(2)}, u32[]{:S(2)}) collective-permute-start(f32[128,256]{1,0:T(8,128)S(1)} %bitcast_add_fusion.2), channel_id=1, source_target_pairs={{0,0},{8,256},{256,8},{264,264},{1,1},{9,257},{257,9},{265,265},{2... | collective-permute-start | bytes 393224 | tf_op jit(solution)/shard_map/ppermute | solution.py:335
  203.3 1.0 copy-start.20
  204.3 1.6 copy-start.35
  206.0 1.0 copy-start.9
  207.0 22.2 %copy-start.10 = (f32[4,256,128]{2,1,0:T(8,128)S(1)}, f32[4,256,128]{2,1,0:T(8,128)}, u32[]{:S(2)}) copy-start(f32[4,256,128]{2,1,0:T(8,128)} %reduce-scatter.2.cloned.1.call-done.refs_7_) | copy-start | bytes 1572868
  208.0 55.1 %copy-start.14 = (f32[128,256]{1,0:T(8,128)S(1)}, f32[128,256]{1,0:T(8,128)}, u32[]{:S(2)}) copy-start(f32[128,256]{1,0:T(8,128)} %refs_1_.3) | copy-start | bytes 393220
  208.0 55.1 %copy-start.16 = (f32[128,256]{1,0:T(8,128)S(1)}, f32[128,256]{1,0:T(8,128)}, u32[]{:S(2)}) copy-start(f32[128,256]{1,0:T(8,128)} %refs_2_.3) | copy-start | bytes 393220
  208.0 55.1 %all-to-all-start.5 = ((f32[32,32,128]{2,1,0:T(8,128)}), f32[32,32,128]{2,1,0:T(8,128)S(1)}, u32[]{:S(2)}, u32[]{:S(2)}) async-start(f32[32,32,128]{2,1,0:T(8,128)} %shard_map.188), calls=%async_computation.6 | async-start | bytes 1048576 | tf_op jit(solution)/shard_map/all_to_all | solution.py:412
  229.3 11.7 %collective-permute-start.7 = (f32[2,256,128]{2,1,0:T(8,128)S(1)}, f32[2,256,128]{2,1,0:T(8,128)S(1)}, u32[]{:S(2)}, u32[]{:S(2)}) collective-permute-start(f32[2,256,128]{2,1,0:T(8,128)S(1)} %dynamic-slice_bitcast_fusion), channel_id=1, source_target_pairs={{0,32},{16,48},{32,0},{48,16},{1,33},{17,49},{33,1},{49,17},{2,34}... | collective-permute-start | bytes 786440 | tf_op jit(solution)/shard_map/ppermute | solution.py:344
  241.1 6.9 %collective-permute-start.8 = (f32[256,128]{1,0:T(8,128)S(1)}, f32[256,128]{1,0:T(8,128)S(1)}, u32[]{:S(2)}, u32[]{:S(2)}) collective-permute-start(f32[256,128]{1,0:T(8,128)S(1)} %dynamic-slice_bitcast_fusion.1), channel_id=1, source_target_pairs={{0,16},{16,0},{32,48},{48,32},{1,17},{17,1},{33,49},{49,33},{2,18}... | collective-permute-start | bytes 393224 | tf_op jit(solution)/shard_map/ppermute | solution.py:344
  (6 other events, 5.3 us)
Sparse Core Ops, SparseCore 0:
  36.1 66.2 all-gather.1
Sparse Core Ops, SparseCore 1:
  151.6 33.9 reduce-scatter.1

commit v11 on v9

--- a/solution.py
+++ b/solution.py
@@ -344,6 +344,11 @@
     return lax.ppermute(block, "k", [(0, 1), (1, 0)])
 
 
+def fold(pair, at, axis, apart):
+    pairs = [(here, here ^ apart) for here in range(lax.axis_size(axis))]
+    return pick(pair, at) + lax.ppermute(pick(pair, 1 - at), axis, pairs)
+
+
 def pick(pair, at):
     return lax.dynamic_index_in_dim(pair, at, 0, False)
 
@@ -356,6 +361,7 @@
     norm_scale = 1.0 / math.sqrt(seq_len)
     tab = tables(seq_len)
     at_m, at_k = (lax.axis_index(name).astype(jnp.int32).reshape(1) for name in ("m", "k"))
+    at_x = lax.axis_index("x")
     at_ctx = lax.axis_index(CTX)
 
     weights = lax.all_gather(out_weight, PLANE, axis=1, tiled=True)
@@ -391,7 +397,8 @@
 
     weight_part = outer(mixed, near, far, at_k)
     weight_part = lax.psum_scatter(weight_part, "y", scatter_dimension=0, tiled=True)
-    weight_grad = lax.psum_scatter(weight_part, "x", scatter_dimension=0, tiled=False) * norm_scale
+    weight_grad = fold(weight_part.reshape((2, 2) + weight_part.shape[1:]), at_x // 2, "x", 2)
+    weight_grad = fold(weight_grad, at_x % 2, "x", 1) * norm_scale
 
     mixed_grad = gradient(weights, near, far, at_k, n_ctx)
     grad_got = lax.all_to_all(after(mixed_grad, (line_got,)), CTX, 0, 0)

time: 265 us -> 255 us (0.962)
  the two profiles are of different devices: /device:TPU:1 before, /device:TPU:129 now
where the time goes in v11:
time: 255 us; the launch traced here: 253 us
  waiting for transfers between devices  104 us (41%)
  starting transfers between devices  98.7 us (39%)
  between operations  16.2 us (6%)
  local copies, waits for them, and re-layouts  13.6 us (5%)
  Pallas kernels  11.8 us (5%)
  other arithmetic  4.55 us (2%)
  matrix products  4.25 us (2%)
    ppermute x4, starting transfers between devices, across(): return lax.ppermute(block, ('h', 'm'), pairs)  26.9 us
    ppermute x4, waiting for transfers between devices, across(): return lax.ppermute(block, ('h', 'm'), pairs)  26.8 us
    all_to_all x1, waiting for transfers between devices, local(): signals = lax.all_to_all(sent, CTX, 0, 0)  23.4 us
    all_to_all x1, starting transfers between devices, local(): near = lax.all_to_all(near, 'l', 0, 0)  15.6 us
    all_to_all x1, starting transfers between devices, local(): signals = lax.all_to_all(sent, CTX, 0, 0)  15.5 us
    unnamed x72, local copies, waits for them, and re-layouts  12.5 us
    all_to_all x1, waiting for transfers between devices, local(): line_got = lax.all_to_all(partial, 'l', 0, 0)  12.3 us
    all_to_all x1, waiting for transfers between devices, local(): near = lax.all_to_all(near, 'l', 0, 0)  12 us
  transfers between devices with their start and end apart: 17, of which 12 were waited for; matrix products, arithmetic and copies ran while one was open for 4% of the time, Pallas kernels for 3%

profile of v11, /device:TPU:129, one launch (start us, length us, event | category | flops | bytes accessed | tf_op | source)
XLA Modules:
  0.0 252.9 jit_solution(15465574829228417773)
XLA Ops:
  8.0 0.9 copy-done.12
  8.9 0.9 copy-done.14
  9.8 0.9 copy-done.16
  10.7 0.9 copy-done.17
  11.6 0.9 shard_map.180
  12.5 15.5 %all-to-all-start = ((f32[32,24,128]{2,1,0:T(8,128)}), f32[32,24,128]{2,1,0:T(8,128)S(1)}, u32[]{:S(2)}, u32[]{:S(2)}) async-start(f32[32,24,128]{2,1,0:T(8,128)} %shard_map.180), calls=%async_computation | async-start | bytes 786432 | tf_op jit(solution)/shard_map/all_to_all | solution.py:373
  29.6 23.4 %all-to-all-done.refs_2_ = f32[32,24,128]{2,1,0:T(8,128)S(1)} async-done(((f32[32,24,128]{2,1,0:T(8,128)}), f32[32,24,128]{2,1,0:T(8,128)S(1)}, u32[]{:S(2)}, u32[]{:S(2)}) %all-to-all-start) | async-done | bytes 393248 | tf_op jit(solution)/shard_map/all_to_all | solution.py:373
  57.1 4.5 %all-to-all-start.1 = ((f32[32,2,8,128]{3,2,1,0:T(8,128)}), f32[32,2,8,128]{3,2,1,0:T(8,128)S(1)}, u32[]{:S(2)}, u32[]{:S(2)}) async-start(f32[32,2,8,128]{3,2,1,0:T(8,128)} %shard_map.181), calls=%async_computation.1 | async-start | bytes 524288 | tf_op jit(solution)/shard_map/all_to_all | solution.py:384
  61.7 2.8 %collective-permute-start.2 = (f32[128,256]{1,0:T(8,128)S(1)}, f32[128,256]{1,0:T(8,128)S(1)}, u32[]{:S(2)}, u32[]{:S(2)}) collective-permute-start(f32[128,256]{1,0:T(8,128)S(1)} %copy-done.35), channel_id=1, source_target_pairs={{0,0},{8,256},{256,8},{264,264},{1,1},{9,257},{257,9},{265,265},{2... | collective-permute-start | bytes 393224 | tf_op jit(solution)/shard_map/ppermute | solution.py:340
  64.4 9.8 %collective-permute-start.3 = (f32[128,256]{1,0:T(8,128)S(1)}, f32[128,256]{1,0:T(8,128)S(1)}, u32[]{:S(2)}, u32[]{:S(2)}) collective-permute-start(f32[128,256]{1,0:T(8,128)S(1)} %copy-done.35), channel_id=1, source_target_pairs={{0,8},{8,264},{256,0},{264,256},{1,9},{9,265},{257,1},{265,257},{2... | collective-permute-start | bytes 393224 | tf_op jit(solution)/shard_map/ppermute | solution.py:340
  74.2 3.8 %collective-permute-done.2.same = f32[128,256]{1,0:T(8,128)S(1)} collective-permute-done((f32[128,256]{1,0:T(8,128)S(1)}, f32[128,256]{1,0:T(8,128)S(1)}, u32[]{:S(2)}, u32[]{:S(2)}) %collective-permute-start.2) | collective-permute-done | bytes 131104 | tf_op jit(solution)/shard_map/ppermute | solution.py:340
  78.0 3.0 %collective-permute-done.3.swap = f32[128,256]{1,0:T(8,128)S(1)} collective-permute-done((f32[128,256]{1,0:T(8,128)S(1)}, f32[128,256]{1,0:T(8,128)S(1)}, u32[]{:S(2)}, u32[]{:S(2)}) %collective-permute-start.3) | collective-permute-done | bytes 131104 | tf_op jit(solution)/shard_map/ppermute | solution.py:340
  81.0 1.0 shard_map.183
  82.0 15.6 %all-to-all-start.2 = ((f32[4,2,128,256]{3,2,1,0:T(8,128)}), f32[4,2,128,256]{3,2,1,0:T(8,128)S(1)}, u32[]{:S(2)}, u32[]{:S(2)}) async-start(f32[4,2,128,256]{3,2,1,0:T(8,128)} %shard_map.183), calls=%async_computation.2 | async-start | bytes 2097152 | tf_op jit(solution)/shard_map/all_to_all | solution.py:387
  97.6 1.6 all-gather.2.cloned.1.call-done.weight.near_w.far_w
  99.2 1.6 copy-done
  100.8 1.4 shard_map.182
  102.3 3.6 %collective-permute-start.1 = (f32[2,2,128,256]{3,2,1,0:T(8,128)S(1)}, f32[2,2,128,256]{3,2,1,0:T(8,128)S(1)}, u32[]{:S(2)}, u32[]{:S(2)}) collective-permute-start(f32[2,2,128,256]{3,2,1,0:T(8,128)S(1)} %get-tuple-element.20), channel_id=1, source_target_pairs={{0,1},{1,0},{2,3},{3,2},{4,5},{5,4},{6,7},{7,6},{8,9},{9,8},{10,11... | collective-permute-start | bytes 1572872 | tf_op jit(solution)/shard_map/ppermute | solution.py:344
  105.9 1.9 collective-permute-start
  107.9 1.9 collective-permute-done
  109.7 1.1 pad_maximum_fusion.refs_0_
  110.8 12.0 %all-to-all-done.2.refs_1_.near = f32[4,2,128,256]{3,2,1,0:T(8,128)S(1)} async-done(((f32[4,2,128,256]{3,2,1,0:T(8,128)}), f32[4,2,128,256]{3,2,1,0:T(8,128)S(1)}, u32[]{:S(2)}, u32[]{:S(2)}) %all-to-all-start.2) | async-done | bytes 1048608 | tf_op jit(solution)/shard_map/all_to_all | solution.py:387
  122.8 1.2 copy-done.8
  124.1 1.4 shard_map.184
  125.5 1.0 copy-done.7
  126.5 4.2 %all-to-all-start.3 = ((f32[4,2,128,256]{3,2,1,0:T(8,128)}), f32[4,2,128,256]{3,2,1,0:T(8,128)}, u32[]{:S(2)}, u32[]{:S(2)}) async-start(f32[4,2,128,256]{3,2,1,0:T(8,128)} %copy-done.7), calls=%async_computation.3 | async-start | bytes 2097152 | tf_op jit(solution)/shard_map/all_to_all | solution.py:393
  130.8 3.4 %collective-permute-start.6 = (f32[4,2,128,256]{3,2,1,0:T(8,128)S(1)}, f32[4,2,128,256]{3,2,1,0:T(8,128)S(1)}, u32[]{:S(2)}, u32[]{:S(2)}) collective-permute-start(f32[4,2,128,256]{3,2,1,0:T(8,128)S(1)} %all-to-all-done.2.refs_1_.near), channel_id=1, source_target_pairs={{0,1},{1,0},{2,3},{3,2},{4,5},{5,4},{6,7},{7,6},{8,9},{9,8},{10,11... | collective-permute-start | bytes 3145736 | tf_op jit(solution)/shard_map/ppermute | solution.py:344
  134.2 2.3 collective-permute-done.6.far
  136.4 1.7 shard_map.187
  138.1 1.3 copy-done.2
  139.4 1.0 copy-done.5
  140.5 1.2 copy-done.6
  141.7 2.0 shard_map.185.value
  143.7 12.3 %all-to-all-done.3.refs_0_ = f32[4,2,128,256]{3,2,1,0:T(8,128)} async-done(((f32[4,2,128,256]{3,2,1,0:T(8,128)}), f32[4,2,128,256]{3,2,1,0:T(8,128)}, u32[]{:S(2)}, u32[]{:S(2)}) %all-to-all-start.3) | async-done | bytes 1048608 | tf_op jit(solution)/shard_map/all_to_all | solution.py:393
  156.7 9.5 %all-to-all-start.4 = ((f32[32,2,8,128]{3,2,1,0:T(8,128)}), f32[32,2,8,128]{3,2,1,0:T(8,128)S(1)}, u32[]{:S(2)}, u32[]{:S(2)}) async-start(f32[32,2,8,128]{3,2,1,0:T(8,128)} %shard_map.186), calls=%async_computation.4 | async-start | bytes 524288 | tf_op jit(solution)/shard_map/all_to_all | solution.py:404
  166.3 1.3 reduce_sum.18
  167.6 12.5 %collective-permute-start.4 = (f32[128,256]{1,0:T(8,128)S(1)}, f32[128,256]{1,0:T(8,128)S(1)}, u32[]{:S(2)}, u32[]{:S(2)}) collective-permute-start(f32[128,256]{1,0:T(8,128)S(1)} %get-tuple-element.42), channel_id=1, source_target_pairs={{0,0},{8,256},{256,8},{264,264},{1,1},{9,257},{257,9},{265,265},{2... | collective-permute-start | bytes 393224 | tf_op jit(solution)/shard_map/ppermute | solution.py:340
  180.1 1.9 collective-permute-start.5
  182.1 20.1 %collective-permute-done.4 = f32[128,256]{1,0:T(8,128)S(1)} collective-permute-done((f32[128,256]{1,0:T(8,128)S(1)}, f32[128,256]{1,0:T(8,128)S(1)}, u32[]{:S(2)}, u32[]{:S(2)}) %collective-permute-start.4) | collective-permute-done | bytes 131104 | tf_op jit(solution)/shard_map/ppermute | solution.py:340
  203.8 0.9 fusion
  205.5 1.0 copy-done.9
  206.6 1.0 shard_map.188
  207.6 6.8 %all-to-all-start.5 = ((f32[32,32,128]{2,1,0:T(8,128)}), f32[32,32,128]{2,1,0:T(8,128)S(1)}, u32[]{:S(2)}, u32[]{:S(2)}) async-start(f32[32,32,128]{2,1,0:T(8,128)} %shard_map.188), calls=%async_computation.6 | async-start | bytes 1048576 | tf_op jit(solution)/shard_map/all_to_all | solution.py:417
  214.5 4.6 %collective-permute-start.7 = (f32[2,256,128]{2,1,0:T(8,128)S(1)}, f32[2,256,128]{2,1,0:T(8,128)S(1)}, u32[]{:S(2)}, u32[]{:S(2)}) collective-permute-start(f32[2,256,128]{2,1,0:T(8,128)S(1)} %dynamic-slice_bitcast_fusion), channel_id=1, source_target_pairs={{0,32},{16,48},{32,0},{48,16},{1,33},{17,49},{33,1},{49,17},{2,34}... | collective-permute-start | bytes 786440 | tf_op jit(solution)/shard_map/ppermute | solution.py:349
  219.2 7.0 %collective-permute-done.7 = f32[2,256,128]{2,1,0:T(8,128)S(1)} collective-permute-done((f32[2,256,128]{2,1,0:T(8,128)S(1)}, f32[2,256,128]{2,1,0:T(8,128)S(1)}, u32[]{:S(2)}, u32[]{:S(2)}) %collective-permute-start.7) | collective-permute-done | bytes 262176 | tf_op jit(solution)/shard_map/ppermute | solution.py:349
  226.2 1.9 collective-permute-start.8
  228.2 3.8 %collective-permute-done.8 = f32[256,128]{1,0:T(8,128)S(1)} collective-permute-done((f32[256,128]{1,0:T(8,128)S(1)}, f32[256,128]{1,0:T(8,128)S(1)}, u32[]{:S(2)}, u32[]{:S(2)}) %collective-permute-start.8) | collective-permute-done | bytes 131104 | tf_op jit(solution)/shard_map/ppermute | solution.py:349
  232.6 11.9 %all-to-all-done.5.refs_0_ = f32[32,32,128]{2,1,0:T(8,128)S(1)} async-done(((f32[32,32,128]{2,1,0:T(8,128)}), f32[32,32,128]{2,1,0:T(8,128)S(1)}, u32[]{:S(2)}, u32[]{:S(2)}) %all-to-all-start.5) | async-done | bytes 524320 | tf_op jit(solution)/shard_map/all_to_all | solution.py:417
  (106 shorter events, 10.3 us)
Async XLA Ops:
  8.0 45.7 %copy-start.26 = (f32[33,128]{1,0:T(8,128)S(1)}, f32[33,128]{1,0:T(8,128)}, u32[]{:S(2)}) copy-start(f32[33,128]{1,0:T(8,128)} %constant.95.clone) | copy-start | bytes 50692
  11.6 41.4 %copy-start.31 = (f32[66,32,1]{0,1,2:T(8,128)S(1)}, f32[66,32,1]{0,1,2:T(8,128)}, u32[]{:S(2)}) copy-start(f32[66,32,1]{0,1,2:T(8,128)} %constant.100) | copy-start | bytes 25348
  11.6 42.1 %copy-start.28 = (f32[33,128]{1,0:T(8,128)S(1)}, f32[33,128]{1,0:T(8,128)}, u32[]{:S(2)}) copy-start(f32[33,128]{1,0:T(8,128)} %constant.94.clone) | copy-start | bytes 50692
  12.5 40.4 %all-to-all-start = ((f32[32,24,128]{2,1,0:T(8,128)}), f32[32,24,128]{2,1,0:T(8,128)S(1)}, u32[]{:S(2)}, u32[]{:S(2)}) async-start(f32[32,24,128]{2,1,0:T(8,128)} %shard_map.180), calls=%async_computation | async-start | bytes 786432 | tf_op jit(solution)/shard_map/all_to_all | solution.py:373
  28.0 25.8 %copy-start.20 = (f32[256,256,1]{1,0,2:T(8,128)S(1)}, f32[256,256,1]{1,0,2:T(8,128)}, u32[]{:S(2)}) copy-start(f32[256,256,1]{1,0,2:T(8,128)} %constant.101) | copy-start | bytes 786436
  28.1 71.2 %all-gather.2.cloned.1.call-start = ((), (), s32[]{:S(2)}) async-start(), calls=%async_computation.7 | async-start | bytes 2228224 | tf_op jit(solution)/shard_map/all_gather | solution.py:367
  29.6 26.7 %copy-start.33 = (f32[8]{0:T(128)}, f32[8]{0:T(128)S(1)}, u32[]{:S(2)}) copy-start(f32[8]{0:T(128)S(1)} %dynamic_slice.24) | copy-start | bytes 100
  53.0 3.3 %copy-start.3 = (f32[32,24,128]{2,1,0:T(8,128)}, f32[32,24,128]{2,1,0:T(8,128)S(1)}, u32[]{:S(2)}) copy-start(f32[32,24,128]{2,1,0:T(8,128)S(1)} %all-to-all-done.refs_2_) | copy-start | bytes 1179652
  53.8 1.6 copy-start.18
  53.9 2.0 copy-start.30
  55.4 6.2 %copy-start.35 = (f32[128,256]{1,0:T(8,128)S(1)}, f32[128,256]{1,0:T(8,128)}, u32[]{:S(2)}) copy-start(f32[128,256]{1,0:T(8,128)} %param.19) | copy-start | bytes 393220
  57.1 23.9 %all-to-all-start.1 = ((f32[32,2,8,128]{3,2,1,0:T(8,128)}), f32[32,2,8,128]{3,2,1,0:T(8,128)S(1)}, u32[]{:S(2)}, u32[]{:S(2)}) async-start(f32[32,2,8,128]{3,2,1,0:T(8,128)} %shard_map.181), calls=%async_computation.1 | async-start | bytes 524288 | tf_op jit(solution)/shard_map/all_to_all | solution.py:384
  61.7 16.4 %collective-permute-start.2 = (f32[128,256]{1,0:T(8,128)S(1)}, f32[128,256]{1,0:T(8,128)S(1)}, u32[]{:S(2)}, u32[]{:S(2)}) collective-permute-start(f32[128,256]{1,0:T(8,128)S(1)} %copy-done.35), channel_id=1, source_target_pairs={{0,0},{8,256},{256,8},{264,264},{1,1},{9,257},{257,9},{265,265},{2... | collective-permute-start | bytes 393224 | tf_op jit(solution)/shard_map/ppermute | solution.py:340
  64.4 16.6 %collective-permute-start.3 = (f32[128,256]{1,0:T(8,128)S(1)}, f32[128,256]{1,0:T(8,128)S(1)}, u32[]{:S(2)}, u32[]{:S(2)}) collective-permute-start(f32[128,256]{1,0:T(8,128)S(1)} %copy-done.35), channel_id=1, source_target_pairs={{0,8},{8,264},{256,0},{264,256},{1,9},{9,265},{257,1},{265,257},{2... | collective-permute-start | bytes 393224 | tf_op jit(solution)/shard_map/ppermute | solution.py:340
  82.0 40.8 %all-to-all-start.2 = ((f32[4,2,128,256]{3,2,1,0:T(8,128)}), f32[4,2,128,256]{3,2,1,0:T(8,128)S(1)}, u32[]{:S(2)}, u32[]{:S(2)}) async-start(f32[4,2,128,256]{3,2,1,0:T(8,128)} %shard_map.183), calls=%async_computation.2 | async-start | bytes 2097152 | tf_op jit(solution)/shard_map/all_to_all | solution.py:387
  99.2 1.6 copy-start
  102.2 20.6 %copy-start.1 = (f32[256,2048]{1,0:T(8,128)S(1)}, f32[256,2048]{1,0:T(8,128)}, u32[]{:S(2)}) copy-start(f32[256,2048]{1,0:T(8,128)} %all-gather.2.cloned.1.call-done.weight.near_w.far_w) | copy-start | bytes 6291460
  102.3 5.5 %collective-permute-start.1 = (f32[2,2,128,256]{3,2,1,0:T(8,128)S(1)}, f32[2,2,128,256]{3,2,1,0:T(8,128)S(1)}, u32[]{:S(2)}, u32[]{:S(2)}) collective-permute-start(f32[2,2,128,256]{3,2,1,0:T(8,128)S(1)} %get-tuple-element.20), channel_id=1, source_target_pairs={{0,1},{1,0},{2,3},{3,2},{4,5},{5,4},{6,7},{7,6},{8,9},{9,8},{10,11... | collective-permute-start | bytes 1572872 | tf_op jit(solution)/shard_map/ppermute | solution.py:344
  105.9 3.8 %collective-permute-start = (f32[2,2,128,256]{3,2,1,0:T(8,128)S(1)}, f32[2,2,128,256]{3,2,1,0:T(8,128)S(1)}, u32[]{:S(2)}, u32[]{:S(2)}) collective-permute-start(f32[2,2,128,256]{3,2,1,0:T(8,128)S(1)} %get-tuple-element.19), channel_id=1, source_target_pairs={{0,1},{1,0},{2,3},{3,2},{4,5},{5,4},{6,7},{7,6},{8,9},{9,8},{10,11... | collective-permute-start | bytes 1572872 | tf_op jit(solution)/shard_map/ppermute | solution.py:344
  122.8 1.2 copy-start.8
  126.5 29.5 %all-to-all-start.3 = ((f32[4,2,128,256]{3,2,1,0:T(8,128)}), f32[4,2,128,256]{3,2,1,0:T(8,128)}, u32[]{:S(2)}, u32[]{:S(2)}) async-start(f32[4,2,128,256]{3,2,1,0:T(8,128)} %copy-done.7), calls=%async_computation.3 | async-start | bytes 2097152 | tf_op jit(solution)/shard_map/all_to_all | solution.py:393
  130.7 74.7 %reduce-scatter.2.cloned.1.call-start = ((), (), s32[]{:S(2)}) async-start(), calls=%async_computation.8 | async-start | bytes 2621440 | tf_op jit(solution)/shard_map/reduce_scatter | solution.py:399
  130.8 5.6 %collective-permute-start.6 = (f32[4,2,128,256]{3,2,1,0:T(8,128)S(1)}, f32[4,2,128,256]{3,2,1,0:T(8,128)S(1)}, u32[]{:S(2)}, u32[]{:S(2)}) collective-permute-start(f32[4,2,128,256]{3,2,1,0:T(8,128)S(1)} %all-to-all-done.2.refs_1_.near), channel_id=1, source_target_pairs={{0,1},{1,0},{2,3},{3,2},{4,5},{5,4},{6,7},{7,6},{8,9},{9,8},{10,11... | collective-permute-start | bytes 3145736 | tf_op jit(solution)/shard_map/ppermute | solution.py:344
  138.1 1.3 copy-start.2
  139.4 1.0 copy-start.5
  140.5 1.2 copy-start.6
  156.7 45.5 %copy-start.4 = (f32[32,24,128]{2,1,0:T(8,128)S(1)}, f32[32,24,128]{2,1,0:T(8,128)}, u32[]{:S(2)}) copy-start(f32[32,24,128]{2,1,0:T(8,128)} %copy-done.3) | copy-start | bytes 1179652
  156.7 45.6 %copy-start.32 = (f32[66,32,1]{0,1,2:T(8,128)S(1)}, f32[66,32,1]{0,1,2:T(8,128)}, u32[]{:S(2)}) copy-start(f32[66,32,1]{0,1,2:T(8,128)} %constant.100) | copy-start | bytes 25348
  156.7 45.5 %all-to-all-start.4 = ((f32[32,2,8,128]{3,2,1,0:T(8,128)}), f32[32,2,8,128]{3,2,1,0:T(8,128)S(1)}, u32[]{:S(2)}, u32[]{:S(2)}) async-start(f32[32,2,8,128]{3,2,1,0:T(8,128)} %shard_map.186), calls=%async_computation.4 | async-start | bytes 524288 | tf_op jit(solution)/shard_map/all_to_all | solution.py:404
  166.2 36.5 %copy-start.27 = (f32[33,128]{1,0:T(8,128)S(1)}, f32[33,128]{1,0:T(8,128)}, u32[]{:S(2)}) copy-start(f32[33,128]{1,0:T(8,128)} %constant.95.clone) | copy-start | bytes 50692
  166.3 36.5 %copy-start.29 = (f32[33,128]{1,0:T(8,128)S(1)}, f32[33,128]{1,0:T(8,128)}, u32[]{:S(2)}) copy-start(f32[33,128]{1,0:T(8,128)} %constant.94.clone) | copy-start | bytes 50692
  167.6 35.3 %copy-start.21 = (f32[256,256,1]{1,0,2:T(8,128)S(1)}, f32[256,256,1]{1,0,2:T(8,128)}, u32[]{:S(2)}) copy-start(f32[256,256,1]{1,0,2:T(8,128)} %constant.101) | copy-start | bytes 786436
  167.6 34.5 %collective-permute-start.4 = (f32[128,256]{1,0:T(8,128)S(1)}, f32[128,256]{1,0:T(8,128)S(1)}, u32[]{:S(2)}, u32[]{:S(2)}) collective-permute-start(f32[128,256]{1,0:T(8,128)S(1)} %get-tuple-element.42), channel_id=1, source_target_pairs={{0,0},{8,256},{256,8},{264,264},{1,1},{9,257},{257,9},{265,265},{2... | collective-permute-start | bytes 393224 | tf_op jit(solution)/shard_map/ppermute | solution.py:340
  180.1 22.0 %collective-permute-start.5 = (f32[128,256]{1,0:T(8,128)S(1)}, f32[128,256]{1,0:T(8,128)S(1)}, u32[]{:S(2)}, u32[]{:S(2)}) collective-permute-start(f32[128,256]{1,0:T(8,128)S(1)} %get-tuple-element.41), channel_id=1, source_target_pairs={{0,256},{8,0},{256,264},{264,8},{1,257},{9,1},{257,265},{265,9},{2... | collective-permute-start | bytes 393224 | tf_op jit(solution)/shard_map/ppermute | solution.py:340
  202.1 3.4 %copy-start.11 = (f32[128,256]{1,0:T(8,128)}, f32[128,256]{1,0:T(8,128)S(1)}, u32[]{:S(2)}) copy-start(f32[128,256]{1,0:T(8,128)S(1)} %add.79.refs_6_) | copy-start | bytes 393220
  202.2 1.2 copy-start.22
  202.2 1.2 copy-start.23
  202.2 1.2 copy-start.24
  202.2 1.2 copy-start.25
  202.8 1.0 copy-start.19
  203.8 1.6 copy-start.34
  205.5 1.0 copy-start.9
  206.6 7.9 %copy-start.10 = (f32[4,256,128]{2,1,0:T(8,128)S(1)}, f32[4,256,128]{2,1,0:T(8,128)}, u32[]{:S(2)}) copy-start(f32[4,256,128]{2,1,0:T(8,128)} %reduce-scatter.2.cloned.1.call-done.refs_7_) | copy-start | bytes 1572868
  207.6 37.0 %copy-start.13 = (f32[128,256]{1,0:T(8,128)S(1)}, f32[128,256]{1,0:T(8,128)}, u32[]{:S(2)}) copy-start(f32[128,256]{1,0:T(8,128)} %refs_1_.3) | copy-start | bytes 393220
  207.6 37.0 %copy-start.15 = (f32[128,256]{1,0:T(8,128)S(1)}, f32[128,256]{1,0:T(8,128)}, u32[]{:S(2)}) copy-start(f32[128,256]{1,0:T(8,128)} %refs_2_.3) | copy-start | bytes 393220
  207.6 37.0 %all-to-all-start.5 = ((f32[32,32,128]{2,1,0:T(8,128)}), f32[32,32,128]{2,1,0:T(8,128)S(1)}, u32[]{:S(2)}, u32[]{:S(2)}) async-start(f32[32,32,128]{2,1,0:T(8,128)} %shard_map.188), calls=%async_computation.6 | async-start | bytes 1048576 | tf_op jit(solution)/shard_map/all_to_all | solution.py:417
  214.5 11.7 %collective-permute-start.7 = (f32[2,256,128]{2,1,0:T(8,128)S(1)}, f32[2,256,128]{2,1,0:T(8,128)S(1)}, u32[]{:S(2)}, u32[]{:S(2)}) collective-permute-start(f32[2,256,128]{2,1,0:T(8,128)S(1)} %dynamic-slice_bitcast_fusion), channel_id=1, source_target_pairs={{0,32},{16,48},{32,0},{48,16},{1,33},{17,49},{33,1},{49,17},{2,34}... | collective-permute-start | bytes 786440 | tf_op jit(solution)/shard_map/ppermute | solution.py:349
  226.2 5.7 %collective-permute-start.8 = (f32[256,128]{1,0:T(8,128)S(1)}, f32[256,128]{1,0:T(8,128)S(1)}, u32[]{:S(2)}, u32[]{:S(2)}) collective-permute-start(f32[256,128]{1,0:T(8,128)S(1)} %dynamic-slice_bitcast_fusion.1), channel_id=1, source_target_pairs={{0,16},{16,0},{32,48},{48,32},{1,17},{17,1},{33,49},{49,33},{2,18}... | collective-permute-start | bytes 393224 | tf_op jit(solution)/shard_map/ppermute | solution.py:349
  (5 other events, 4.6 us)
Sparse Core Ops, SparseCore 0:
  31.9 67.2 all-gather.1
Sparse Core Ops, SparseCore 1:
  140.5 40.7 reduce-scatter.1
